TPU v7x, 32 devices: a whole 2x2x4 slice. The times are simulated.
32 devices in a mesh: ctx: 4 (over z), ch: 8 (over y, x, core).
Axes of the slice: x: 2, y: 2, z: 4, core: 2. Of those that a mesh axis runs over, the one named last changes fastest.
Arguments:
- query_gate: bfloat16 [2048, 4096], P('ctx', 'ch'), may hold values from -6 to 6
- key_proj: bfloat16 [2048, 4096], P('ctx', 'ch'), may hold values from -6 to 6
- value_proj: bfloat16 [2048, 4096], P('ctx', 'ch'), may hold values from -6 to 6
- output_grad: bfloat16 [2048, 4096], P('ctx', 'ch'), may hold values from -6 to 6
- output_weight: bfloat16 [4096, 4096], P('ch'), may hold values from -0.09375 to 0.09375
- filter_taps: bfloat16 [2048, 4096], P('ctx', 'ch'), may hold values from -0.125 to 0.125
Outputs:
- grad_key: bfloat16 [2048, 4096], P('ctx', 'ch')
- grad_value: bfloat16 [2048, 4096], P('ctx', 'ch')
- grad_taps: float32 [2048, 4096], P('ctx', 'ch')
All inputs are finite; a program needn't handle non-finite values.
Results may differ from a plain program's by a relative error of at most 0.012.
Values may be sent and summed in bfloat16 or wider, within the bound.
No kernel may reach another device: no remote copies, remote signals or barrier semaphores. Data moves between devices by JAX's collectives and lax.ppermute only.
A program may use at most 128 MiB of HBM per device.

v0:
```python
import math

import jax
import jax.numpy as jnp
from jax import lax
from jax.sharding import PartitionSpec as P

matmul_precision_mode = lax.Precision.HIGH


def dft_tables(period):
    indices = jnp.arange(period, dtype=jnp.int32)
    product = indices[:, None] * indices[None, :] % period
    angles = product.astype(jnp.float32) * (2.0 * math.pi / period)
    return (jnp.cos(angles), jnp.sin(angles))


def spectrum(cosine_table, sine_table, framed_blocks):
    real_component = jnp.einsum(
        "br,irh->ibh", cosine_table, framed_blocks, precision=matmul_precision_mode
    )
    imaginary_component = -jnp.einsum(
        "br,irh->ibh", sine_table, framed_blocks, precision=matmul_precision_mode
    )
    return (real_component, imaginary_component)


def padded_spectrum(cosine_table, sine_table, blocks):
    framed_blocks = jnp.concatenate([blocks, jnp.zeros_like(blocks)], axis=1)
    return spectrum(cosine_table, sine_table, framed_blocks)


def inverse_rows(cosine_table, sine_table, real_component, imaginary_component, period):
    first_operand = jnp.einsum(
        "ir,qrb->qib", cosine_table, real_component, precision=matmul_precision_mode
    )
    second_operand = jnp.einsum(
        "ir,qrb->qib", sine_table, imaginary_component, precision=matmul_precision_mode
    )
    return (first_operand - second_operand) / period


def per_device(query_gate, key_proj, value_proj, output_grad, output_weight, filter_taps):
    length = query_gate.shape[0]
    channels = query_gate.shape[1]
    period = 2 * length
    members = lax.axis_size("ctx")
    position = lax.axis_index("ctx")
    cosine_table, sine_table = dft_tables(period)
    mixed_grad = lax.dot_general(
        lax.all_gather(output_grad, "ch", axis=1, tiled=True),
        output_weight,
        (((1,), (1,)), ((), ())),
        preferred_element_type=jnp.float32,
    )
    conv_grad = (query_gate.astype(jnp.float32) * mixed_grad).astype(jnp.bfloat16)
    conv_grad = lax.optimization_barrier(conv_grad)
    product = (key_proj.astype(jnp.float32) * value_proj.astype(jnp.float32)).astype(jnp.bfloat16)
    product = lax.optimization_barrier(product)
    inner = product.astype(jnp.float32)
    inner_re, inner_im = padded_spectrum(cosine_table, sine_table, inner[None])
    inner_re = inner_re[0]
    inner_im = inner_im[0]
    whole_taps = lax.all_gather(filter_taps, "ctx", axis=0, tiled=True).astype(jnp.float32)
    leading = jnp.zeros((length, channels), jnp.float32)
    tap_blocks = jnp.concatenate([leading, whole_taps], axis=0).reshape(
        members + 1, length, channels
    )
    segments = jnp.concatenate([tap_blocks[:-1], tap_blocks[1:]], axis=1)
    segment_real, segment_imaginary = spectrum(cosine_table, sine_table, segments)
    lane_ids = jnp.arange(members, dtype=jnp.int32)
    blocks = (
        lax.all_gather(conv_grad, "ctx", axis=0, tiled=True)
        .astype(jnp.float32)
        .reshape(-1, length, channels)
    )
    anchor = jnp.arange(blocks.shape[0], dtype=jnp.int32)
    grad_re, grad_im = padded_spectrum(cosine_table, sine_table, blocks)
    offset = anchor - position
    select_entries = (offset[:, None] == lane_ids[None, :]).astype(jnp.float32)
    filter_tap_real = jnp.einsum(
        "so,owz->swz", select_entries, segment_real, precision=matmul_precision_mode
    )
    filter_tap_imaginary = jnp.einsum(
        "so,owz->swz", select_entries, segment_imaginary, precision=matmul_precision_mode
    )
    input_re = jnp.sum(filter_tap_real * grad_re + filter_tap_imaginary * grad_im, axis=0)
    input_im = jnp.sum(filter_tap_real * grad_im - filter_tap_imaginary * grad_re, axis=0)
    cross_re = inner_re * grad_re + inner_im * grad_im
    cross_im = inner_re * grad_im - inner_im * grad_re
    lagged = inverse_rows(cosine_table, sine_table, cross_re, cross_im, period)
    before = ((offset - 1)[:, None] == lane_ids[None, :]).astype(jnp.float32)
    upper = jnp.einsum(
        "pn,plc->nlc", select_entries, lagged[:, :length], precision=matmul_precision_mode
    )
    lower = jnp.einsum("pn,plc->nlc", before, lagged[:, length:], precision=matmul_precision_mode)
    input_grad = jnp.dot(
        cosine_table[length:], input_re, precision=matmul_precision_mode
    ) - jnp.dot(sine_table[length:], input_im, precision=matmul_precision_mode)
    input_grad = input_grad / period
    grad_key = (value_proj.astype(jnp.float32) * input_grad).astype(jnp.bfloat16)
    grad_value = (key_proj.astype(jnp.float32) * input_grad).astype(jnp.bfloat16)
    factor = 1.0 / math.sqrt(members * length)
    summed = lax.psum_scatter(
        (upper + lower).reshape(members * length, channels).astype(jnp.bfloat16),
        "ctx",
        scatter_dimension=0,
        tiled=True,
    ).astype(jnp.float32)
    grad_taps = summed * factor
    return (grad_key, grad_value, grad_taps)


def solution(mesh):
    return jax.shard_map(
        per_device,
        mesh=mesh,
        in_specs=(
            P("ctx", "ch"),
            P("ctx", "ch"),
            P("ctx", "ch"),
            P("ctx", "ch"),
            P("ch", None),
            P("ctx", "ch"),
        ),
        out_specs=(P("ctx", "ch"), P("ctx", "ch"), P("ctx", "ch")),
        check_vma=False,
    )
```

profile of v0, /device:TPU:0, one launch (start us, length us, event | category | flops | bytes accessed | tf_op | source)
XLA Modules:
  0.0 493.3 jit_solution(4956073272209902304)
XLA Ops:
  8.7 16.4 %fusion.47 = f32[1024,1024]{1,0:T(8,128)} fusion(), kind=kLoop, calls=%fused_computation.54 | loop fusion | flops 14680064 | bytes 4194304 | tf_op jit(solution)/shard_map/sin | solution.py:15
  25.1 16.2 %fusion.48 = f32[1024,1024]{1,0:T(8,128)} fusion(), kind=kLoop, calls=%fused_computation.55 | loop fusion | flops 14680064 | bytes 4194304 | tf_op jit(solution)/shard_map/cos | solution.py:15
  41.3 17.0 %all-gather.4.cloned.1.call-done = bf16[2048,512]{1,0:T(8,128)(2,1)} async-done(((bf16[512,512]{1,0:T(8,128)(2,1)}), bf16[2048,512]{1,0:T(8,128)(2,1)}) %all-gather.4.cloned.1.call-update) | async-done | bytes 2097168 | tf_op jit(solution)/shard_map/all_gather | solution.py:64
  58.3 2.2 convert_element_type.62
  60.4 2.8 pad_slice_fusion
  63.8 5.3 %copy.58 = f32[4,512,512]{1,2,0:T(8,128)} copy(f32[4,512,512]{2,1,0:T(8,128)} %bitcast.107) | data formatting | bytes 8388608 | tf_op jit(solution)/shard_map/slice | solution.py:69
  69.1 5.3 %copy.59 = f32[4,512,512]{1,2,0:T(8,128)} copy(f32[4,512,512]{2,1,0:T(8,128)} %bitcast.106) | data formatting | bytes 8388608 | tf_op jit(solution)/shard_map/slice | solution.py:69
  74.5 21.8 %all-gather.6.cloned.1.call-done = bf16[512,4096]{1,0:T(8,128)(2,1)} async-done(((bf16[512,512]{1,0:T(8,128)(2,1)}), bf16[512,4096]{1,0:T(8,128)(2,1)}) %all-gather.6.cloned.1.call-update) | async-done | bytes 4194320 | tf_op jit(solution)/shard_map/all_gather | solution.py:51
  96.2 6.6 %fusion.70 = bf16[512,512]{1,0:T(8,128)(2,1)} fusion(bf16[512,4096]{1,0:T(8,128)(2,1)} %all-gather.6.cloned.1.call-done, bf16[512,4096]{1,0:T(8,128)(2,1)} %param.10, bf16[512,512]{1,0:T(8,128)(2,1)S(1)} %copy-done.6), kind=kOutput, calls=%fused_computation.65 | convolution fusion | flops 2148270080 | bytes 9437184 | tf_op jit(solution)/shard_map/dot_general | solution.py:50
  102.9 33.4 %fusion.34 = f32[4,1024,512]{1,2,0:T(8,128)} fusion(f32[4,512,512]{1,2,0:T(8,128)} %copy.59, f32[4,512,512]{1,2,0:T(8,128)} %copy.58), kind=kOutput, calls=%fused_computation.48 | convolution fusion | flops 12901679104 | bytes 16777216 | tf_op jit(solution)/shard_map/br,irh->ibh/dot_general | solution.py:19
  136.3 10.3 %copy.61 = f32[4,1024,512]{2,0,1:T(4,128)} copy(f32[4,1024,512]{1,2,0:T(8,128)} %fusion.34) | data formatting | bytes 16777216 | tf_op jit(solution)/shard_map/br,irh->ibh/transpose | solution.py:19
  146.6 10.4 %fusion.124 = f32[4,1024,512]{2,0,1:T(4,128)} fusion(f32[4,1024,512]{2,0,1:T(4,128)} %copy.61, s32[4]{0:T(128)S(1)} %get-tuple-element.11), kind=kOutput, calls=%fused_computation.121 | convolution fusion | flops 50331664 | bytes 16777232 | tf_op jit(solution)/shard_map/so,owz->swz/dot_general | solution.py:81
  157.0 9.9 %copy.63 = f32[4,1024,512]{1,2,0:T(8,128)} copy(f32[4,1024,512]{2,0,1:T(4,128)} %fusion.124) | data formatting | bytes 16777216 | tf_op jit(solution)/shard_map/so,owz->swz/dot_general | solution.py:81
  167.0 33.0 %negate_bitcast_fusion = f32[4,1024,512]{1,2,0:T(8,128)} fusion(f32[4,512,512]{1,2,0:T(8,128)} %copy.59, f32[4,512,512]{1,2,0:T(8,128)} %copy.58), kind=kOutput, calls=%fused_computation.18 | convolution fusion | flops 12903776256 | bytes 16777216 | tf_op jit(solution)/shard_map/br,irh->ibh/dot_general | solution.py:22
  200.0 10.3 %copy.65 = f32[4,1024,512]{2,0,1:T(4,128)} copy(f32[4,1024,512]{1,2,0:T(8,128)} %negate_bitcast_fusion) | data formatting | bytes 16777216 | tf_op jit(solution)/shard_map/neg | solution.py:22
  210.3 10.4 %fusion.122 = f32[4,1024,512]{2,0,1:T(4,128)} fusion(f32[4,1024,512]{2,0,1:T(4,128)} %copy.65, s32[4]{0:T(128)S(1)} %get-tuple-element.11), kind=kOutput, calls=%fused_computation.120 | convolution fusion | flops 50331664 | bytes 16777232 | tf_op jit(solution)/shard_map/so,owz->swz/dot_general | solution.py:84
  220.7 9.9 %copy.66 = f32[4,1024,512]{1,2,0:T(8,128)} copy(f32[4,1024,512]{2,0,1:T(4,128)} %fusion.122) | data formatting | bytes 16777216 | tf_op jit(solution)/shard_map/so,owz->swz/dot_general | solution.py:84
  230.6 2.8 copy.62
  233.4 24.5 %fusion.16 = f32[4,512,1024]{2,1,0:T(8,128)} fusion(bf16[4,512,512]{1,2,0:T(8,128)(2,1)S(1)} %copy.62), kind=kOutput, calls=%fused_computation.29 | convolution fusion | flops 12899581952 | bytes 10485760 | tf_op jit(solution)/shard_map/br,irh->ibh/dot_general | solution.py:22
  257.9 27.9 %fusion.1 = (f32[1024,512]{0,1:T(8,128)S(1)}, f32[1024,512]{0,1:T(8,128)S(1)}, f32[4,512,1024]{2,1,0:T(8,128)}) fusion(f32[4,1024,512]{1,2,0:T(8,128)S(1)} %copy-done.3, f32[4,1024,512]{1,2,0:T(8,128)} %copy.63, f32[4,512,1024]{2,1,0:T(8,128)} %fusion.16, bf16[4,512,512]{1,2,0:T(8,128)(2,1)S(1)} %copy.62), kind=kOutput, calls=%fused_computation.6 | convolution fusion | flops 12917407744 | bytes 39845888 | tf_op jit(solution)/shard_map/br,irh->ibh/dot_general | solution.py:19
  288.3 3.2 fusion.72
  291.5 19.1 %fusion.59 = f32[1024,512]{0,1:T(8,128)} fusion(bf16[1,512,512]{2,1,0:T(8,128)(2,1)S(1)} %bitcast.110), kind=kOutput, calls=%fused_computation.58 | convolution fusion | flops 3235905536 | bytes 2621440 | tf_op jit(solution)/shard_map/br,irh->ibh/dot_general | solution.py:19
  310.5 18.9 %negate_bitcast_fusion.1 = f32[1024,512]{0,1:T(8,128)} fusion(bf16[1,512,512]{2,1,0:T(8,128)(2,1)S(1)} %bitcast.111), kind=kOutput, calls=%fused_computation.53 | convolution fusion | flops 3236429824 | bytes 2621440 | tf_op jit(solution)/shard_map/br,irh->ibh/dot_general | solution.py:22
  329.5 37.2 %fusion.5 = f32[4,512,1024]{2,1,0:T(8,128)} fusion(f32[4,512,1024]{2,1,0:T(8,128)} %get-tuple-element.10, f32[4,512,1024]{2,1,0:T(8,128)S(1)} %bitcast.113, f32[1024,512]{0,1:T(8,128)} %negate_bitcast_fusion.1, f32[1024,512]{0,1:T(8,128)} %fusion.59), kind=kOutput, calls=%fused_computation.10 | convolution fusion | flops 12907970560 | bytes 29360128 | tf_op jit(solution)/shard_map/ir,qrb->qib/dot_general | solution.py:34
  366.6 40.3 %multiply_bitcast_fusion = f32[4,1024,512]{1,2,0:T(8,128)} fusion(f32[4,512,1024]{2,1,0:T(8,128)} %fusion.5, f32[4,512,1024]{2,1,0:T(8,128)} %get-tuple-element.10, f32[4,512,1024]{2,1,0:T(8,128)} %fusion.16, f32[1024,512]{0,1:T(8,128)} %negate_bitcast_fusion.1, f32[1024,512]{0,1:T(8,128)} %fusion.59), kind=kOutput, calls=%fused_computation.17 | convolution fusion | flops 12912164864 | bytes 37748736 | tf_op jit(solution)/shard_map/ir,qrb->qib/dot_general | solution.py:37
  406.9 7.7 %fusion.126 = (f32[4,512,512]{1,2,0:T(8,128)}, f32[4,512,512]{1,2,0:T(8,128)}) fusion(f32[4,1024,512]{1,2,0:T(8,128)} %multiply_bitcast_fusion), kind=kLoop, calls=%fused_computation.122 | loop fusion | bytes 16777216 | tf_op jit(solution)/shard_map/slice | solution.py:96
  414.6 5.5 %copy.69 = f32[4,512,512]{2,0,1:T(4,128)} copy(f32[4,512,512]{1,2,0:T(8,128)} %get-tuple-element.6) | data formatting | bytes 8388608 | tf_op jit(solution)/shard_map/slice | solution.py:94
  420.1 6.6 %fusion.120 = f32[4,512,512]{2,0,1:T(4,128)} fusion(f32[4,512,512]{2,0,1:T(4,128)} %copy.69, s32[4]{0:T(128)S(1)} %get-tuple-element.11), kind=kOutput, calls=%fused_computation.119 | convolution fusion | flops 25165840 | bytes 8388624 | tf_op jit(solution)/shard_map/pn,plc->nlc/dot_general | solution.py:93
  426.7 5.5 %copy.70 = f32[4,512,512]{2,0,1:T(4,128)} copy(f32[4,512,512]{1,2,0:T(8,128)} %get-tuple-element.5) | data formatting | bytes 8388608 | tf_op jit(solution)/shard_map/slice | solution.py:96
  432.1 6.5 %add_convert_fusion = bf16[4,512,512]{2,0,1:T(4,128)(2,1)S(1)} fusion(f32[4,512,512]{2,0,1:T(4,128)} %fusion.120, f32[4,512,512]{2,0,1:T(4,128)} %copy.70, s32[4]{0:T(128)S(1)} %get-tuple-element.12), kind=kOutput, calls=%fused_computation.40 | convolution fusion | flops 27262992 | bytes 10485776 | tf_op jit(solution)/shard_map/pn,plc->nlc/dot_general | solution.py:96
  440.4 44.0 %reduce-scatter.2.cloned.1.call-done = bf16[512,512]{1,0:T(8,128)(2,1)} async-done(((bf16[2048,512]{1,0:T(8,128)(2,1)}), bf16[512,512]{1,0:T(8,128)(2,1)}) %reduce-scatter.2.cloned.1.call-update) | async-done | bytes 524304 | tf_op jit(solution)/shard_map/reduce_scatter | solution.py:104
  484.4 2.2 convert_multiply_fusion.3
  (31 shorter events, 6.3 us)
Async XLA Ops:
  7.2 51.1 %all-gather.4.cloned.1.call-start = ((), (), s32[]{:S(2)}) async-start(), calls=%async_computation.1 | async-start | bytes 2621440 | tf_op jit(solution)/shard_map/all_gather | solution.py:64
  7.9 88.3 %all-gather.6.cloned.1.call-start = ((), (), s32[]{:S(2)}) async-start(), calls=%async_computation.2 | async-start | bytes 4718592 | tf_op jit(solution)/shard_map/all_gather | solution.py:51
  8.6 222.0 %all-gather.8.cloned.1.call-start = ((), (), s32[]{:S(2)}) async-start(), calls=%async_computation.3 | async-start | bytes 2621440 | tf_op jit(solution)/shard_map/all_gather | solution.py:73
  60.4 3.4 copy-start
  69.1 27.1 %copy-start.6 = (bf16[512,512]{1,0:T(8,128)(2,1)S(1)}, bf16[512,512]{1,0:T(8,128)(2,1)}, u32[]{:S(2)}) copy-start(bf16[512,512]{1,0:T(8,128)(2,1)} %param.6) | copy-start | bytes 1572868
  102.9 381.5 %reduce-scatter.2.cloned.1.call-start = ((), (), s32[]{:S(2)}) async-start(), calls=%async_computation.4 | async-start | bytes 2621440 | tf_op jit(solution)/shard_map/reduce_scatter | solution.py:104
  233.4 24.5 %copy-start.3 = (f32[4,1024,512]{1,2,0:T(8,128)S(1)}, f32[4,1024,512]{1,2,0:T(8,128)}, u32[]{:S(2)}) copy-start(f32[4,1024,512]{1,2,0:T(8,128)} %copy.66) | copy-start | bytes 25165828
  257.9 28.0 %copy-start.1 = (f32[1024,1024]{1,0:T(8,128)S(1)}, f32[1024,1024]{1,0:T(8,128)}, u32[]{:S(2)}) copy-start(f32[1024,1024]{1,0:T(8,128)} %fusion.47) | copy-start | bytes 12582916
  285.8 2.2 copy-start.2
  285.8 2.3 copy-start.4
  285.8 2.5 copy-start.5
  291.4 38.0 %slice-start = ((s8[8388608]{0:T(1024)(128)(4,1)}), s8[4194304]{0:T(1024)(128)(4,1)S(1)}, s32[]{:S(2)}) async-start(s8[8388608]{0:T(1024)(128)(4,1)} %bitcast.112), calls=%async_computation.5 | async-start | bytes 8388608
  310.5 19.0 %slice-start.1 = ((s8[8388608]{0:T(1024)(128)(4,1)}), s8[4194304]{0:T(1024)(128)(4,1)S(1)}, s32[]{:S(2)}) async-start(s8[8388608]{0:T(1024)(128)(4,1)} %bitcast.112), calls=%async_computation.6 | async-start | bytes 8388608
Sparse Core Ops, SparseCore 0:
  9.6 48.6 all-gather.3
  60.1 36.0 all-gather.5
  103.0 45.9 all-gather.7
  440.5 43.8 reduce-scatter.1
where the time goes:
time: 499 us; the launch traced here: 493 us
  matrix products  280 us (56%)
  waiting for transfers between devices  84.2 us (17%)
  local copies, waits for them, and re-layouts  78.1 us (16%)
  other arithmetic  36.9 us (7%)
  between operations  14.1 us (3%)
    dot_general x3, matrix products, spectrum(): jnp.einsum('br,irh->ibh', cosine_table, framed_blocks, precision=matmul_p...  80.4 us
    dot_general x3, matrix products, spectrum(): jnp.einsum('br,irh->ibh', sine_table, framed_blocks, precision=matmul_pre...  76.4 us
    reduce_scatter x1, waiting for transfers between devices, per_device(): lax.psum_scatter((upper + lower).reshape(members * length, channels).asty...  44 us
    dot_general x1, matrix products, inverse_rows(): jnp.einsum('ir,qrb->qib', sine_table, imaginary_component, precision=matm...  40.3 us
    dot_general x1, matrix products, inverse_rows(): jnp.einsum('ir,qrb->qib', cosine_table, real_component, precision=matmul_...  37.2 us
    all_gather x1, waiting for transfers between devices, per_device(): lax.all_gather(output_grad, 'ch', axis=1, tiled=True)  21.8 us
    all_gather x1, waiting for transfers between devices, per_device(): lax.all_gather(filter_taps, 'ctx', axis=0, tiled=True).astype(jnp.float32)  17 us
    sin x1, other arithmetic, dft_tables(): return (jnp.cos(angles), jnp.sin(angles))  16.4 us
  transfers between devices with their start and end apart: 4, of which 3 were waited for; matrix products, arithmetic and copies ran while one was open for 36% of the time, Pallas kernels for 0%

commit v1 on v0

--- a/solution.py
+++ b/solution.py
@@ -1,11 +1,353 @@
+import functools
 import math
 
 import jax
 import jax.numpy as jnp
+import ml_dtypes
+import numpy as np
 from jax import lax
+from jax.experimental import pallas as pl
+from jax.experimental.pallas import tpu as pltpu
 from jax.sharding import PartitionSpec as P
 
-matmul_precision_mode = lax.Precision.HIGH
+BF16, F32 = jnp.bfloat16, jnp.float32
+FOLDS = 16
+LANES = 128
+
+
+def spectral_tables(period):
+    rows = period // FOLDS
+    half = rows // 2
+    place = np.arange(rows, dtype=np.int64)
+
+    def angles(r):
+        return 2.0 * np.pi * ((np.outer(FOLDS * place + r, place)) % period) / period
+
+    forward_real = np.zeros((2, rows, rows))
+    backward_real = np.zeros((2, rows, rows))
+    for slot, r in ((0, 0), (1, FOLDS // 2)):
+        a = angles(r)
+        table = np.concatenate([np.cos(a[:half]), -np.sin(a[:half])], axis=0)
+        if r == 0:
+            table[half] = np.cos(a[half])
+        forward_real[slot] = table
+        inverse = table.T.copy()
+        if r == 0:
+            inverse[:, 0] *= 0.5
+            inverse[:, half] *= 0.5
+        backward_real[slot] = inverse
+    forward, backward = [], []
+    for r in range(1, FOLDS // 2):
+        a = angles(r)
+        forward.append(np.concatenate([np.cos(a), np.sin(a)], axis=0))
+        backward.append(np.concatenate([np.cos(a).T, np.sin(a).T], axis=0))
+    held = lambda t: np.asarray(t).astype(ml_dtypes.bfloat16)
+    return held(forward_real), held(np.stack(forward)), held(backward_real), held(np.stack(backward))
+
+
+def total(terms):
+    terms = [t for t in terms if t is not None]
+    while len(terms) > 1:
+        terms = [a + b for a, b in zip(terms[::2], terms[1::2])] + ([terms[-1]] if len(terms) % 2 else [])
+    return terms[0]
+
+
+C1, S1, C2 = math.cos(math.pi / 8), math.sin(math.pi / 8), math.sqrt(0.5)
+
+
+def fold_forward(x):
+    u = [x[j] + x[j + 4] for j in range(4)]
+    v = [x[j] - x[j + 4] for j in range(4)]
+    u02, u13 = u[0] + u[2], u[1] + u[3]
+    y = [None] * 9
+    y[0] = (u02 + u13, None)
+    y[8] = (u02 - u13, None)
+    y[4] = (u[0] - u[2], u[3] - u[1])
+    a, b = C2 * (v[1] - v[3]), C2 * (v[1] + v[3])
+    y[2] = (v[0] + a, -(v[2] + b))
+    y[6] = (v[0] - a, v[2] - b)
+    for r, partner, sign, turns in ((1, 7, -1.0, ((C1, S1), (C2, C2), (S1, C1))), (3, 5, 1.0, ((S1, C1), (-C2, C2), (-C1, -S1)))):
+        re, im = [x[0]], [x[4] if sign > 0 else -x[4]]
+        for j, (c, s) in zip((1, 2, 3), turns):
+            p, q = x[j], x[j + 4]
+            if sign < 0:
+                re.append(c * p - s * q)
+                im.append(-(s * p + c * q))
+            else:
+                re.append(c * p + s * q)
+                im.append(c * q - s * p)
+        er, orr = re[0] + re[2], re[1] + re[3]
+        ei, oi = im[0] + im[2], im[1] + im[3]
+        y[r] = (er + orr, ei + oi)
+        y[partner] = (er - orr, oi - ei)
+    return y
+
+
+def fold_backward(z):
+    out = [None] * 8
+    for parity in (0, 1):
+        sign = 1.0 - 2.0 * parity
+        a = {}
+        for r in (1, 2, 3):
+            zr, zi = z[r]
+            pr, pi = z[8 - r]
+            a[r] = (zr + pr, zi - pi) if parity == 0 else (zr - pr, zi + pi)
+        base = z[0][0] + z[8][0] if parity == 0 else z[0][0] - z[8][0]
+        z4r, z4i = z[4]
+        a1r, a1i = a[1]
+        a2r, a2i = a[2]
+        a3r, a3i = a[3]
+        if parity == 0:
+            p0, p1 = base + z4r, base - z4r
+            q0, q1 = p0 + a2r, p0 - a2r
+            t0, t1 = p1 - a2i, p1 + a2i
+            s = a1r + a3r
+            out[0], d = q0 + s, None
+            out[4] = q1 - a1i + a3i
+            m, n = C2 * (a1r - a3r), C2 * (a1i + a3i)
+            out[2] = t0 + m - n
+            out[6] = t1 - m - n
+        else:
+            p0, p1 = base - z4i, base + z4i
+            m, n = C2 * a2r, C2 * a2i
+            e = {1: p0 + m - n, 3: p1 - m - n, 5: p0 - m + n, 7: p1 + m + n}
+            c1r, s1r, c1i, s1i = C1 * a1r, S1 * a1r, C1 * a1i, S1 * a1i
+            c3r, s3r, c3i, s3i = C1 * a3r, S1 * a3r, C1 * a3i, S1 * a3i
+            out[1] = e[1] + (c1r - s1i) + (s3r - c3i)
+            out[3] = e[3] + (s1r - c1i) + (-c3r + s3i)
+            out[5] = e[5] + (-s1r - c1i) + (c3r + s3i)
+            out[7] = e[7] + (-c1r - s1i) + (-s3r - c3i)
+    return out
+
+
+def pack_kernel(taps_ref, key_ref, value_ref, out_ref):
+    for j in range(out_ref.shape[0]):
+        cols = slice(j * LANES, (j + 1) * LANES)
+        out_ref[j, :, :LANES] = taps_ref[:, cols]
+        product = key_ref[:, cols].astype(F32) * value_ref[:, cols].astype(F32)
+        out_ref[j, :, LANES:] = product.astype(BF16)
+
+
+def spectrum_kernel(x_ref, real_ref, table_ref, out_ref, yr_ref, yi_ref):
+    rows = real_ref.shape[1]
+    step = 16
+
+    def fold(i, carry):
+        at = pl.multiple_of(i * step, step)
+        x = [x_ref[pl.ds(j * rows + at, step), :].astype(F32) for j in range(8)]
+        for r, (re, im) in enumerate(fold_forward(x)):
+            yr_ref[r, pl.ds(at, step), :] = re.astype(BF16)
+            if im is not None:
+                yi_ref[r, pl.ds(at, step), :] = im.astype(BF16)
+        return carry
+
+    lax.fori_loop(0, rows // step, fold, 0)
+    dot = functools.partial(jnp.dot, preferred_element_type=F32)
+    out_ref[0, :rows] = dot(real_ref[0], yr_ref[0]).astype(out_ref.dtype)
+    out_ref[0, rows:] = dot(real_ref[1], yr_ref[8]).astype(out_ref.dtype)
+    for r in range(1, 8):
+        a = dot(table_ref[r - 1], yr_ref[r])
+        b = dot(table_ref[r - 1], yi_ref[r])
+        out_ref[r, :rows] = (a[:rows] + b[rows:]).astype(out_ref.dtype)
+        out_ref[r, rows:] = (b[:rows] - a[rows:]).astype(out_ref.dtype)
+
+
+def correlate_kernel(ids_ref, g0, g1, g2, g3, spec_ref, fr_ref, f_ref, br_ref, b_ref, o0, o1, o2, o3, x_ref, y_ref, zr_ref, zi_ref, res_ref):
+    rows = fr_ref.shape[1]
+    half = rows // 2
+    length = g0.shape[0]
+    step = 16
+    z = ids_ref[0]
+    dot = functools.partial(jnp.dot, preferred_element_type=F32)
+    for s, g in enumerate((g0, g1, g2, g3)):
+        x_ref[pl.ds(pl.multiple_of((z ^ s) * length, length), length), :] = g[...]
+
+    def fold(i, carry):
+        at = pl.multiple_of(i * step, step)
+        x = [x_ref[pl.ds(j * rows + at, step), :].astype(F32) for j in range(8)]
+        y = fold_forward(x)
+        y_ref[0, pl.ds(at, step), :LANES] = y[0][0].astype(BF16)
+        y_ref[0, pl.ds(at, step), LANES:] = y[8][0].astype(BF16)
+        for r in range(1, 8):
+            y_ref[r, pl.ds(at, step), :LANES] = y[r][0].astype(BF16)
+            y_ref[r, pl.ds(at, step), LANES:] = y[r][1].astype(BF16)
+        return carry
+
+    lax.fori_loop(0, rows // step, fold, 0)
+    twice = lambda a: jnp.concatenate([a, a], axis=1)
+
+    for r in range(1, 8):
+        d = dot(f_ref[r - 1], y_ref[r])
+        gr = twice(d[:rows, :LANES] + d[rows:, LANES:])
+        gi = twice(d[:rows, LANES:] - d[rows:, :LANES])
+        ar, ai = spec_ref[r, :rows].astype(F32), spec_ref[r, rows:].astype(F32)
+        pr = (ar * gr + ai * gi).astype(BF16)
+        pi = (ar * gi - ai * gr).astype(BF16)
+        p = dot(b_ref[r - 1], pr)
+        q = dot(b_ref[r - 1], pi)
+        zr_ref[r] = p[:rows] - q[rows:]
+        zi_ref[r] = q[:rows] + p[rows:]
+    first = lax.broadcasted_iota(jnp.int32, (half, 2 * LANES), 0) == 0
+    for slot, r in ((0, 0), (1, 8)):
+        g = twice(dot(fr_ref[slot], y_ref[0, :, slot * LANES : (slot + 1) * LANES]))
+        a = spec_ref[0, slot * rows : (slot + 1) * rows].astype(F32)
+        gr, gi, ar, ai = g[:half], g[half:], a[:half], a[half:]
+        pr = ar * gr + ai * gi
+        pi = ar * gi - ai * gr
+        if slot == 0:
+            pr = jnp.where(first, ar * gr, pr)
+            pi = jnp.where(first, ai * gi, pi)
+        zr_ref[r] = dot(br_ref[slot], jnp.concatenate([pr, pi], axis=0).astype(BF16))
+    scale = 1.0 / (FOLDS // 2 * rows)
+
+    def unfold(i, carry):
+        at = pl.multiple_of(i * step, step)
+        for lane in (0, LANES):
+            pick = lambda ref, r: ref[r, pl.ds(at, step), lane : lane + LANES]
+            zs = [(pick(zr_ref, r), pick(zi_ref, r) if 0 < r < 8 else None) for r in range(9)]
+            for j, out in enumerate(fold_backward(zs)):
+                res_ref[pl.ds(j * rows + at, step), lane : lane + LANES] = (out * scale).astype(BF16)
+        return carry
+
+    lax.fori_loop(0, rows // step, unfold, 0)
+    for s, o in enumerate((o0, o1, o2, o3)):
+        o[...] = res_ref[pl.ds(pl.multiple_of((z ^ s) * length, length), length), :]
+
+
+def finish_kernel(factor, ids_ref, r0, r1, r2, r3, key_ref, value_ref, gk_ref, gv_ref, gt_ref):
+    z = ids_ref[0]
+    for s, r in enumerate((r0, r1, r2, r3)):
+        cols = pl.ds(pl.multiple_of((z ^ s) * LANES, LANES), LANES)
+        grad = r[:, :LANES].astype(F32)
+        gk_ref[:, cols] = (value_ref[:, cols].astype(F32) * grad).astype(BF16)
+        gv_ref[:, cols] = (key_ref[:, cols].astype(F32) * grad).astype(BF16)
+        gt_ref[:, cols] = r[:, LANES:].astype(F32) * factor
+
+
+def project_kernel(n_weights, pairs, has_total, has_gate, ids_ref, *refs):
+    refs = list(refs)
+    weights = [refs.pop(0) for _ in range(n_weights)]
+    blocks = [refs.pop(0) for _ in range(1 + max(p[0] for p in pairs))]
+    before = refs.pop(0) if has_total else None
+    gate = refs.pop(0) if has_gate else None
+    sums = refs.pop() if has_gate else refs[0]
+    rows = sums.shape[0]
+    edges = sorted({p[2] for p in pairs}) + [rows]
+    for lo, hi in zip(edges[:-1], edges[1:]):
+        acc = before[lo:hi] if has_total else None
+        for b, w, first in pairs:
+            block = blocks[b]
+            if not (first <= lo and hi <= first + block.shape[0]):
+                continue
+            part = lax.dot_general(block[lo - first : hi - first, :], weights[w][...], (((1,), (1,)), ((), ())), preferred_element_type=F32)
+            acc = part if acc is None else acc + part
+        sums[lo:hi] = acc
+    if has_gate:
+        z = ids_ref[0]
+        for s, o in enumerate(refs):
+            cols = pl.ds(pl.multiple_of((z ^ s) * LANES, LANES), LANES)
+            o[...] = (gate[:, cols].astype(F32) * sums[:, cols]).astype(BF16)
+
+
+VMEM = pl.BlockSpec(memory_space=pltpu.VMEM)
+SMEM = pl.BlockSpec(memory_space=pltpu.SMEM)
+
+
+def cost(flops, nbytes):
+    return pl.CostEstimate(flops=flops, bytes_accessed=nbytes, transcendentals=0)
+
+
+def limits(mib):
+    return pltpu.CompilerParams(vmem_limit_bytes=mib * 2**20)
+
+
+def project(ids, weight, offsets, blocks, pairs, before=None, gate=None, rows=None):
+    channels = weight.shape[0]
+    depth = blocks[0].shape[1]
+    rows = rows or max(p[2] + blocks[p[0]].shape[0] for p in pairs)
+    whole = lambda a: pl.BlockSpec(a.shape, lambda i, ids: (0, 0))
+    ins = [weight] * len(offsets) + list(blocks)
+    specs = [pl.BlockSpec((channels, depth), (lambda m: lambda i, ids: (0, ids[1] ^ m))(m)) for m in offsets]
+    specs += [whole(b) for b in blocks]
+    for extra in (before, gate):
+        if extra is not None:
+            ins.append(extra)
+            specs.append(whole(extra))
+    if gate is None:
+        shapes = jax.ShapeDtypeStruct((rows, channels), F32)
+        outs, scratch = whole(shapes), []
+    else:
+        shapes = [jax.ShapeDtypeStruct((rows, LANES), BF16)] * (channels // LANES)
+        outs, scratch = [whole(s) for s in shapes], [pltpu.VMEM((rows, channels), F32)]
+    kernel = functools.partial(project_kernel, len(offsets), tuple(pairs), before is not None, gate is not None)
+    flops = 2 * sum(blocks[p[0]].shape[0] for p in pairs) * depth * channels
+    return pl.pallas_call(
+        kernel,
+        grid_spec=pltpu.PrefetchScalarGridSpec(num_scalar_prefetch=1, grid=(1,), in_specs=specs, out_specs=outs, scratch_shapes=scratch),
+        out_shape=shapes,
+        compiler_params=limits(32),
+        cost_estimate=cost(flops, sum(a.size * a.dtype.itemsize for a in ins[len(offsets):]) + 2 * len(offsets) * channels * depth),
+    )(ids, *ins)
+
+
+def pack(taps, key, value, parts):
+    length = taps.shape[0]
+    return pl.pallas_call(
+        pack_kernel,
+        out_shape=jax.ShapeDtypeStruct((parts, length, 2 * LANES), BF16),
+        in_specs=[VMEM] * 3,
+        out_specs=VMEM,
+        compiler_params=limits(16),
+        cost_estimate=cost(taps.size, 5 * 2 * taps.size),
+    )(taps, key, value)
+
+
+def block_spectrum(x, real, table):
+    rows = real.shape[1]
+    return pl.pallas_call(
+        spectrum_kernel,
+        out_shape=jax.ShapeDtypeStruct((8, 2 * rows, 2 * LANES), BF16),
+        in_specs=[VMEM] * 3,
+        out_specs=VMEM,
+        scratch_shapes=[pltpu.VMEM((9, rows, 2 * LANES), BF16), pltpu.VMEM((8, rows, 2 * LANES), BF16)],
+        compiler_params=limits(24),
+        cost_estimate=cost(2 * 15 * 2 * rows * rows * 2 * LANES, 2 * (x.size + table.size + 16 * rows * 2 * LANES)),
+    )(x, real, table)
+
+
+def correlate(ids, grads, spec, tables):
+    length = grads[0].shape[0]
+    rows = tables[0].shape[1]
+    return pl.pallas_call(
+        correlate_kernel,
+        out_shape=[jax.ShapeDtypeStruct((length, 2 * LANES), BF16)] * 4,
+        in_specs=[SMEM] + [VMEM] * 9,
+        out_specs=[VMEM] * 4,
+        scratch_shapes=[
+            pltpu.VMEM((8 * rows, LANES), BF16),
+            pltpu.VMEM((8, rows, 2 * LANES), BF16),
+            pltpu.VMEM((9, rows, 2 * LANES), F32),
+            pltpu.VMEM((8, rows, 2 * LANES), F32),
+            pltpu.VMEM((8 * rows, 2 * LANES), BF16),
+        ],
+        compiler_params=limits(32),
+        cost_estimate=cost(2 * 8 * 6 * rows * rows * 2 * LANES, 2 * (4 * length * LANES * 3 + spec.size + 2 * tables[1].size)),
+    )(ids, *grads, spec, *tables)
+
+
+def finish(ids, parts, key, value, factor):
+    shape = key.shape
+    return pl.pallas_call(
+        functools.partial(finish_kernel, factor),
+        out_shape=[jax.ShapeDtypeStruct(shape, BF16), jax.ShapeDtypeStruct(shape, BF16), jax.ShapeDtypeStruct(shape, F32)],
+        in_specs=[SMEM] + [VMEM] * 6,
+        out_specs=[VMEM] * 3,
+        compiler_params=limits(16),
+        cost_estimate=cost(4 * key.size, 16 * key.size),
+    )(ids, *parts, key, value)
+
+
+PRECISION = lax.Precision.HIGH
 
 
 def dft_tables(period):
@@ -17,10 +359,10 @@
 
 def spectrum(cosine_table, sine_table, framed_blocks):
     real_component = jnp.einsum(
-        "br,irh->ibh", cosine_table, framed_blocks, precision=matmul_precision_mode
+        "br,irh->ibh", cosine_table, framed_blocks, precision=PRECISION
     )
     imaginary_component = -jnp.einsum(
-        "br,irh->ibh", sine_table, framed_blocks, precision=matmul_precision_mode
+        "br,irh->ibh", sine_table, framed_blocks, precision=PRECISION
     )
     return (real_component, imaginary_component)
 
@@ -32,15 +374,15 @@
 
 def inverse_rows(cosine_table, sine_table, real_component, imaginary_component, period):
     first_operand = jnp.einsum(
-        "ir,qrb->qib", cosine_table, real_component, precision=matmul_precision_mode
+        "ir,qrb->qib", cosine_table, real_component, precision=PRECISION
     )
     second_operand = jnp.einsum(
-        "ir,qrb->qib", sine_table, imaginary_component, precision=matmul_precision_mode
+        "ir,qrb->qib", sine_table, imaginary_component, precision=PRECISION
     )
     return (first_operand - second_operand) / period
 
 
-def per_device(query_gate, key_proj, value_proj, output_grad, output_weight, filter_taps):
+def general_layer(query_gate, key_proj, value_proj, output_grad, output_weight, filter_taps):
     length = query_gate.shape[0]
     channels = query_gate.shape[1]
     period = 2 * length
@@ -79,10 +421,10 @@
     offset = anchor - position
     select_entries = (offset[:, None] == lane_ids[None, :]).astype(jnp.float32)
     filter_tap_real = jnp.einsum(
-        "so,owz->swz", select_entries, segment_real, precision=matmul_precision_mode
+        "so,owz->swz", select_entries, segment_real, precision=PRECISION
     )
     filter_tap_imaginary = jnp.einsum(
-        "so,owz->swz", select_entries, segment_imaginary, precision=matmul_precision_mode
+        "so,owz->swz", select_entries, segment_imaginary, precision=PRECISION
     )
     input_re = jnp.sum(filter_tap_real * grad_re + filter_tap_imaginary * grad_im, axis=0)
     input_im = jnp.sum(filter_tap_real * grad_im - filter_tap_imaginary * grad_re, axis=0)
@@ -91,12 +433,12 @@
     lagged = inverse_rows(cosine_table, sine_table, cross_re, cross_im, period)
     before = ((offset - 1)[:, None] == lane_ids[None, :]).astype(jnp.float32)
     upper = jnp.einsum(
-        "pn,plc->nlc", select_entries, lagged[:, :length], precision=matmul_precision_mode
-    )
-    lower = jnp.einsum("pn,plc->nlc", before, lagged[:, length:], precision=matmul_precision_mode)
+        "pn,plc->nlc", select_entries, lagged[:, :length], precision=PRECISION
+    )
+    lower = jnp.einsum("pn,plc->nlc", before, lagged[:, length:], precision=PRECISION)
     input_grad = jnp.dot(
-        cosine_table[length:], input_re, precision=matmul_precision_mode
-    ) - jnp.dot(sine_table[length:], input_im, precision=matmul_precision_mode)
+        cosine_table[length:], input_re, precision=PRECISION
+    ) - jnp.dot(sine_table[length:], input_im, precision=PRECISION)
     input_grad = input_grad / period
     grad_key = (value_proj.astype(jnp.float32) * input_grad).astype(jnp.bfloat16)
     grad_value = (key_proj.astype(jnp.float32) * input_grad).astype(jnp.bfloat16)
@@ -109,6 +451,40 @@
     ).astype(jnp.float32)
     grad_taps = summed * factor
     return (grad_key, grad_value, grad_taps)
+
+
+def hop(x, axis, distance):
+    n = lax.axis_size(axis)
+    return lax.ppermute(x, axis, [(j, j ^ distance) for j in range(n)])
+
+
+def exchanged_layer(query_gate, key_proj, value_proj, output_grad, output_weight, filter_taps):
+    length, channels = query_gate.shape
+    parts = lax.axis_size("ctx")
+    tables = [jnp.asarray(t) for t in spectral_tables(2 * parts * length)]
+    ids = jnp.stack([lax.axis_index("ctx"), lax.axis_index("ch")]).astype(jnp.int32)
+    half = length // 2
+    sent = pack(filter_taps, key_proj, value_proj, parts)
+    from_x, from_y, from_core = hop(output_grad, "ch", 2), hop(output_grad, "ch", 4), hop(output_grad, "ch", 1)
+    series = lax.all_to_all(sent, "ctx", 0, 0, tiled=True).reshape(parts * length, 2 * LANES)
+    spec = block_spectrum(series, tables[0], tables[1])
+    total = project(ids, output_weight, (0, 1), [output_grad, from_core], [(0, 0, 0), (1, 1, 0)])
+    far_top, far_low = hop(from_y[:half], "ch", 2), hop(from_x[half:], "ch", 4)
+    core_x, core_y = hop(from_x, "ch", 1), hop(from_y, "ch", 1)
+    total = project(ids, output_weight, (2, 3, 4, 5), [from_x, core_x, from_y, core_y], [(j, j, 0) for j in range(4)], before=total)
+    core_top, core_low = hop(far_top, "ch", 1), hop(far_low, "ch", 1)
+    grads = project(ids, output_weight, (6, 7), [far_top, core_top, far_low, core_low], [(0, 0, 0), (1, 1, 0), (2, 0, half), (3, 1, half)], before=total, gate=query_gate)
+    grads = [grads[0]] + [hop(grads[s], "ctx", s) for s in range(1, parts)]
+    results = correlate(ids, grads, spec, tables)
+    results = [results[0]] + [hop(results[s], "ctx", s) for s in range(1, parts)]
+    return tuple(finish(ids, results, key_proj, value_proj, 1.0 / math.sqrt(parts * length)))
+
+
+def per_device(*arrays):
+    length, channels = arrays[0].shape
+    if lax.axis_size("ctx") == 4 and lax.axis_size("ch") == 8 and channels == 4 * LANES and length % 32 == 0:
+        return exchanged_layer(*arrays)
+    return general_layer(*arrays)
 
 
 def solution(mesh):

time: 499 us -> 94.2 us (0.19)
  the two profiles are of different devices: /device:TPU:0 before, /device:TPU:20 now
where the time goes in v1:
time: 94.2 us; the launch traced here: 93.8 us
  waiting for transfers between devices  51.7 us (55%)
  Pallas kernels  18.2 us (19%)
  starting transfers between devices  16.9 us (18%)
  local copies, waits for them, and re-layouts  6.09 us (6%)
    ppermute x15, waiting for transfers between devices, hop(): return lax.ppermute(x, axis, [(j, j ^ distance) for j in range(n)])  51.7 us
    ppermute x15, starting transfers between devices, hop(): return lax.ppermute(x, axis, [(j, j ^ distance) for j in range(n)])  11.7 us
    pallas_call x3, Pallas kernels, project(): pl.pallas_call(kernel, grid_spec=pltpu.PrefetchScalarGridSpec(num_scalar_...  7.56 us
    unnamed x22, local copies, waits for them, and re-layouts  5.35 us
    all_to_all x1, starting transfers between devices, exchanged_layer(): lax.all_to_all(sent, 'ctx', 0, 0, tiled=True)  5.2 us
    pallas_call x1, Pallas kernels, correlate(): pl.pallas_call(correlate_kernel, out_shape=[jax.ShapeDtypeStruct((length,...  5.16 us
    pallas_call x1, Pallas kernels, finish(): pl.pallas_call(functools.partial(finish_kernel, factor), out_shape=[jax.S...  2.2 us
    pallas_call x1, Pallas kernels, block_spectrum(): pl.pallas_call(spectrum_kernel, out_shape=jax.ShapeDtypeStruct((8, 2 * ro...  2.09 us
  transfers between devices with their start and end apart: 16, of which 9 were waited for; matrix products, arithmetic and copies ran while one was open for 1% of the time, Pallas kernels for 10%

profile of v1, /device:TPU:20, one launch (start us, length us, event | category | flops | bytes accessed | tf_op | source)
XLA Modules:
  0.0 93.8 jit_solution(8198206305198109643)
XLA Ops:
  0.6 1.0 %copy-done.2 = bf16[512,512]{1,0:T(8,128)(2,1)S(1)} copy-done((bf16[512,512]{1,0:T(8,128)(2,1)S(1)}, bf16[512,512]{1,0:T(8,128)(2,1)}, u32[]{:S(2)}) %copy-start.2) | copy-done | bytes 524312
  1.7 1.0 %copy-done.4 = bf16[512,512]{1,0:T(8,128)(2,1)S(1)} copy-done((bf16[512,512]{1,0:T(8,128)(2,1)S(1)}, bf16[512,512]{1,0:T(8,128)(2,1)}, u32[]{:S(2)}) %copy-start.4) | copy-done | bytes 524312
  2.7 1.0 %copy-done.8 = bf16[512,512]{1,0:T(8,128)(2,1)S(1)} copy-done((bf16[512,512]{1,0:T(8,128)(2,1)S(1)}, bf16[512,512]{1,0:T(8,128)(2,1)}, u32[]{:S(2)}) %copy-start.8) | copy-done | bytes 524312
  3.8 1.2 %shard_map.124 = bf16[4,512,256]{2,1,0:T(8,128)(2,1)} custom-call(bf16[512,512]{1,0:T(8,128)(2,1)S(1)} %copy-done.8, bf16[512,512]{1,0:T(8,128)(2,1)S(1)} %copy-done.2, bf16[512,512]{1,0:T(8,128)(2,1)S(1)} %copy-done.4), custom_call_target="tpu_custom_call" | custom-call | flops 262144 | bytes 2621440 | tf_op jit(solution)/shard_map/pallas_call | solution.py:295
  4.9 5.2 %all-to-all-start = ((bf16[4,512,256]{2,1,0:T(8,128)(2,1)}), bf16[4,512,256]{2,1,0:T(8,128)(2,1)S(1)}, u32[]{:S(2)}, u32[]{:S(2)}) async-start(bf16[4,512,256]{2,1,0:T(8,128)(2,1)} %shard_map.124), calls=%async_computation | async-start | bytes 2097152 | tf_op jit(solution)/shard_map/all_to_all | solution.py:469
  10.1 1.5 %collective-permute-start.3 = (bf16[512,512]{1,0:T(8,128)(2,1)}, bf16[512,512]{1,0:T(8,128)(2,1)S(1)}, u32[]{:S(2)}, u32[]{:S(2)}) collective-permute-start(bf16[512,512]{1,0:T(8,128)(2,1)} %refs_2_.2), channel_id=1, source_target_pairs={{0,2},{1,3},{2,0},{3,1},{4,6},{5,7},{6,4},{7,5},{8,10},{9,11},{10,... | collective-permute-start | bytes 1572872 | tf_op jit(solution)/shard_map/ppermute | solution.py:458
  11.6 0.5 collective-permute-start
  12.1 11.3 %collective-permute-done.3.refs_4_ = bf16[512,512]{1,0:T(8,128)(2,1)S(1)} collective-permute-done((bf16[512,512]{1,0:T(8,128)(2,1)}, bf16[512,512]{1,0:T(8,128)(2,1)S(1)}, u32[]{:S(2)}, u32[]{:S(2)}) %collective-permute-start.3) | collective-permute-done | bytes 524320 | tf_op jit(solution)/shard_map/ppermute | solution.py:458
  23.5 1.2 %collective-permute-done.refs_6_ = bf16[512,512]{1,0:T(8,128)(2,1)S(1)} collective-permute-done((bf16[512,512]{1,0:T(8,128)(2,1)}, bf16[512,512]{1,0:T(8,128)(2,1)S(1)}, u32[]{:S(2)}, u32[]{:S(2)}) %collective-permute-start) | collective-permute-done | bytes 524320 | tf_op jit(solution)/shard_map/ppermute | solution.py:458
  24.7 0.7 slice.8
  25.4 0.8 collective-permute-start.1
  26.2 0.6 collective-permute-start.4
  26.8 7.6 %collective-permute-done.1.refs_2_ = bf16[256,512]{1,0:T(8,128)(2,1)} collective-permute-done((bf16[256,512]{1,0:T(8,128)(2,1)}, bf16[256,512]{1,0:T(8,128)(2,1)}, u32[]{:S(2)}, u32[]{:S(2)}) %collective-permute-start.1) | collective-permute-done | bytes 262176 | tf_op jit(solution)/shard_map/ppermute | solution.py:458
  34.4 0.1 collective-permute-done.4.refs_4_
  34.6 0.4 collective-permute-start.5
  35.0 2.2 %copy-done = bf16[512,4096]{1,0:T(8,128)(2,1)S(1)} copy-done((bf16[512,4096]{1,0:T(8,128)(2,1)S(1)}, bf16[512,4096]{1,0:T(8,128)(2,1)}, u32[]{:S(2)}) %copy-start) | copy-done | bytes 4194328
  37.2 2.5 %shard_map.121.refs_8_ = f32[512,512]{1,0:T(8,128)S(1)} custom-call(s32[2]{0:T(128)S(1)} %pad_add_fusion.ids_ref, bf16[512,4096]{1,0:T(8,128)(2,1)S(1)} %copy-done, bf16[512,4096]{1,0:T(8,128)(2,1)S(1)} %copy-done, bf16[512,512]{1,0:T(8,128)(2,1)} %refs_2_.2, bf16[512,512]{1,0:T(8,128)(2,1)} %collective-permute-done.8.refs_3_), custom_call_target="tpu_custom_call" | custom-call | flops 536870912 | bytes 2097152 | tf_op jit(solution)/shard_map/pallas_call | solution.py:284
  39.7 1.8 %shard_map.122.refs_6_ = f32[512,512]{1,0:T(8,128)S(1)} custom-call(s32[2]{0:T(128)S(1)} %pad_add_fusion.ids_ref, bf16[512,4096]{1,0:T(8,128)(2,1)S(1)} %copy-done, bf16[512,4096]{1,0:T(8,128)(2,1)S(1)} %copy-done, bf16[512,4096]{1,0:T(8,128)(2,1)S(1)} %copy-done, bf16[512,4096]{1,0:T(8,128)(2,1)S(1)} %copy-done, ...), custom_call_target="tpu_custom_call" | custom-call | flops 1073741824 | bytes 5242880 | tf_op jit(solution)/shard_map/pallas_call | solution.py:284
  41.6 3.2 %shard_map.123 = (bf16[512,128]{1,0:T(8,128)(2,1)S(1)}, bf16[512,128]{1,0:T(8,128)(2,1)}, bf16[512,128]{1,0:T(8,128)(2,1)}, bf16[512,128]{1,0:T(8,128)(2,1)}) custom-call(s32[2]{0:T(128)S(1)} %pad_add_fusion.ids_ref, bf16[512,4096]{1,0:T(8,128)(2,1)S(1)} %copy-done, bf16[512,4096]{1,0:T(8,128)(2,1)S(1)} %copy-done, ...), custom_call_target="tpu_custom_call" | custom-call | flops 536870912 | bytes 3670016 | tf_op jit(solution)/shard_map/pallas_call | solution.py:284
  44.9 0.3 collective-permute-start.10
  45.2 2.7 %collective-permute-start.11 = (bf16[512,128]{1,0:T(8,128)(2,1)}, bf16[512,128]{1,0:T(8,128)(2,1)S(1)}, u32[]{:S(2)}, u32[]{:S(2)}) collective-permute-start(bf16[512,128]{1,0:T(8,128)(2,1)} %get-tuple-element.14), channel_id=1, source_target_pairs={{0,24},{8,16},{16,8},{24,0},{1,25},{9,17},{17,9},{25,1},{2,26},{10... | collective-permute-start | bytes 393224 | tf_op jit(solution)/shard_map/ppermute | solution.py:458
  47.8 1.4 %collective-permute-start.9 = (bf16[512,128]{1,0:T(8,128)(2,1)}, bf16[512,128]{1,0:T(8,128)(2,1)}, u32[]{:S(2)}, u32[]{:S(2)}) collective-permute-start(bf16[512,128]{1,0:T(8,128)(2,1)} %get-tuple-element.12), channel_id=1, source_target_pairs={{0,8},{8,0},{16,24},{24,16},{1,9},{9,1},{17,25},{25,17},{2,10},{10... | collective-permute-start | bytes 393224 | tf_op jit(solution)/shard_map/ppermute | solution.py:458
  49.3 2.1 %shard_map.125.spec_ref = bf16[8,512,256]{2,1,0:T(8,128)(2,1)S(1)} custom-call(bf16[2048,256]{1,0:T(8,128)(2,1)S(1)} %bitcast.3, bf16[2,256,256]{2,1,0:T(8,128)(2,1)S(1)} %copy-done.7, bf16[7,512,256]{2,1,0:T(8,128)(2,1)S(1)} %copy-done.1), custom_call_target="tpu_custom_call" | custom-call | flops 1006632960 | bytes 4980736 | tf_op jit(solution)/shard_map/pallas_call | solution.py:307
  51.4 3.6 %collective-permute-done.10.g2 = bf16[512,128]{1,0:T(8,128)(2,1)S(1)} collective-permute-done((bf16[512,128]{1,0:T(8,128)(2,1)}, bf16[512,128]{1,0:T(8,128)(2,1)S(1)}, u32[]{:S(2)}, u32[]{:S(2)}) %collective-permute-start.10) | collective-permute-done | bytes 131104 | tf_op jit(solution)/shard_map/ppermute | solution.py:458
  55.0 5.0 %collective-permute-done.11.g3 = bf16[512,128]{1,0:T(8,128)(2,1)S(1)} collective-permute-done((bf16[512,128]{1,0:T(8,128)(2,1)}, bf16[512,128]{1,0:T(8,128)(2,1)S(1)}, u32[]{:S(2)}, u32[]{:S(2)}) %collective-permute-start.11) | collective-permute-done | bytes 131104 | tf_op jit(solution)/shard_map/ppermute | solution.py:458
  60.0 5.2 %shard_map.126 = (bf16[512,256]{1,0:T(8,128)(2,1)S(1)}, bf16[512,256]{1,0:T(8,128)(2,1)S(1)}, bf16[512,256]{1,0:T(8,128)(2,1)S(1)}, bf16[512,256]{1,0:T(8,128)(2,1)S(1)}) custom-call(s32[2]{0:T(128)S(1)} %pad_add_fusion.ids_ref, bf16[512,128]{1,0:T(8,128)(2,1)S(1)} %get-tuple-element.11.g0, bf16[512,128]{1,0:T(8,128)(2,1)} %collective-permute-done.9.g1, ...), custom_call_target="tpu_custom_call" | custom-call | flops 1610612736 | bytes 7340032 | tf_op jit(solution)/shard_map/pallas_call | solution.py:321
  65.3 1.0 %collective-permute-start.13 = (bf16[512,256]{1,0:T(8,128)(2,1)S(1)}, bf16[512,256]{1,0:T(8,128)(2,1)S(1)}, u32[]{:S(2)}, u32[]{:S(2)}) collective-permute-start(bf16[512,256]{1,0:T(8,128)(2,1)S(1)} %get-tuple-element.17), channel_id=1, source_target_pairs={{0,16},{8,24},{16,0},{24,8},{1,17},{9,25},{17,1},{25,9},{2,18},{10... | collective-permute-start | bytes 786440 | tf_op jit(solution)/shard_map/ppermute | solution.py:458
  66.4 2.4 %collective-permute-start.14 = (bf16[512,256]{1,0:T(8,128)(2,1)S(1)}, bf16[512,256]{1,0:T(8,128)(2,1)S(1)}, u32[]{:S(2)}, u32[]{:S(2)}) collective-permute-start(bf16[512,256]{1,0:T(8,128)(2,1)S(1)} %get-tuple-element.18), channel_id=1, source_target_pairs={{0,24},{8,16},{16,8},{24,0},{1,25},{9,17},{17,9},{25,1},{2,26},{10... | collective-permute-start | bytes 786440 | tf_op jit(solution)/shard_map/ppermute | solution.py:458
  68.8 6.1 %collective-permute-done.12.r1 = bf16[512,256]{1,0:T(8,128)(2,1)S(1)} collective-permute-done((bf16[512,256]{1,0:T(8,128)(2,1)S(1)}, bf16[512,256]{1,0:T(8,128)(2,1)S(1)}, u32[]{:S(2)}, u32[]{:S(2)}) %collective-permute-start.12) | collective-permute-done | bytes 262176 | tf_op jit(solution)/shard_map/ppermute | solution.py:458
  74.9 9.3 %collective-permute-done.13.r2 = bf16[512,256]{1,0:T(8,128)(2,1)S(1)} collective-permute-done((bf16[512,256]{1,0:T(8,128)(2,1)S(1)}, bf16[512,256]{1,0:T(8,128)(2,1)S(1)}, u32[]{:S(2)}, u32[]{:S(2)}) %collective-permute-start.13) | collective-permute-done | bytes 262176 | tf_op jit(solution)/shard_map/ppermute | solution.py:458
  84.2 7.4 %collective-permute-done.14.r3 = bf16[512,256]{1,0:T(8,128)(2,1)S(1)} collective-permute-done((bf16[512,256]{1,0:T(8,128)(2,1)S(1)}, bf16[512,256]{1,0:T(8,128)(2,1)S(1)}, u32[]{:S(2)}, u32[]{:S(2)}) %collective-permute-start.14) | collective-permute-done | bytes 262176 | tf_op jit(solution)/shard_map/ppermute | solution.py:458
  91.6 2.2 %shard_map.127 = (bf16[512,512]{1,0:T(8,128)(2,1)}, bf16[512,512]{1,0:T(8,128)(2,1)}, f32[512,512]{1,0:T(8,128)}) custom-call(s32[2]{0:T(128)S(1)} %pad_add_fusion.ids_ref, bf16[512,256]{1,0:T(8,128)(2,1)S(1)} %get-tuple-element.15.r0, bf16[512,256]{1,0:T(8,128)(2,1)S(1)} %collective-permute-done.12.r1, bf16[512,256]{1,0:T(8,128)(2,1)S(1)} %collective-permute-done.13.r2, ...), custom_call_target="tpu_custom_call" | custom-call | flops 1048576 | bytes 4194304 | tf_op jit(solution)/shard_map/pallas_call | solution.py:340
  (32 shorter events, 0.3 us)
Async XLA Ops:
  0.6 1.0 %copy-start.2 = (bf16[512,512]{1,0:T(8,128)(2,1)S(1)}, bf16[512,512]{1,0:T(8,128)(2,1)}, u32[]{:S(2)}) copy-start(bf16[512,512]{1,0:T(8,128)(2,1)} %key_ref.3) | copy-start | bytes 1572868
  1.7 1.0 %copy-start.4 = (bf16[512,512]{1,0:T(8,128)(2,1)S(1)}, bf16[512,512]{1,0:T(8,128)(2,1)}, u32[]{:S(2)}) copy-start(bf16[512,512]{1,0:T(8,128)(2,1)} %value_ref.3) | copy-start | bytes 1572868
  2.7 1.0 %copy-start.8 = (bf16[512,512]{1,0:T(8,128)(2,1)S(1)}, bf16[512,512]{1,0:T(8,128)(2,1)}, u32[]{:S(2)}) copy-start(bf16[512,512]{1,0:T(8,128)(2,1)} %taps_ref.1) | copy-start | bytes 1572868
  4.9 44.3 %all-to-all-start = ((bf16[4,512,256]{2,1,0:T(8,128)(2,1)}), bf16[4,512,256]{2,1,0:T(8,128)(2,1)S(1)}, u32[]{:S(2)}, u32[]{:S(2)}) async-start(bf16[4,512,256]{2,1,0:T(8,128)(2,1)} %shard_map.124), calls=%async_computation | async-start | bytes 2097152 | tf_op jit(solution)/shard_map/all_to_all | solution.py:469
  10.1 13.3 %collective-permute-start.3 = (bf16[512,512]{1,0:T(8,128)(2,1)}, bf16[512,512]{1,0:T(8,128)(2,1)S(1)}, u32[]{:S(2)}, u32[]{:S(2)}) collective-permute-start(bf16[512,512]{1,0:T(8,128)(2,1)} %refs_2_.2), channel_id=1, source_target_pairs={{0,2},{1,3},{2,0},{3,1},{4,6},{5,7},{6,4},{7,5},{8,10},{9,11},{10,... | collective-permute-start | bytes 1572872 | tf_op jit(solution)/shard_map/ppermute | solution.py:458
  11.6 13.0 %collective-permute-start = (bf16[512,512]{1,0:T(8,128)(2,1)}, bf16[512,512]{1,0:T(8,128)(2,1)S(1)}, u32[]{:S(2)}, u32[]{:S(2)}) collective-permute-start(bf16[512,512]{1,0:T(8,128)(2,1)} %refs_2_.2), channel_id=1, source_target_pairs={{0,4},{1,5},{2,6},{3,7},{4,0},{5,1},{6,2},{7,3},{8,12},{9,13},{10,... | collective-permute-start | bytes 1572872 | tf_op jit(solution)/shard_map/ppermute | solution.py:458
  12.1 22.9 %collective-permute-start.8 = (bf16[512,512]{1,0:T(8,128)(2,1)}, bf16[512,512]{1,0:T(8,128)(2,1)}, u32[]{:S(2)}, u32[]{:S(2)}) collective-permute-start(bf16[512,512]{1,0:T(8,128)(2,1)} %refs_2_.2), channel_id=1, source_target_pairs={{0,1},{1,0},{2,3},{3,2},{4,5},{5,4},{6,7},{7,6},{8,9},{9,8},{10,11... | collective-permute-start | bytes 1572872 | tf_op jit(solution)/shard_map/ppermute | solution.py:458
  23.5 16.3 %collective-permute-start.6 = (bf16[512,512]{1,0:T(8,128)(2,1)S(1)}, bf16[512,512]{1,0:T(8,128)(2,1)S(1)}, u32[]{:S(2)}, u32[]{:S(2)}) collective-permute-start(bf16[512,512]{1,0:T(8,128)(2,1)S(1)} %collective-permute-done.3.refs_4_), channel_id=1, source_target_pairs={{0,1},{1,0},{2,3},{3,2},{4,5},{5,4},{6,7},{7,6},{8,9},{9,8},{10,11... | collective-permute-start | bytes 1572872 | tf_op jit(solution)/shard_map/ppermute | solution.py:458
  24.7 15.1 %collective-permute-start.7 = (bf16[512,512]{1,0:T(8,128)(2,1)S(1)}, bf16[512,512]{1,0:T(8,128)(2,1)S(1)}, u32[]{:S(2)}, u32[]{:S(2)}) collective-permute-start(bf16[512,512]{1,0:T(8,128)(2,1)S(1)} %collective-permute-done.refs_6_), channel_id=1, source_target_pairs={{0,1},{1,0},{2,3},{3,2},{4,5},{5,4},{6,7},{7,6},{8,9},{9,8},{10,11... | collective-permute-start | bytes 1572872 | tf_op jit(solution)/shard_map/ppermute | solution.py:458
  25.4 9.0 %collective-permute-start.1 = (bf16[256,512]{1,0:T(8,128)(2,1)}, bf16[256,512]{1,0:T(8,128)(2,1)}, u32[]{:S(2)}, u32[]{:S(2)}) collective-permute-start(bf16[256,512]{1,0:T(8,128)(2,1)} %slice.8), channel_id=1, source_target_pairs={{0,2},{1,3},{2,0},{3,1},{4,6},{5,7},{6,4},{7,5},{8,10},{9,11},{10,... | collective-permute-start | bytes 786440 | tf_op jit(solution)/shard_map/ppermute | solution.py:458
  26.2 8.4 %collective-permute-start.4 = (bf16[256,512]{1,0:T(8,128)(2,1)S(1)}, bf16[256,512]{1,0:T(8,128)(2,1)}, u32[]{:S(2)}, u32[]{:S(2)}) collective-permute-start(bf16[256,512]{1,0:T(8,128)(2,1)S(1)} %slice.9), channel_id=1, source_target_pairs={{0,4},{1,5},{2,6},{3,7},{4,0},{5,1},{6,2},{7,3},{8,12},{9,13},{10,... | collective-permute-start | bytes 786440 | tf_op jit(solution)/shard_map/ppermute | solution.py:458
  34.4 7.2 %collective-permute-start.2 = (bf16[256,512]{1,0:T(8,128)(2,1)}, bf16[256,512]{1,0:T(8,128)(2,1)S(1)}, u32[]{:S(2)}, u32[]{:S(2)}) collective-permute-start(bf16[256,512]{1,0:T(8,128)(2,1)} %collective-permute-done.1.refs_2_), channel_id=1, source_target_pairs={{0,1},{1,0},{2,3},{3,2},{4,5},{5,4},{6,7},{7,6},{8,9},{9,8},{10,11... | collective-permute-start | bytes 786440 | tf_op jit(solution)/shard_map/ppermute | solution.py:458
  34.6 7.1 %collective-permute-start.5 = (bf16[256,512]{1,0:T(8,128)(2,1)}, bf16[256,512]{1,0:T(8,128)(2,1)S(1)}, u32[]{:S(2)}, u32[]{:S(2)}) collective-permute-start(bf16[256,512]{1,0:T(8,128)(2,1)} %collective-permute-done.4.refs_4_), channel_id=1, source_target_pairs={{0,1},{1,0},{2,3},{3,2},{4,5},{5,4},{6,7},{7,6},{8,9},{9,8},{10,11... | collective-permute-start | bytes 786440 | tf_op jit(solution)/shard_map/ppermute | solution.py:458
  35.0 2.2 %copy-start = (bf16[512,4096]{1,0:T(8,128)(2,1)S(1)}, bf16[512,4096]{1,0:T(8,128)(2,1)}, u32[]{:S(2)}) copy-start(bf16[512,4096]{1,0:T(8,128)(2,1)} %refs_1_.5) | copy-start | bytes 12582916
  39.7 1.9 %copy-start.9 = (bf16[512,512]{1,0:T(8,128)(2,1)S(1)}, bf16[512,512]{1,0:T(8,128)(2,1)}, u32[]{:S(2)}) copy-start(bf16[512,512]{1,0:T(8,128)(2,1)} %refs_7_.1) | copy-start | bytes 1572868
  41.6 7.7 %copy-start.1 = (bf16[7,512,256]{2,1,0:T(8,128)(2,1)S(1)}, bf16[7,512,256]{2,1,0:T(8,128)(2,1)}, u32[]{:S(2)}) copy-start(bf16[7,512,256]{2,1,0:T(8,128)(2,1)} %constant.17.clone.table_ref.f_ref) | copy-start | bytes 5505028
  41.6 7.7 %copy-start.7 = (bf16[2,256,256]{2,1,0:T(8,128)(2,1)S(1)}, bf16[2,256,256]{2,1,0:T(8,128)(2,1)}, u32[]{:S(2)}) copy-start(bf16[2,256,256]{2,1,0:T(8,128)(2,1)} %constant.16.clone.real_ref.fr_ref) | copy-start | bytes 786436
  44.9 10.1 %collective-permute-start.10 = (bf16[512,128]{1,0:T(8,128)(2,1)}, bf16[512,128]{1,0:T(8,128)(2,1)S(1)}, u32[]{:S(2)}, u32[]{:S(2)}) collective-permute-start(bf16[512,128]{1,0:T(8,128)(2,1)} %get-tuple-element.13), channel_id=1, source_target_pairs={{0,16},{8,24},{16,0},{24,8},{1,17},{9,25},{17,1},{25,9},{2,18},{10... | collective-permute-start | bytes 393224 | tf_op jit(solution)/shard_map/ppermute | solution.py:458
  45.2 14.8 %collective-permute-start.11 = (bf16[512,128]{1,0:T(8,128)(2,1)}, bf16[512,128]{1,0:T(8,128)(2,1)S(1)}, u32[]{:S(2)}, u32[]{:S(2)}) collective-permute-start(bf16[512,128]{1,0:T(8,128)(2,1)} %get-tuple-element.14), channel_id=1, source_target_pairs={{0,24},{8,16},{16,8},{24,0},{1,25},{9,17},{17,9},{25,1},{2,26},{10... | collective-permute-start | bytes 393224 | tf_op jit(solution)/shard_map/ppermute | solution.py:458
  47.8 12.2 %collective-permute-start.9 = (bf16[512,128]{1,0:T(8,128)(2,1)}, bf16[512,128]{1,0:T(8,128)(2,1)}, u32[]{:S(2)}, u32[]{:S(2)}) collective-permute-start(bf16[512,128]{1,0:T(8,128)(2,1)} %get-tuple-element.12), channel_id=1, source_target_pairs={{0,8},{8,0},{16,24},{24,16},{1,9},{9,1},{17,25},{25,17},{2,10},{10... | collective-permute-start | bytes 393224 | tf_op jit(solution)/shard_map/ppermute | solution.py:458
  49.3 10.7 %copy-start.6 = (bf16[7,512,256]{2,1,0:T(8,128)(2,1)S(1)}, bf16[7,512,256]{2,1,0:T(8,128)(2,1)}, u32[]{:S(2)}) copy-start(bf16[7,512,256]{2,1,0:T(8,128)(2,1)} %constant.19.clone.b_ref) | copy-start | bytes 5505028
  49.3 10.7 %copy-start.10 = (bf16[2,256,256]{2,1,0:T(8,128)(2,1)S(1)}, bf16[2,256,256]{2,1,0:T(8,128)(2,1)}, u32[]{:S(2)}) copy-start(bf16[2,256,256]{2,1,0:T(8,128)(2,1)} %constant.18.clone.br_ref) | copy-start | bytes 786436
  60.0 31.6 %copy-start.3 = (bf16[512,512]{1,0:T(8,128)(2,1)S(1)}, bf16[512,512]{1,0:T(8,128)(2,1)}, u32[]{:S(2)}) copy-start(bf16[512,512]{1,0:T(8,128)(2,1)} %key_ref.3) | copy-start | bytes 1572868
  60.0 31.6 %copy-start.5 = (bf16[512,512]{1,0:T(8,128)(2,1)S(1)}, bf16[512,512]{1,0:T(8,128)(2,1)}, u32[]{:S(2)}) copy-start(bf16[512,512]{1,0:T(8,128)(2,1)} %value_ref.3) | copy-start | bytes 1572868
  65.2 9.7 %collective-permute-start.12 = (bf16[512,256]{1,0:T(8,128)(2,1)S(1)}, bf16[512,256]{1,0:T(8,128)(2,1)S(1)}, u32[]{:S(2)}, u32[]{:S(2)}) collective-permute-start(bf16[512,256]{1,0:T(8,128)(2,1)S(1)} %get-tuple-element.16), channel_id=1, source_target_pairs={{0,8},{8,0},{16,24},{24,16},{1,9},{9,1},{17,25},{25,17},{2,10},{10... | collective-permute-start | bytes 786440 | tf_op jit(solution)/shard_map/ppermute | solution.py:458
  65.3 18.9 %collective-permute-start.13 = (bf16[512,256]{1,0:T(8,128)(2,1)S(1)}, bf16[512,256]{1,0:T(8,128)(2,1)S(1)}, u32[]{:S(2)}, u32[]{:S(2)}) collective-permute-start(bf16[512,256]{1,0:T(8,128)(2,1)S(1)} %get-tuple-element.17), channel_id=1, source_target_pairs={{0,16},{8,24},{16,0},{24,8},{1,17},{9,25},{17,1},{25,9},{2,18},{10... | collective-permute-start | bytes 786440 | tf_op jit(solution)/shard_map/ppermute | solution.py:458
  66.4 25.2 %collective-permute-start.14 = (bf16[512,256]{1,0:T(8,128)(2,1)S(1)}, bf16[512,256]{1,0:T(8,128)(2,1)S(1)}, u32[]{:S(2)}, u32[]{:S(2)}) collective-permute-start(bf16[512,256]{1,0:T(8,128)(2,1)S(1)} %get-tuple-element.18), channel_id=1, source_target_pairs={{0,24},{8,16},{16,8},{24,0},{1,25},{9,17},{17,9},{25,1},{2,26},{10... | collective-permute-start | bytes 786440 | tf_op jit(solution)/shard_map/ppermute | solution.py:458

commit v2 on v1

--- a/solution.py
+++ b/solution.py
@@ -120,76 +120,103 @@
     return out
 
 
-def pack_kernel(taps_ref, key_ref, value_ref, out_ref):
-    for j in range(out_ref.shape[0]):
-        cols = slice(j * LANES, (j + 1) * LANES)
-        out_ref[j, :, :LANES] = taps_ref[:, cols]
-        product = key_ref[:, cols].astype(F32) * value_ref[:, cols].astype(F32)
-        out_ref[j, :, LANES:] = product.astype(BF16)
-
-
-def spectrum_kernel(x_ref, real_ref, table_ref, out_ref, yr_ref, yi_ref):
-    rows = real_ref.shape[1]
-    step = 16
+HALF = LANES // 2
+
+
+def low_lanes(shape):
+    return lax.broadcasted_iota(jnp.int32, shape, 1) < HALF
+
+
+def swap_halves(a):
+    return pltpu.roll(a, HALF, 1)
+
+
+def join_low(a, b):
+    return jnp.where(low_lanes(a.shape), a, swap_halves(b))
+
+
+def join_high(a, b):
+    return jnp.where(low_lanes(a.shape), swap_halves(a), b)
+
+
+def pack_kernel(taps_hbm, key_hbm, value_hbm, out_hbm, taps_ref, key_ref, value_ref, out_ref, in_sems, out_sems):
+    parts = out_ref.shape[0]
+    reads = []
+    for j in range(parts):
+        cols = pl.ds(j * LANES, LANES)
+        for i, (src, dst) in enumerate(((key_hbm, key_ref), (value_hbm, value_ref), (taps_hbm, taps_ref))):
+            reads.append(pltpu.make_async_copy(src.at[:, cols], dst.at[j], in_sems.at[i, j]))
+            reads[-1].start()
+    writes = []
+    for j in range(parts):
+        for read in reads[3 * j : 3 * j + 3]:
+            read.wait()
+        inner = key_ref[j].astype(F32) * value_ref[j].astype(F32)
+        taps = taps_ref[j].astype(F32)
+        out_ref[j, :, :LANES] = join_low(taps, inner).astype(BF16)
+        out_ref[j, :, LANES:] = join_high(taps, inner).astype(BF16)
+        writes.append(pltpu.make_async_copy(out_ref.at[j], out_hbm.at[j], out_sems.at[j]))
+        writes[-1].start()
+    for write in writes:
+        write.wait()
+
+
+def fold_into(y_ref, x_ref, lane=0):
+    rows, step = y_ref.shape[1], 16
 
     def fold(i, carry):
         at = pl.multiple_of(i * step, step)
-        x = [x_ref[pl.ds(j * rows + at, step), :].astype(F32) for j in range(8)]
-        for r, (re, im) in enumerate(fold_forward(x)):
-            yr_ref[r, pl.ds(at, step), :] = re.astype(BF16)
-            if im is not None:
-                yi_ref[r, pl.ds(at, step), :] = im.astype(BF16)
+        y = fold_forward([x_ref[pl.ds(j * rows + at, step), lane : lane + LANES].astype(F32) for j in range(8)])
+        for r in range(8):
+            left, right = y[r] if r else (y[0][0], y[8][0])
+            y_ref[r, pl.ds(at, step), :LANES] = left.astype(BF16)
+            y_ref[r, pl.ds(at, step), LANES:] = right.astype(BF16)
         return carry
 
-    lax.fori_loop(0, rows // step, fold, 0)
-    dot = functools.partial(jnp.dot, preferred_element_type=F32)
-    out_ref[0, :rows] = dot(real_ref[0], yr_ref[0]).astype(out_ref.dtype)
-    out_ref[0, rows:] = dot(real_ref[1], yr_ref[8]).astype(out_ref.dtype)
+    lax.fori_loop(0, rows // step, fold, 0, unroll=rows // step)
+
+
+def dot(a, b):
+    return jnp.dot(a, b, preferred_element_type=F32)
+
+
+def spectrum_kernel(lane, x_ref, real_ref, table_ref, out_ref, y_ref):
+    rows = real_ref.shape[1]
+    fold_into(y_ref, x_ref, lane)
+    out_ref[0, :rows] = dot(real_ref[0], y_ref[0, :, :LANES]).astype(out_ref.dtype)
+    out_ref[0, rows:] = dot(real_ref[1], y_ref[0, :, LANES:]).astype(out_ref.dtype)
     for r in range(1, 8):
-        a = dot(table_ref[r - 1], yr_ref[r])
-        b = dot(table_ref[r - 1], yi_ref[r])
-        out_ref[r, :rows] = (a[:rows] + b[rows:]).astype(out_ref.dtype)
-        out_ref[r, rows:] = (b[:rows] - a[rows:]).astype(out_ref.dtype)
+        d = dot(table_ref[r - 1], y_ref[r])
+        out_ref[r, :rows] = (d[:rows, :LANES] + d[rows:, LANES:]).astype(out_ref.dtype)
+        out_ref[r, rows:] = (d[:rows, LANES:] - d[rows:, :LANES]).astype(out_ref.dtype)
 
 
 def correlate_kernel(ids_ref, g0, g1, g2, g3, spec_ref, fr_ref, f_ref, br_ref, b_ref, o0, o1, o2, o3, x_ref, y_ref, zr_ref, zi_ref, res_ref):
     rows = fr_ref.shape[1]
     half = rows // 2
-    length = g0.shape[0]
+    length = 2 * rows
     step = 16
     z = ids_ref[0]
-    dot = functools.partial(jnp.dot, preferred_element_type=F32)
     for s, g in enumerate((g0, g1, g2, g3)):
-        x_ref[pl.ds(pl.multiple_of((z ^ s) * length, length), length), :] = g[...]
-
-    def fold(i, carry):
-        at = pl.multiple_of(i * step, step)
-        x = [x_ref[pl.ds(j * rows + at, step), :].astype(F32) for j in range(8)]
-        y = fold_forward(x)
-        y_ref[0, pl.ds(at, step), :LANES] = y[0][0].astype(BF16)
-        y_ref[0, pl.ds(at, step), LANES:] = y[8][0].astype(BF16)
-        for r in range(1, 8):
-            y_ref[r, pl.ds(at, step), :LANES] = y[r][0].astype(BF16)
-            y_ref[r, pl.ds(at, step), LANES:] = y[r][1].astype(BF16)
-        return carry
-
-    lax.fori_loop(0, rows // step, fold, 0)
-    twice = lambda a: jnp.concatenate([a, a], axis=1)
+        start = pl.multiple_of((z ^ s) * length, length)
+        both = g[...].astype(F32)
+        x_ref[pl.ds(start, rows), :] = join_low(both, both).astype(BF16)
+        x_ref[pl.ds(start + rows, rows), :] = join_high(both, both).astype(BF16)
+
+    fold_into(y_ref, x_ref)
+    beside = lambda a, b: jnp.concatenate([a, b], axis=1).astype(BF16)
 
     for r in range(1, 8):
         d = dot(f_ref[r - 1], y_ref[r])
-        gr = twice(d[:rows, :LANES] + d[rows:, LANES:])
-        gi = twice(d[:rows, LANES:] - d[rows:, :LANES])
+        gr = d[:rows, :LANES] + d[rows:, LANES:]
+        gi = d[:rows, LANES:] - d[rows:, :LANES]
         ar, ai = spec_ref[r, :rows].astype(F32), spec_ref[r, rows:].astype(F32)
-        pr = (ar * gr + ai * gi).astype(BF16)
-        pi = (ar * gi - ai * gr).astype(BF16)
-        p = dot(b_ref[r - 1], pr)
-        q = dot(b_ref[r - 1], pi)
-        zr_ref[r] = p[:rows] - q[rows:]
-        zi_ref[r] = q[:rows] + p[rows:]
-    first = lax.broadcasted_iota(jnp.int32, (half, 2 * LANES), 0) == 0
+        p = dot(b_ref[r - 1], beside(ar * gr + ai * gi, ar * gi - ai * gr))
+        zr_ref[r] = p[:rows, :LANES] - p[rows:, LANES:]
+        zi_ref[r] = p[:rows, LANES:] + p[rows:, :LANES]
+    first = lax.broadcasted_iota(jnp.int32, (half, LANES), 0) == 0
     for slot, r in ((0, 0), (1, 8)):
-        g = twice(dot(fr_ref[slot], y_ref[0, :, slot * LANES : (slot + 1) * LANES]))
+        g = dot(fr_ref[slot], y_ref[0, :, slot * LANES : (slot + 1) * LANES])
         a = spec_ref[0, slot * rows : (slot + 1) * rows].astype(F32)
         gr, gi, ar, ai = g[:half], g[half:], a[:half], a[half:]
         pr = ar * gr + ai * gi
@@ -202,55 +229,63 @@
 
     def unfold(i, carry):
         at = pl.multiple_of(i * step, step)
-        for lane in (0, LANES):
-            pick = lambda ref, r: ref[r, pl.ds(at, step), lane : lane + LANES]
-            zs = [(pick(zr_ref, r), pick(zi_ref, r) if 0 < r < 8 else None) for r in range(9)]
-            for j, out in enumerate(fold_backward(zs)):
-                res_ref[pl.ds(j * rows + at, step), lane : lane + LANES] = (out * scale).astype(BF16)
+        zs = [(zr_ref[r, pl.ds(at, step), :], zi_ref[r, pl.ds(at, step), :] if 0 < r < 8 else None) for r in range(9)]
+        for j, out in enumerate(fold_backward(zs)):
+            res_ref[pl.ds(j * rows + at, step), :] = (out * scale).astype(BF16)
         return carry
 
-    lax.fori_loop(0, rows // step, unfold, 0)
+    lax.fori_loop(0, rows // step, unfold, 0, unroll=rows // step)
     for s, o in enumerate((o0, o1, o2, o3)):
         o[...] = res_ref[pl.ds(pl.multiple_of((z ^ s) * length, length), length), :]
 
 
-def finish_kernel(factor, ids_ref, r0, r1, r2, r3, key_ref, value_ref, gk_ref, gv_ref, gt_ref):
+def finish_kernel(factor, ids_ref, *refs):
+    lows, highs = refs[:4], refs[4:8]
+    key_ref, value_ref, gk_ref, gv_ref, gt_ref = refs[8:]
     z = ids_ref[0]
-    for s, r in enumerate((r0, r1, r2, r3)):
+    for s in range(4):
+        low, high = lows[s][...].astype(F32), highs[s][...].astype(F32)
         cols = pl.ds(pl.multiple_of((z ^ s) * LANES, LANES), LANES)
-        grad = r[:, :LANES].astype(F32)
+        gt_ref[:, cols] = join_high(low, high) * factor
+        grad = join_low(low, high)
         gk_ref[:, cols] = (value_ref[:, cols].astype(F32) * grad).astype(BF16)
         gv_ref[:, cols] = (key_ref[:, cols].astype(F32) * grad).astype(BF16)
-        gt_ref[:, cols] = r[:, LANES:].astype(F32) * factor
-
-
-def project_kernel(n_weights, pairs, has_total, has_gate, ids_ref, *refs):
-    refs = list(refs)
-    weights = [refs.pop(0) for _ in range(n_weights)]
-    blocks = [refs.pop(0) for _ in range(1 + max(p[0] for p in pairs))]
-    before = refs.pop(0) if has_total else None
-    gate = refs.pop(0) if has_gate else None
-    sums = refs.pop() if has_gate else refs[0]
-    rows = sums.shape[0]
-    edges = sorted({p[2] for p in pairs}) + [rows]
-    for lo, hi in zip(edges[:-1], edges[1:]):
-        acc = before[lo:hi] if has_total else None
-        for b, w, first in pairs:
-            block = blocks[b]
-            if not (first <= lo and hi <= first + block.shape[0]):
-                continue
-            part = lax.dot_general(block[lo - first : hi - first, :], weights[w][...], (((1,), (1,)), ((), ())), preferred_element_type=F32)
-            acc = part if acc is None else acc + part
-        sums[lo:hi] = acc
-    if has_gate:
-        z = ids_ref[0]
-        for s, o in enumerate(refs):
-            cols = pl.ds(pl.multiple_of((z ^ s) * LANES, LANES), LANES)
-            o[...] = (gate[:, cols].astype(F32) * sums[:, cols]).astype(BF16)
+
+
+def project_near_kernel(ids_ref, weight_ref, *refs):
+    *blocks, sums, turned = refs
+    depth = blocks[0].shape[1]
+
+    def weight(distance):
+        return weight_ref[:, pl.ds(pl.multiple_of((ids_ref[1] ^ distance) * depth, depth), depth)]
+
+    acc = None
+    for distance, block in enumerate(blocks):
+        part = lax.dot_general(block[...], weight(distance), (((1,), (1,)), ((), ())), preferred_element_type=F32)
+        acc = part if acc is None else acc + part
+    sums[...] = acc
+    for i in range(2):
+        turned[i * depth : (i + 1) * depth] = weight(len(blocks) + i).T
+
+
+def project_far_kernel(ids_ref, turned_ref, top0, top1, low0, low1, before, gate, *refs):
+    outs, (block, sums) = refs[:-2], refs[-2:]
+    half, depth = top0.shape
+    for i, (top, low) in enumerate(((top0, low0), (top1, low1))):
+        block[:half, i * depth : (i + 1) * depth] = top[...]
+        block[half:, i * depth : (i + 1) * depth] = low[...]
+    sums[...] = before[...] + dot(block[...], turned_ref[...])
+    z = ids_ref[0]
+    for s in range(4):
+        cols = pl.ds(pl.multiple_of((z ^ s) * LANES, LANES), LANES)
+        grad = gate[:, cols].astype(F32) * sums[:, cols]
+        outs[s][...] = join_low(grad[:half], grad[half:]).astype(BF16)
+        outs[4 + s][...] = join_high(grad[:half], grad[half:]).astype(BF16)
 
 
 VMEM = pl.BlockSpec(memory_space=pltpu.VMEM)
 SMEM = pl.BlockSpec(memory_space=pltpu.SMEM)
+ANY = pl.BlockSpec(memory_space=pl.ANY)
 
 
 def cost(flops, nbytes):
@@ -261,90 +296,90 @@
     return pltpu.CompilerParams(vmem_limit_bytes=mib * 2**20)
 
 
-def project(ids, weight, offsets, blocks, pairs, before=None, gate=None, rows=None):
+def project_near(ids, weight, blocks, hint):
     channels = weight.shape[0]
-    depth = blocks[0].shape[1]
-    rows = rows or max(p[2] + blocks[p[0]].shape[0] for p in pairs)
-    whole = lambda a: pl.BlockSpec(a.shape, lambda i, ids: (0, 0))
-    ins = [weight] * len(offsets) + list(blocks)
-    specs = [pl.BlockSpec((channels, depth), (lambda m: lambda i, ids: (0, ids[1] ^ m))(m)) for m in offsets]
-    specs += [whole(b) for b in blocks]
-    for extra in (before, gate):
-        if extra is not None:
-            ins.append(extra)
-            specs.append(whole(extra))
-    if gate is None:
-        shapes = jax.ShapeDtypeStruct((rows, channels), F32)
-        outs, scratch = whole(shapes), []
-    else:
-        shapes = [jax.ShapeDtypeStruct((rows, LANES), BF16)] * (channels // LANES)
-        outs, scratch = [whole(s) for s in shapes], [pltpu.VMEM((rows, channels), F32)]
-    kernel = functools.partial(project_kernel, len(offsets), tuple(pairs), before is not None, gate is not None)
-    flops = 2 * sum(blocks[p[0]].shape[0] for p in pairs) * depth * channels
+    rows, depth = blocks[0].shape
     return pl.pallas_call(
-        kernel,
-        grid_spec=pltpu.PrefetchScalarGridSpec(num_scalar_prefetch=1, grid=(1,), in_specs=specs, out_specs=outs, scratch_shapes=scratch),
-        out_shape=shapes,
-        compiler_params=limits(32),
-        cost_estimate=cost(flops, sum(a.size * a.dtype.itemsize for a in ins[len(offsets):]) + 2 * len(offsets) * channels * depth),
-    )(ids, *ins)
+        project_near_kernel,
+        in_specs=[SMEM] + [VMEM] * (1 + len(blocks)),
+        out_specs=[VMEM] * 2,
+        out_shape=[jax.ShapeDtypeStruct((rows, channels), F32), jax.ShapeDtypeStruct((2 * depth, channels), BF16)],
+        compiler_params=limits(24),
+        cost_estimate=cost(int(hint), 0),
+    )(ids, weight, *blocks)
+
+
+def project_far(ids, turned, blocks, before, gate):
+    rows, channels = gate.shape
+    return pl.pallas_call(
+        project_far_kernel,
+        in_specs=[SMEM] + [VMEM] * 7,
+        out_specs=[VMEM] * 8,
+        out_shape=[jax.ShapeDtypeStruct((rows // 2, LANES), BF16)] * 8,
+        scratch_shapes=[pltpu.VMEM((rows, turned.shape[0]), BF16), pltpu.VMEM((rows, channels), F32)],
+        compiler_params=limits(24),
+        cost_estimate=cost(2 * rows * turned.size, 0),
+    )(ids, turned, *blocks, before, gate)
 
 
 def pack(taps, key, value, parts):
     length = taps.shape[0]
+    shape = (parts, length, 2 * LANES)
     return pl.pallas_call(
         pack_kernel,
-        out_shape=jax.ShapeDtypeStruct((parts, length, 2 * LANES), BF16),
+        out_shape=jax.ShapeDtypeStruct(shape, BF16),
+        in_specs=[ANY] * 3,
+        out_specs=ANY,
+        scratch_shapes=[pltpu.VMEM((parts, length, LANES), BF16)] * 3
+        + [pltpu.VMEM(shape, BF16), pltpu.SemaphoreType.DMA((3, parts)), pltpu.SemaphoreType.DMA((parts,))],
+        compiler_params=limits(56),
+        cost_estimate=cost(0, 10 * taps.size),
+    )(taps, key, value)
+
+
+def block_spectrum(x, lane, real, table):
+    rows = real.shape[1]
+    return pl.pallas_call(
+        functools.partial(spectrum_kernel, lane),
+        out_shape=jax.ShapeDtypeStruct((8, 2 * rows, LANES), BF16),
         in_specs=[VMEM] * 3,
         out_specs=VMEM,
-        compiler_params=limits(16),
-        cost_estimate=cost(taps.size, 5 * 2 * taps.size),
-    )(taps, key, value)
-
-
-def block_spectrum(x, real, table):
-    rows = real.shape[1]
-    return pl.pallas_call(
-        spectrum_kernel,
-        out_shape=jax.ShapeDtypeStruct((8, 2 * rows, 2 * LANES), BF16),
-        in_specs=[VMEM] * 3,
-        out_specs=VMEM,
-        scratch_shapes=[pltpu.VMEM((9, rows, 2 * LANES), BF16), pltpu.VMEM((8, rows, 2 * LANES), BF16)],
+        scratch_shapes=[pltpu.VMEM((8, rows, 2 * LANES), BF16)],
         compiler_params=limits(24),
-        cost_estimate=cost(2 * 15 * 2 * rows * rows * 2 * LANES, 2 * (x.size + table.size + 16 * rows * 2 * LANES)),
+        cost_estimate=cost(2 * 8 * 2 * rows * rows * 2 * LANES, 0),
     )(x, real, table)
 
 
 def correlate(ids, grads, spec, tables):
-    length = grads[0].shape[0]
     rows = tables[0].shape[1]
+    length = 2 * rows
     return pl.pallas_call(
         correlate_kernel,
-        out_shape=[jax.ShapeDtypeStruct((length, 2 * LANES), BF16)] * 4,
+        out_shape=[jax.ShapeDtypeStruct((length, LANES), BF16)] * 4,
         in_specs=[SMEM] + [VMEM] * 9,
         out_specs=[VMEM] * 4,
         scratch_shapes=[
             pltpu.VMEM((8 * rows, LANES), BF16),
             pltpu.VMEM((8, rows, 2 * LANES), BF16),
-            pltpu.VMEM((9, rows, 2 * LANES), F32),
-            pltpu.VMEM((8, rows, 2 * LANES), F32),
-            pltpu.VMEM((8 * rows, 2 * LANES), BF16),
+            pltpu.VMEM((9, rows, LANES), F32),
+            pltpu.VMEM((8, rows, LANES), F32),
+            pltpu.VMEM((8 * rows, LANES), BF16),
         ],
-        compiler_params=limits(32),
-        cost_estimate=cost(2 * 8 * 6 * rows * rows * 2 * LANES, 2 * (4 * length * LANES * 3 + spec.size + 2 * tables[1].size)),
+        compiler_params=limits(24),
+        cost_estimate=cost(2 * 8 * 4 * rows * rows * 2 * LANES, 0),
     )(ids, *grads, spec, *tables)
 
 
-def finish(ids, parts, key, value, factor):
+def finish(ids, lows, highs, key, value, factor):
     shape = key.shape
     return pl.pallas_call(
         functools.partial(finish_kernel, factor),
         out_shape=[jax.ShapeDtypeStruct(shape, BF16), jax.ShapeDtypeStruct(shape, BF16), jax.ShapeDtypeStruct(shape, F32)],
-        in_specs=[SMEM] + [VMEM] * 6,
+        in_specs=[SMEM] + [VMEM] * 10,
         out_specs=[VMEM] * 3,
-        compiler_params=limits(16),
+        compiler_params=limits(24),
         cost_estimate=cost(4 * key.size, 16 * key.size),
-    )(ids, *parts, key, value)
+    )(ids, *lows, *highs, key, value)
 
 
 PRECISION = lax.Precision.HIGH
@@ -453,6 +488,7 @@
     return (grad_key, grad_value, grad_taps)
 
 
+HINT = 5e9
 def hop(x, axis, distance):
     n = lax.axis_size(axis)
     return lax.ppermute(x, axis, [(j, j ^ distance) for j in range(n)])
@@ -464,20 +500,21 @@
     tables = [jnp.asarray(t) for t in spectral_tables(2 * parts * length)]
     ids = jnp.stack([lax.axis_index("ctx"), lax.axis_index("ch")]).astype(jnp.int32)
     half = length // 2
+    from_x, from_y, from_core = hop(output_grad, "ch", 2), hop(output_grad, "ch", 4), hop(output_grad, "ch", 1)
     sent = pack(filter_taps, key_proj, value_proj, parts)
-    from_x, from_y, from_core = hop(output_grad, "ch", 2), hop(output_grad, "ch", 4), hop(output_grad, "ch", 1)
     series = lax.all_to_all(sent, "ctx", 0, 0, tiled=True).reshape(parts * length, 2 * LANES)
-    spec = block_spectrum(series, tables[0], tables[1])
-    total = project(ids, output_weight, (0, 1), [output_grad, from_core], [(0, 0, 0), (1, 1, 0)])
+    low_spec, high_spec = [block_spectrum(series, lane, tables[0], tables[1]) for lane in (0, LANES)]
     far_top, far_low = hop(from_y[:half], "ch", 2), hop(from_x[half:], "ch", 4)
     core_x, core_y = hop(from_x, "ch", 1), hop(from_y, "ch", 1)
-    total = project(ids, output_weight, (2, 3, 4, 5), [from_x, core_x, from_y, core_y], [(j, j, 0) for j in range(4)], before=total)
+    total, turned = project_near(ids, output_weight, [output_grad, from_core, from_x, core_x, from_y, core_y], HINT)
+    far_top, far_low, total = lax.optimization_barrier((far_top, far_low, total))
     core_top, core_low = hop(far_top, "ch", 1), hop(far_low, "ch", 1)
-    grads = project(ids, output_weight, (6, 7), [far_top, core_top, far_low, core_low], [(0, 0, 0), (1, 1, 0), (2, 0, half), (3, 1, half)], before=total, gate=query_gate)
-    grads = [grads[0]] + [hop(grads[s], "ctx", s) for s in range(1, parts)]
-    results = correlate(ids, grads, spec, tables)
-    results = [results[0]] + [hop(results[s], "ctx", s) for s in range(1, parts)]
-    return tuple(finish(ids, results, key_proj, value_proj, 1.0 / math.sqrt(parts * length)))
+    grads = project_far(ids, turned, [far_top, core_top, far_low, core_low], total, query_gate)
+    spread = lambda blocks: [blocks[0]] + [hop(blocks[s], "ctx", s) for s in range(1, parts)]
+    low_grads, high_grads = spread(grads[:parts]), spread(grads[parts:])
+    low = spread(correlate(ids, low_grads, low_spec, tables))
+    high = spread(correlate(ids, high_grads, high_spec, tables))
+    return tuple(finish(ids, low, high, key_proj, value_proj, 1.0 / math.sqrt(parts * length)))
 
 
 def per_device(*arrays):

time: 94.2 us -> 75.8 us (0.80)
  the two profiles are of different devices: /device:TPU:20 before, /device:TPU:0 now
where the time goes in v2:
time: 75.8 us; the launch traced here: 75.5 us
  starting transfers between devices  29.6 us (39%)
  waiting for transfers between devices  23.9 us (32%)
  Pallas kernels  18.1 us (24%)
  local copies, waits for them, and re-layouts  3.02 us (4%)
  between operations  0.8 us (1%)
    ppermute x21, starting transfers between devices, hop(): return lax.ppermute(x, axis, [(j, j ^ distance) for j in range(n)])  24.7 us
    ppermute x21, waiting for transfers between devices, hop(): return lax.ppermute(x, axis, [(j, j ^ distance) for j in range(n)])  18.7 us
    pallas_call x2, Pallas kernels, correlate(): pl.pallas_call(correlate_kernel, out_shape=[jax.ShapeDtypeStruct((length,...  5.75 us
    all_to_all x1, waiting for transfers between devices, exchanged_layer(): lax.all_to_all(sent, 'ctx', 0, 0, tiled=True)  5.21 us
    all_to_all x1, starting transfers between devices, exchanged_layer(): lax.all_to_all(sent, 'ctx', 0, 0, tiled=True)  4.88 us
    pallas_call x1, Pallas kernels, project_near(): pl.pallas_call(project_near_kernel, in_specs=[SMEM] + [VMEM] * (1 + len(b...  3.04 us
    unnamed x22, local copies, waits for them, and re-layouts  2.98 us
    pallas_call x1, Pallas kernels, pack(): pl.pallas_call(pack_kernel, out_shape=jax.ShapeDtypeStruct(shape, BF16),...  2.49 us
  transfers between devices with their start and end apart: 22, of which 10 were waited for; matrix products, arithmetic and copies ran while one was open for 0% of the time, Pallas kernels for 21%

profile of v2, /device:TPU:0, one launch (start us, length us, event | category | flops | bytes accessed | tf_op | source)
XLA Modules:
  0.0 75.5 jit_solution(16717949376595597869)
XLA Ops:
  0.6 3.0 %collective-permute-start.1 = (bf16[512,512]{1,0:T(8,128)(2,1)}, bf16[512,512]{1,0:T(8,128)(2,1)S(1)}, u32[]{:S(2)}, u32[]{:S(2)}) collective-permute-start(bf16[512,512]{1,0:T(8,128)(2,1)} %refs_0_.1), channel_id=1, source_target_pairs={{0,2},{1,3},{2,0},{3,1},{4,6},{5,7},{6,4},{7,5},{8,10},{9,11},{10,... | collective-permute-start | bytes 1572872 | tf_op jit(solution)/shard_map/ppermute | solution.py:494
  3.6 1.5 %collective-permute-start.3 = (bf16[512,512]{1,0:T(8,128)(2,1)}, bf16[512,512]{1,0:T(8,128)(2,1)S(1)}, u32[]{:S(2)}, u32[]{:S(2)}) collective-permute-start(bf16[512,512]{1,0:T(8,128)(2,1)} %refs_0_.1), channel_id=1, source_target_pairs={{0,4},{1,5},{2,6},{3,7},{4,0},{5,1},{6,2},{7,3},{8,12},{9,13},{10,... | collective-permute-start | bytes 1572872 | tf_op jit(solution)/shard_map/ppermute | solution.py:494
  5.2 2.5 %shard_map.123 = bf16[4,512,256]{2,1,0:T(8,128)(2,1)} custom-call(bf16[512,512]{1,0:T(8,128)(2,1)} %taps_hbm.1, bf16[512,512]{1,0:T(8,128)(2,1)} %refs_8_.1, bf16[512,512]{1,0:T(8,128)(2,1)} %refs_9_.1), custom_call_target="tpu_custom_call" | custom-call | bytes 2621440 | tf_op jit(solution)/shard_map/pallas_call | solution.py:328
  7.7 4.9 %all-to-all-start = ((bf16[4,512,256]{2,1,0:T(8,128)(2,1)}), bf16[4,512,256]{2,1,0:T(8,128)(2,1)S(1)}, u32[]{:S(2)}, u32[]{:S(2)}) async-start(bf16[4,512,256]{2,1,0:T(8,128)(2,1)} %shard_map.123), calls=%async_computation | async-start | bytes 2097152 | tf_op jit(solution)/shard_map/all_to_all | solution.py:505
  12.6 3.2 %collective-permute-done.1.refs_2_ = bf16[512,512]{1,0:T(8,128)(2,1)S(1)} collective-permute-done((bf16[512,512]{1,0:T(8,128)(2,1)}, bf16[512,512]{1,0:T(8,128)(2,1)S(1)}, u32[]{:S(2)}, u32[]{:S(2)}) %collective-permute-start.1) | collective-permute-done | bytes 524320 | tf_op jit(solution)/shard_map/ppermute | solution.py:494
  15.8 1.5 %collective-permute-done.3.refs_4_ = bf16[512,512]{1,0:T(8,128)(2,1)S(1)} collective-permute-done((bf16[512,512]{1,0:T(8,128)(2,1)}, bf16[512,512]{1,0:T(8,128)(2,1)S(1)}, u32[]{:S(2)}, u32[]{:S(2)}) %collective-permute-start.3) | collective-permute-done | bytes 524320 | tf_op jit(solution)/shard_map/ppermute | solution.py:494
  17.3 0.9 %collective-permute-start.5 = (bf16[256,512]{1,0:T(8,128)(2,1)S(1)}, bf16[256,512]{1,0:T(8,128)(2,1)S(1)}, u32[]{:S(2)}, u32[]{:S(2)}) collective-permute-start(bf16[256,512]{1,0:T(8,128)(2,1)S(1)} %slice.8), channel_id=1, source_target_pairs={{0,2},{1,3},{2,0},{3,1},{4,6},{5,7},{6,4},{7,5},{8,10},{9,11},{10,... | collective-permute-start | bytes 786440 | tf_op jit(solution)/shard_map/ppermute | solution.py:494
  18.2 1.6 %collective-permute-start.6 = (bf16[256,512]{1,0:T(8,128)(2,1)S(1)}, bf16[256,512]{1,0:T(8,128)(2,1)S(1)}, u32[]{:S(2)}, u32[]{:S(2)}) collective-permute-start(bf16[256,512]{1,0:T(8,128)(2,1)S(1)} %slice.9), channel_id=1, source_target_pairs={{0,4},{1,5},{2,6},{3,7},{4,0},{5,1},{6,2},{7,3},{8,12},{9,13},{10,... | collective-permute-start | bytes 786440 | tf_op jit(solution)/shard_map/ppermute | solution.py:494
  19.8 2.2 %copy-done.7 = bf16[512,4096]{1,0:T(8,128)(2,1)S(1)} copy-done((bf16[512,4096]{1,0:T(8,128)(2,1)S(1)}, bf16[512,4096]{1,0:T(8,128)(2,1)}, u32[]{:S(2)}) %copy-start.7) | copy-done | bytes 4194328
  22.0 3.0 %shard_map.121 = (f32[512,512]{1,0:T(8,128)S(1)}, bf16[1024,512]{1,0:T(8,128)(2,1)S(1)}) custom-call(s32[2]{0:T(128)S(1)} %pad_add_fusion.ids_ref, bf16[512,4096]{1,0:T(8,128)(2,1)S(1)} %copy-done.7, bf16[512,512]{1,0:T(8,128)(2,1)S(1)} %copy-done.8, bf16[512,512]{1,0:T(8,128)(2,1)S(1)} %collective-permute-done.refs_1_, ...), custom_call_target="tpu_custom_call" | custom-call | flops 5000000000 | tf_op jit(solution)/shard_map/pallas_call | solution.py:302
  25.1 1.1 %collective-permute-done.5.top0 = bf16[256,512]{1,0:T(8,128)(2,1)S(1)} collective-permute-done((bf16[256,512]{1,0:T(8,128)(2,1)S(1)}, bf16[256,512]{1,0:T(8,128)(2,1)S(1)}, u32[]{:S(2)}, u32[]{:S(2)}) %collective-permute-start.5) | collective-permute-done | bytes 262176 | tf_op jit(solution)/shard_map/ppermute | solution.py:494
  26.3 0.5 collective-permute-start.8
  26.8 1.0 %collective-permute-done.7.top1 = bf16[256,512]{1,0:T(8,128)(2,1)S(1)} collective-permute-done((bf16[256,512]{1,0:T(8,128)(2,1)S(1)}, bf16[256,512]{1,0:T(8,128)(2,1)S(1)}, u32[]{:S(2)}, u32[]{:S(2)}) %collective-permute-start.7) | collective-permute-done | bytes 262176 | tf_op jit(solution)/shard_map/ppermute | solution.py:494
  28.2 2.2 %shard_map.122 = (bf16[256,128]{1,0:T(8,128)(2,1)S(1)}, bf16[256,128]{1,0:T(8,128)(2,1)S(1)}, bf16[256,128]{1,0:T(8,128)(2,1)}, bf16[256,128]{1,0:T(8,128)(2,1)}...) custom-call(s32[2]{0:T(128)S(1)} %pad_add_fusion.ids_ref, ...), custom_call_target="tpu_custom_call" | custom-call | flops 536870912 | tf_op jit(solution)/shard_map/pallas_call | solution.py:314
  30.4 0.6 copy-done.9
  31.1 1.7 %collective-permute-start.15 = (bf16[256,128]{1,0:T(8,128)(2,1)}, bf16[256,128]{1,0:T(8,128)(2,1)S(1)}, u32[]{:S(2)}, u32[]{:S(2)}) collective-permute-start(bf16[256,128]{1,0:T(8,128)(2,1)} %get-tuple-element.38), channel_id=1, source_target_pairs={{0,8},{8,0},{16,24},{24,16},{1,9},{9,1},{17,25},{25,17},{2,10},{10... | collective-permute-start | bytes 196616 | tf_op jit(solution)/shard_map/ppermute | solution.py:494
  32.8 2.6 %collective-permute-start.16 = (bf16[256,128]{1,0:T(8,128)(2,1)}, bf16[256,128]{1,0:T(8,128)(2,1)S(1)}, u32[]{:S(2)}, u32[]{:S(2)}) collective-permute-start(bf16[256,128]{1,0:T(8,128)(2,1)} %get-tuple-element.39), channel_id=1, source_target_pairs={{0,16},{8,24},{16,0},{24,8},{1,17},{9,25},{17,1},{25,9},{2,18},{10... | collective-permute-start | bytes 196616 | tf_op jit(solution)/shard_map/ppermute | solution.py:494
  35.5 1.9 %collective-permute-start.10 = (bf16[256,128]{1,0:T(8,128)(2,1)}, bf16[256,128]{1,0:T(8,128)(2,1)S(1)}, u32[]{:S(2)}, u32[]{:S(2)}) collective-permute-start(bf16[256,128]{1,0:T(8,128)(2,1)} %get-tuple-element.31), channel_id=1, source_target_pairs={{0,16},{8,24},{16,0},{24,8},{1,17},{9,25},{17,1},{25,9},{2,18},{10... | collective-permute-start | bytes 196616 | tf_op jit(solution)/shard_map/ppermute | solution.py:494
  37.3 1.9 %collective-permute-start.11 = (bf16[256,128]{1,0:T(8,128)(2,1)}, bf16[256,128]{1,0:T(8,128)(2,1)S(1)}, u32[]{:S(2)}, u32[]{:S(2)}) collective-permute-start(bf16[256,128]{1,0:T(8,128)(2,1)} %get-tuple-element.32), channel_id=1, source_target_pairs={{0,24},{8,16},{16,8},{24,0},{1,25},{9,17},{17,9},{25,1},{2,26},{10... | collective-permute-start | bytes 196616 | tf_op jit(solution)/shard_map/ppermute | solution.py:494
  39.2 5.2 %all-to-all-done = bf16[4,512,256]{2,1,0:T(8,128)(2,1)S(1)} async-done(((bf16[4,512,256]{2,1,0:T(8,128)(2,1)}), bf16[4,512,256]{2,1,0:T(8,128)(2,1)S(1)}, u32[]{:S(2)}, u32[]{:S(2)}) %all-to-all-start) | async-done | bytes 1048608 | tf_op jit(solution)/shard_map/all_to_all | solution.py:505
  44.5 1.1 %shard_map.126.spec_ref = bf16[8,512,128]{2,1,0:T(8,128)(2,1)S(1)} custom-call(bf16[2048,256]{1,0:T(8,128)(2,1)S(1)} %bitcast.3, bf16[2,256,256]{2,1,0:T(8,128)(2,1)S(1)} %copy-done.2, bf16[7,512,256]{2,1,0:T(8,128)(2,1)S(1)} %copy-done), custom_call_target="tpu_custom_call" | custom-call | flops 536870912 | tf_op jit(solution)/shard_map/pallas_call | solution.py:342
  46.0 3.0 %shard_map.127 = (bf16[512,128]{1,0:T(8,128)(2,1)S(1)}, bf16[512,128]{1,0:T(8,128)(2,1)S(1)}, bf16[512,128]{1,0:T(8,128)(2,1)S(1)}, bf16[512,128]{1,0:T(8,128)(2,1)S(1)}) custom-call(s32[2]{0:T(128)S(1)} %pad_add_fusion.ids_ref, bf16[256,128]{1,0:T(8,128)(2,1)S(1)} %get-tuple-element.37.g0, bf16[256,128]{1,0:T(8,128)(2,1)S(1)} %collective-permute-done.15.g1, ...), custom_call_target="tpu_custom_call" | custom-call | flops 1073741824 | tf_op jit(solution)/shard_map/pallas_call | solution.py:356
  49.0 2.0 %collective-permute-start.18 = (bf16[512,128]{1,0:T(8,128)(2,1)S(1)}, bf16[512,128]{1,0:T(8,128)(2,1)S(1)}, u32[]{:S(2)}, u32[]{:S(2)}) collective-permute-start(bf16[512,128]{1,0:T(8,128)(2,1)S(1)} %get-tuple-element.42), channel_id=1, source_target_pairs={{0,8},{8,0},{16,24},{24,16},{1,9},{9,1},{17,25},{25,17},{2,10},{10... | collective-permute-start | bytes 393224 | tf_op jit(solution)/shard_map/ppermute | solution.py:494
  51.0 1.1 %shard_map.124.spec_ref = bf16[8,512,128]{2,1,0:T(8,128)(2,1)S(1)} custom-call(bf16[2048,256]{1,0:T(8,128)(2,1)S(1)} %bitcast.4, bf16[2,256,256]{2,1,0:T(8,128)(2,1)S(1)} %copy-done.2, bf16[7,512,256]{2,1,0:T(8,128)(2,1)S(1)} %copy-done), custom_call_target="tpu_custom_call" | custom-call | flops 536870912 | tf_op jit(solution)/shard_map/pallas_call | solution.py:342
  52.1 2.5 %collective-permute-start.20 = (bf16[512,128]{1,0:T(8,128)(2,1)S(1)}, bf16[512,128]{1,0:T(8,128)(2,1)S(1)}, u32[]{:S(2)}, u32[]{:S(2)}) collective-permute-start(bf16[512,128]{1,0:T(8,128)(2,1)S(1)} %get-tuple-element.44), channel_id=1, source_target_pairs={{0,24},{8,16},{16,8},{24,0},{1,25},{9,17},{17,9},{25,1},{2,26},{10... | collective-permute-start | bytes 393224 | tf_op jit(solution)/shard_map/ppermute | solution.py:494
  54.6 2.7 %shard_map.125 = (bf16[512,128]{1,0:T(8,128)(2,1)S(1)}, bf16[512,128]{1,0:T(8,128)(2,1)S(1)}, bf16[512,128]{1,0:T(8,128)(2,1)S(1)}, bf16[512,128]{1,0:T(8,128)(2,1)S(1)}) custom-call(s32[2]{0:T(128)S(1)} %pad_add_fusion.ids_ref, bf16[256,128]{1,0:T(8,128)(2,1)S(1)} %get-tuple-element.29.g0, bf16[256,128]{1,0:T(8,128)(2,1)S(1)} %collective-permute-done.9.g1, ...), custom_call_target="tpu_custom_call" | custom-call | flops 1073741824 | tf_op jit(solution)/shard_map/pallas_call | solution.py:356
  57.4 1.1 %collective-permute-start.12 = (bf16[512,128]{1,0:T(8,128)(2,1)S(1)}, bf16[512,128]{1,0:T(8,128)(2,1)S(1)}, u32[]{:S(2)}, u32[]{:S(2)}) collective-permute-start(bf16[512,128]{1,0:T(8,128)(2,1)S(1)} %get-tuple-element.34), channel_id=1, source_target_pairs={{0,8},{8,0},{16,24},{24,16},{1,9},{9,1},{17,25},{25,17},{2,10},{10... | collective-permute-start | bytes 393224 | tf_op jit(solution)/shard_map/ppermute | solution.py:494
  58.5 0.9 %collective-permute-start.13 = (bf16[512,128]{1,0:T(8,128)(2,1)S(1)}, bf16[512,128]{1,0:T(8,128)(2,1)S(1)}, u32[]{:S(2)}, u32[]{:S(2)}) collective-permute-start(bf16[512,128]{1,0:T(8,128)(2,1)S(1)} %get-tuple-element.35), channel_id=1, source_target_pairs={{0,16},{8,24},{16,0},{24,8},{1,17},{9,25},{17,1},{25,9},{2,18},{10... | collective-permute-start | bytes 393224 | tf_op jit(solution)/shard_map/ppermute | solution.py:494
  59.4 2.4 %collective-permute-start.14 = (bf16[512,128]{1,0:T(8,128)(2,1)S(1)}, bf16[512,128]{1,0:T(8,128)(2,1)S(1)}, u32[]{:S(2)}, u32[]{:S(2)}) collective-permute-start(bf16[512,128]{1,0:T(8,128)(2,1)S(1)} %get-tuple-element.36), channel_id=1, source_target_pairs={{0,24},{8,16},{16,8},{24,0},{1,25},{9,17},{17,9},{25,1},{2,26},{10... | collective-permute-start | bytes 393224 | tf_op jit(solution)/shard_map/ppermute | solution.py:494
  61.8 1.6 %collective-permute-done.19.refs_6_ = bf16[512,128]{1,0:T(8,128)(2,1)S(1)} collective-permute-done((bf16[512,128]{1,0:T(8,128)(2,1)S(1)}, bf16[512,128]{1,0:T(8,128)(2,1)S(1)}, u32[]{:S(2)}, u32[]{:S(2)}) %collective-permute-start.19) | collective-permute-done | bytes 131104 | tf_op jit(solution)/shard_map/ppermute | solution.py:494
  63.4 9.6 %collective-permute-done.13.refs_2_ = bf16[512,128]{1,0:T(8,128)(2,1)S(1)} collective-permute-done((bf16[512,128]{1,0:T(8,128)(2,1)S(1)}, bf16[512,128]{1,0:T(8,128)(2,1)S(1)}, u32[]{:S(2)}, u32[]{:S(2)}) %collective-permute-start.13) | collective-permute-done | bytes 131104 | tf_op jit(solution)/shard_map/ppermute | solution.py:494
  73.0 2.5 %shard_map.128 = (bf16[512,512]{1,0:T(8,128)(2,1)}, bf16[512,512]{1,0:T(8,128)(2,1)}, f32[512,512]{1,0:T(8,128)}) custom-call(s32[2]{0:T(128)S(1)} %pad_add_fusion.ids_ref, bf16[512,128]{1,0:T(8,128)(2,1)S(1)} %get-tuple-element.33.refs_0_, bf16[512,128]{1,0:T(8,128)(2,1)S(1)} %collective-permute-done.12.refs_1_, ...), custom_call_target="tpu_custom_call" | custom-call | flops 1048576 | bytes 4194304 | tf_op jit(solution)/shard_map/pallas_call | solution.py:375
  (45 shorter events, 1.2 us)
Async XLA Ops:
  0.6 11.9 %copy-start.8 = (bf16[512,512]{1,0:T(8,128)(2,1)S(1)}, bf16[512,512]{1,0:T(8,128)(2,1)}, u32[]{:S(2)}) copy-start(bf16[512,512]{1,0:T(8,128)(2,1)} %refs_0_.1) | copy-start | bytes 1572868
  0.6 15.1 %collective-permute-start.1 = (bf16[512,512]{1,0:T(8,128)(2,1)}, bf16[512,512]{1,0:T(8,128)(2,1)S(1)}, u32[]{:S(2)}, u32[]{:S(2)}) collective-permute-start(bf16[512,512]{1,0:T(8,128)(2,1)} %refs_0_.1), channel_id=1, source_target_pairs={{0,2},{1,3},{2,0},{3,1},{4,6},{5,7},{6,4},{7,5},{8,10},{9,11},{10,... | collective-permute-start | bytes 1572872 | tf_op jit(solution)/shard_map/ppermute | solution.py:494
  3.6 13.6 %collective-permute-start.3 = (bf16[512,512]{1,0:T(8,128)(2,1)}, bf16[512,512]{1,0:T(8,128)(2,1)S(1)}, u32[]{:S(2)}, u32[]{:S(2)}) collective-permute-start(bf16[512,512]{1,0:T(8,128)(2,1)} %refs_0_.1), channel_id=1, source_target_pairs={{0,4},{1,5},{2,6},{3,7},{4,0},{5,1},{6,2},{7,3},{8,12},{9,13},{10,... | collective-permute-start | bytes 1572872 | tf_op jit(solution)/shard_map/ppermute | solution.py:494
  7.7 36.8 %all-to-all-start = ((bf16[4,512,256]{2,1,0:T(8,128)(2,1)}), bf16[4,512,256]{2,1,0:T(8,128)(2,1)S(1)}, u32[]{:S(2)}, u32[]{:S(2)}) async-start(bf16[4,512,256]{2,1,0:T(8,128)(2,1)} %shard_map.123), calls=%async_computation | async-start | bytes 2097152 | tf_op jit(solution)/shard_map/all_to_all | solution.py:505
  12.6 7.3 %collective-permute-start = (bf16[512,512]{1,0:T(8,128)(2,1)S(1)}, bf16[512,512]{1,0:T(8,128)(2,1)S(1)}, u32[]{:S(2)}, u32[]{:S(2)}) collective-permute-start(bf16[512,512]{1,0:T(8,128)(2,1)S(1)} %copy-done.8), channel_id=1, source_target_pairs={{0,1},{1,0},{2,3},{3,2},{4,5},{5,4},{6,7},{7,6},{8,9},{9,8},{10,11... | collective-permute-start | bytes 1572872 | tf_op jit(solution)/shard_map/ppermute | solution.py:494
  15.8 4.0 %collective-permute-start.2 = (bf16[512,512]{1,0:T(8,128)(2,1)S(1)}, bf16[512,512]{1,0:T(8,128)(2,1)}, u32[]{:S(2)}, u32[]{:S(2)}) collective-permute-start(bf16[512,512]{1,0:T(8,128)(2,1)S(1)} %collective-permute-done.1.refs_2_), channel_id=1, source_target_pairs={{0,1},{1,0},{2,3},{3,2},{4,5},{5,4},{6,7},{7,6},{8,9},{9,8},{10,11... | collective-permute-start | bytes 1572872 | tf_op jit(solution)/shard_map/ppermute | solution.py:494
  17.2 2.6 %collective-permute-start.4 = (bf16[512,512]{1,0:T(8,128)(2,1)S(1)}, bf16[512,512]{1,0:T(8,128)(2,1)}, u32[]{:S(2)}, u32[]{:S(2)}) collective-permute-start(bf16[512,512]{1,0:T(8,128)(2,1)S(1)} %collective-permute-done.3.refs_4_), channel_id=1, source_target_pairs={{0,1},{1,0},{2,3},{3,2},{4,5},{5,4},{6,7},{7,6},{8,9},{9,8},{10,11... | collective-permute-start | bytes 1572872 | tf_op jit(solution)/shard_map/ppermute | solution.py:494
  17.3 8.8 %collective-permute-start.5 = (bf16[256,512]{1,0:T(8,128)(2,1)S(1)}, bf16[256,512]{1,0:T(8,128)(2,1)S(1)}, u32[]{:S(2)}, u32[]{:S(2)}) collective-permute-start(bf16[256,512]{1,0:T(8,128)(2,1)S(1)} %slice.8), channel_id=1, source_target_pairs={{0,2},{1,3},{2,0},{3,1},{4,6},{5,7},{6,4},{7,5},{8,10},{9,11},{10,... | collective-permute-start | bytes 786440 | tf_op jit(solution)/shard_map/ppermute | solution.py:494
  18.2 10.0 %copy-start.6 = (bf16[512,512]{1,0:T(8,128)(2,1)S(1)}, bf16[512,512]{1,0:T(8,128)(2,1)}, u32[]{:S(2)}) copy-start(bf16[512,512]{1,0:T(8,128)(2,1)} %gate.1) | copy-start | bytes 1572868
  18.2 8.1 %collective-permute-start.6 = (bf16[256,512]{1,0:T(8,128)(2,1)S(1)}, bf16[256,512]{1,0:T(8,128)(2,1)S(1)}, u32[]{:S(2)}, u32[]{:S(2)}) collective-permute-start(bf16[256,512]{1,0:T(8,128)(2,1)S(1)} %slice.9), channel_id=1, source_target_pairs={{0,4},{1,5},{2,6},{3,7},{4,0},{5,1},{6,2},{7,3},{8,12},{9,13},{10,... | collective-permute-start | bytes 786440 | tf_op jit(solution)/shard_map/ppermute | solution.py:494
  19.8 2.2 %copy-start.7 = (bf16[512,4096]{1,0:T(8,128)(2,1)S(1)}, bf16[512,4096]{1,0:T(8,128)(2,1)}, u32[]{:S(2)}) copy-start(bf16[512,4096]{1,0:T(8,128)(2,1)} %weight_ref.1) | copy-start | bytes 12582916
  26.3 1.5 %collective-permute-start.7 = (bf16[256,512]{1,0:T(8,128)(2,1)S(1)}, bf16[256,512]{1,0:T(8,128)(2,1)S(1)}, u32[]{:S(2)}, u32[]{:S(2)}) collective-permute-start(bf16[256,512]{1,0:T(8,128)(2,1)S(1)} %collective-permute-done.5.top0), channel_id=1, source_target_pairs={{0,1},{1,0},{2,3},{3,2},{4,5},{5,4},{6,7},{7,6},{8,9},{9,8},{10,11... | collective-permute-start | bytes 786440 | tf_op jit(solution)/shard_map/ppermute | solution.py:494
  26.3 1.9 %collective-permute-start.8 = (bf16[256,512]{1,0:T(8,128)(2,1)S(1)}, bf16[256,512]{1,0:T(8,128)(2,1)S(1)}, u32[]{:S(2)}, u32[]{:S(2)}) collective-permute-start(bf16[256,512]{1,0:T(8,128)(2,1)S(1)} %collective-permute-done.6.low0), channel_id=1, source_target_pairs={{0,1},{1,0},{2,3},{3,2},{4,5},{5,4},{6,7},{7,6},{8,9},{9,8},{10,11... | collective-permute-start | bytes 786440 | tf_op jit(solution)/shard_map/ppermute | solution.py:494
  28.2 16.2 %copy-start = (bf16[7,512,256]{2,1,0:T(8,128)(2,1)S(1)}, bf16[7,512,256]{2,1,0:T(8,128)(2,1)}, u32[]{:S(2)}) copy-start(bf16[7,512,256]{2,1,0:T(8,128)(2,1)} %constant.17.clone.table_ref.f_ref) | copy-start | bytes 5505028
  28.2 16.2 %copy-start.2 = (bf16[2,256,256]{2,1,0:T(8,128)(2,1)S(1)}, bf16[2,256,256]{2,1,0:T(8,128)(2,1)}, u32[]{:S(2)}) copy-start(bf16[2,256,256]{2,1,0:T(8,128)(2,1)} %constant.16.clone.real_ref.fr_ref) | copy-start | bytes 786436
  31.1 14.5 %collective-permute-start.15 = (bf16[256,128]{1,0:T(8,128)(2,1)}, bf16[256,128]{1,0:T(8,128)(2,1)S(1)}, u32[]{:S(2)}, u32[]{:S(2)}) collective-permute-start(bf16[256,128]{1,0:T(8,128)(2,1)} %get-tuple-element.38), channel_id=1, source_target_pairs={{0,8},{8,0},{16,24},{24,16},{1,9},{9,1},{17,25},{25,17},{2,10},{10... | collective-permute-start | bytes 196616 | tf_op jit(solution)/shard_map/ppermute | solution.py:494
  32.8 13.0 %collective-permute-start.16 = (bf16[256,128]{1,0:T(8,128)(2,1)}, bf16[256,128]{1,0:T(8,128)(2,1)S(1)}, u32[]{:S(2)}, u32[]{:S(2)}) collective-permute-start(bf16[256,128]{1,0:T(8,128)(2,1)} %get-tuple-element.39), channel_id=1, source_target_pairs={{0,16},{8,24},{16,0},{24,8},{1,17},{9,25},{17,1},{25,9},{2,18},{10... | collective-permute-start | bytes 196616 | tf_op jit(solution)/shard_map/ppermute | solution.py:494
  35.4 10.4 %collective-permute-start.17 = (bf16[256,128]{1,0:T(8,128)(2,1)}, bf16[256,128]{1,0:T(8,128)(2,1)}, u32[]{:S(2)}, u32[]{:S(2)}) collective-permute-start(bf16[256,128]{1,0:T(8,128)(2,1)} %get-tuple-element.40), channel_id=1, source_target_pairs={{0,24},{8,16},{16,8},{24,0},{1,25},{9,17},{17,9},{25,1},{2,26},{10... | collective-permute-start | bytes 196616 | tf_op jit(solution)/shard_map/ppermute | solution.py:494
  35.5 16.6 %collective-permute-start.10 = (bf16[256,128]{1,0:T(8,128)(2,1)}, bf16[256,128]{1,0:T(8,128)(2,1)S(1)}, u32[]{:S(2)}, u32[]{:S(2)}) collective-permute-start(bf16[256,128]{1,0:T(8,128)(2,1)} %get-tuple-element.31), channel_id=1, source_target_pairs={{0,16},{8,24},{16,0},{24,8},{1,17},{9,25},{17,1},{25,9},{2,18},{10... | collective-permute-start | bytes 196616 | tf_op jit(solution)/shard_map/ppermute | solution.py:494
  37.3 17.3 %collective-permute-start.11 = (bf16[256,128]{1,0:T(8,128)(2,1)}, bf16[256,128]{1,0:T(8,128)(2,1)S(1)}, u32[]{:S(2)}, u32[]{:S(2)}) collective-permute-start(bf16[256,128]{1,0:T(8,128)(2,1)} %get-tuple-element.32), channel_id=1, source_target_pairs={{0,24},{8,16},{16,8},{24,0},{1,25},{9,17},{17,9},{25,1},{2,26},{10... | collective-permute-start | bytes 196616 | tf_op jit(solution)/shard_map/ppermute | solution.py:494
  44.4 1.1 %copy-start.10 = (bf16[256,128]{1,0:T(8,128)(2,1)S(1)}, bf16[256,128]{1,0:T(8,128)(2,1)}, u32[]{:S(2)}) copy-start(bf16[256,128]{1,0:T(8,128)(2,1)} %copy-done.9) | copy-start | bytes 196612
  44.4 1.5 %copy-start.1 = (bf16[7,512,256]{2,1,0:T(8,128)(2,1)S(1)}, bf16[7,512,256]{2,1,0:T(8,128)(2,1)}, u32[]{:S(2)}) copy-start(bf16[7,512,256]{2,1,0:T(8,128)(2,1)} %constant.19.clone.b_ref) | copy-start | bytes 5505028
  44.4 1.5 %copy-start.5 = (bf16[2,256,256]{2,1,0:T(8,128)(2,1)S(1)}, bf16[2,256,256]{2,1,0:T(8,128)(2,1)}, u32[]{:S(2)}) copy-start(bf16[2,256,256]{2,1,0:T(8,128)(2,1)} %constant.18.clone.br_ref) | copy-start | bytes 786436
  45.6 9.1 %collective-permute-start.9 = (bf16[256,128]{1,0:T(8,128)(2,1)S(1)}, bf16[256,128]{1,0:T(8,128)(2,1)S(1)}, u32[]{:S(2)}, u32[]{:S(2)}) collective-permute-start(bf16[256,128]{1,0:T(8,128)(2,1)S(1)} %copy-done.10), channel_id=1, source_target_pairs={{0,8},{8,0},{16,24},{24,16},{1,9},{9,1},{17,25},{25,17},{2,10},{10... | collective-permute-start | bytes 196616 | tf_op jit(solution)/shard_map/ppermute | solution.py:494
  49.0 10.4 %collective-permute-start.18 = (bf16[512,128]{1,0:T(8,128)(2,1)S(1)}, bf16[512,128]{1,0:T(8,128)(2,1)S(1)}, u32[]{:S(2)}, u32[]{:S(2)}) collective-permute-start(bf16[512,128]{1,0:T(8,128)(2,1)S(1)} %get-tuple-element.42), channel_id=1, source_target_pairs={{0,8},{8,0},{16,24},{24,16},{1,9},{9,1},{17,25},{25,17},{2,10},{10... | collective-permute-start | bytes 393224 | tf_op jit(solution)/shard_map/ppermute | solution.py:494
  51.0 12.4 %collective-permute-start.19 = (bf16[512,128]{1,0:T(8,128)(2,1)S(1)}, bf16[512,128]{1,0:T(8,128)(2,1)S(1)}, u32[]{:S(2)}, u32[]{:S(2)}) collective-permute-start(bf16[512,128]{1,0:T(8,128)(2,1)S(1)} %get-tuple-element.43), channel_id=1, source_target_pairs={{0,16},{8,24},{16,0},{24,8},{1,17},{9,25},{17,1},{25,9},{2,18},{10... | collective-permute-start | bytes 393224 | tf_op jit(solution)/shard_map/ppermute | solution.py:494
  52.1 11.3 %collective-permute-start.20 = (bf16[512,128]{1,0:T(8,128)(2,1)S(1)}, bf16[512,128]{1,0:T(8,128)(2,1)S(1)}, u32[]{:S(2)}, u32[]{:S(2)}) collective-permute-start(bf16[512,128]{1,0:T(8,128)(2,1)S(1)} %get-tuple-element.44), channel_id=1, source_target_pairs={{0,24},{8,16},{16,8},{24,0},{1,25},{9,17},{17,9},{25,1},{2,26},{10... | collective-permute-start | bytes 393224 | tf_op jit(solution)/shard_map/ppermute | solution.py:494
  54.6 18.4 %copy-start.3 = (bf16[512,512]{1,0:T(8,128)(2,1)S(1)}, bf16[512,512]{1,0:T(8,128)(2,1)}, u32[]{:S(2)}) copy-start(bf16[512,512]{1,0:T(8,128)(2,1)} %refs_8_.1) | copy-start | bytes 1572868
  54.6 18.4 %copy-start.4 = (bf16[512,512]{1,0:T(8,128)(2,1)S(1)}, bf16[512,512]{1,0:T(8,128)(2,1)}, u32[]{:S(2)}) copy-start(bf16[512,512]{1,0:T(8,128)(2,1)} %refs_9_.1) | copy-start | bytes 1572868
  57.4 6.0 %collective-permute-start.12 = (bf16[512,128]{1,0:T(8,128)(2,1)S(1)}, bf16[512,128]{1,0:T(8,128)(2,1)S(1)}, u32[]{:S(2)}, u32[]{:S(2)}) collective-permute-start(bf16[512,128]{1,0:T(8,128)(2,1)S(1)} %get-tuple-element.34), channel_id=1, source_target_pairs={{0,8},{8,0},{16,24},{24,16},{1,9},{9,1},{17,25},{25,17},{2,10},{10... | collective-permute-start | bytes 393224 | tf_op jit(solution)/shard_map/ppermute | solution.py:494
  58.5 14.5 %collective-permute-start.13 = (bf16[512,128]{1,0:T(8,128)(2,1)S(1)}, bf16[512,128]{1,0:T(8,128)(2,1)S(1)}, u32[]{:S(2)}, u32[]{:S(2)}) collective-permute-start(bf16[512,128]{1,0:T(8,128)(2,1)S(1)} %get-tuple-element.35), channel_id=1, source_target_pairs={{0,16},{8,24},{16,0},{24,8},{1,17},{9,25},{17,1},{25,9},{2,18},{10... | collective-permute-start | bytes 393224 | tf_op jit(solution)/shard_map/ppermute | solution.py:494
  59.4 13.6 %collective-permute-start.14 = (bf16[512,128]{1,0:T(8,128)(2,1)S(1)}, bf16[512,128]{1,0:T(8,128)(2,1)S(1)}, u32[]{:S(2)}, u32[]{:S(2)}) collective-permute-start(bf16[512,128]{1,0:T(8,128)(2,1)S(1)} %get-tuple-element.36), channel_id=1, source_target_pairs={{0,24},{8,16},{16,8},{24,0},{1,25},{9,17},{17,9},{25,1},{2,26},{10... | collective-permute-start | bytes 393224 | tf_op jit(solution)/shard_map/ppermute | solution.py:494
  (1 other events, 0.6 us)

commit v3 on v2

--- a/solution.py
+++ b/solution.py
@@ -239,17 +239,24 @@
         o[...] = res_ref[pl.ds(pl.multiple_of((z ^ s) * length, length), length), :]
 
 
-def finish_kernel(factor, ids_ref, *refs):
-    lows, highs = refs[:4], refs[4:8]
-    key_ref, value_ref, gk_ref, gv_ref, gt_ref = refs[8:]
-    z = ids_ref[0]
-    for s in range(4):
-        low, high = lows[s][...].astype(F32), highs[s][...].astype(F32)
-        cols = pl.ds(pl.multiple_of((z ^ s) * LANES, LANES), LANES)
-        gt_ref[:, cols] = join_high(low, high) * factor
+def finish_kernel(factor, distances, ids_ref, *refs):
+    n = len(distances)
+    lows, highs = refs[:n], refs[n : 2 * n]
+    key_ref, value_ref = refs[2 * n : 2 * n + 2]
+    gk_hbm, gv_hbm, gt_hbm, gk_ref, gv_ref, gt_ref, sems = refs[-7:]
+    writes = []
+    for i, distance in enumerate(distances):
+        low, high = lows[i][...].astype(F32), highs[i][...].astype(F32)
+        cols = pl.ds(pl.multiple_of((ids_ref[0] ^ distance) * LANES, LANES), LANES)
+        gt_ref[i] = join_high(low, high) * factor
         grad = join_low(low, high)
-        gk_ref[:, cols] = (value_ref[:, cols].astype(F32) * grad).astype(BF16)
-        gv_ref[:, cols] = (key_ref[:, cols].astype(F32) * grad).astype(BF16)
+        gk_ref[i] = (value_ref[:, cols].astype(F32) * grad).astype(BF16)
+        gv_ref[i] = (key_ref[:, cols].astype(F32) * grad).astype(BF16)
+        for k, (held, out) in enumerate(((gt_ref, gt_hbm), (gk_ref, gk_hbm), (gv_ref, gv_hbm))):
+            writes.append(pltpu.make_async_copy(held.at[i], out.at[:, cols], sems.at[k, i]))
+            writes[-1].start()
+    for write in writes:
+        write.wait()
 
 
 def project_near_kernel(ids_ref, weight_ref, *refs):
@@ -268,19 +275,25 @@
         turned[i * depth : (i + 1) * depth] = weight(len(blocks) + i).T
 
 
-def project_far_kernel(ids_ref, turned_ref, top0, top1, low0, low1, before, gate, *refs):
-    outs, (block, sums) = refs[:-2], refs[-2:]
+def project_far_kernel(ids_ref, turned_ref, top0, top1, low0, low1, before, gate, o0, o1, o2, o3, sums, block):
     half, depth = top0.shape
     for i, (top, low) in enumerate(((top0, low0), (top1, low1))):
         block[:half, i * depth : (i + 1) * depth] = top[...]
         block[half:, i * depth : (i + 1) * depth] = low[...]
     sums[...] = before[...] + dot(block[...], turned_ref[...])
-    z = ids_ref[0]
-    for s in range(4):
-        cols = pl.ds(pl.multiple_of((z ^ s) * LANES, LANES), LANES)
+    gate_half(join_low, ids_ref, sums, gate, (o0, o1, o2, o3))
+
+
+def gate_half(join, ids_ref, sums, gate, outs):
+    half = sums.shape[0] // 2
+    for s, o in enumerate(outs):
+        cols = pl.ds(pl.multiple_of((ids_ref[0] ^ s) * LANES, LANES), LANES)
         grad = gate[:, cols].astype(F32) * sums[:, cols]
-        outs[s][...] = join_low(grad[:half], grad[half:]).astype(BF16)
-        outs[4 + s][...] = join_high(grad[:half], grad[half:]).astype(BF16)
+        o[...] = join(grad[:half], grad[half:]).astype(BF16)
+
+
+def gate_high_kernel(ids_ref, sums, gate, o0, o1, o2, o3):
+    gate_half(join_high, ids_ref, sums, gate, (o0, o1, o2, o3))
 
 
 VMEM = pl.BlockSpec(memory_space=pltpu.VMEM)
@@ -311,15 +324,29 @@
 
 def project_far(ids, turned, blocks, before, gate):
     rows, channels = gate.shape
+    halves = [jax.ShapeDtypeStruct((rows // 2, LANES), BF16)] * (channels // LANES)
     return pl.pallas_call(
         project_far_kernel,
         in_specs=[SMEM] + [VMEM] * 7,
-        out_specs=[VMEM] * 8,
-        out_shape=[jax.ShapeDtypeStruct((rows // 2, LANES), BF16)] * 8,
-        scratch_shapes=[pltpu.VMEM((rows, turned.shape[0]), BF16), pltpu.VMEM((rows, channels), F32)],
+        out_specs=[VMEM] * (len(halves) + 1),
+        out_shape=halves + [jax.ShapeDtypeStruct((rows, channels), F32)],
+        scratch_shapes=[pltpu.VMEM((rows, turned.shape[0]), BF16)],
         compiler_params=limits(24),
         cost_estimate=cost(2 * rows * turned.size, 0),
     )(ids, turned, *blocks, before, gate)
+
+
+def gate_high(ids, sums, gate):
+    rows, channels = gate.shape
+    halves = [jax.ShapeDtypeStruct((rows // 2, LANES), BF16)] * (channels // LANES)
+    return pl.pallas_call(
+        gate_high_kernel,
+        in_specs=[SMEM] + [VMEM] * 2,
+        out_specs=[VMEM] * len(halves),
+        out_shape=halves,
+        compiler_params=limits(24),
+        cost_estimate=cost(sums.size, 0),
+    )(ids, sums, gate)
 
 
 def pack(taps, key, value, parts):
@@ -370,16 +397,20 @@
     )(ids, *grads, spec, *tables)
 
 
-def finish(ids, lows, highs, key, value, factor):
-    shape = key.shape
-    return pl.pallas_call(
-        functools.partial(finish_kernel, factor),
-        out_shape=[jax.ShapeDtypeStruct(shape, BF16), jax.ShapeDtypeStruct(shape, BF16), jax.ShapeDtypeStruct(shape, F32)],
-        in_specs=[SMEM] + [VMEM] * 10,
-        out_specs=[VMEM] * 3,
+def finish(ids, lows, highs, distances, key, value, factor, before=()):
+    length, n = key.shape[0], len(distances)
+    ins = [*lows, *highs, key, value, *before]
+    held = lambda dtype: pltpu.VMEM((n, length, LANES), dtype)
+    return pl.pallas_call(
+        functools.partial(finish_kernel, factor, distances),
+        out_shape=[jax.ShapeDtypeStruct(key.shape, BF16), jax.ShapeDtypeStruct(key.shape, BF16), jax.ShapeDtypeStruct(key.shape, F32)],
+        in_specs=[SMEM] + [VMEM] * (2 * n + 2) + [ANY] * len(before),
+        out_specs=[ANY] * 3,
+        scratch_shapes=[held(BF16), held(BF16), held(F32), pltpu.SemaphoreType.DMA((3, n))],
+        input_output_aliases={2 * n + 3 + i: i for i in range(len(before))},
         compiler_params=limits(24),
-        cost_estimate=cost(4 * key.size, 16 * key.size),
-    )(ids, *lows, *highs, key, value)
+        cost_estimate=cost(0, 16 * n * length * LANES),
+    )(ids, *ins)
 
 
 PRECISION = lax.Precision.HIGH
@@ -509,12 +540,17 @@
     total, turned = project_near(ids, output_weight, [output_grad, from_core, from_x, core_x, from_y, core_y], HINT)
     far_top, far_low, total = lax.optimization_barrier((far_top, far_low, total))
     core_top, core_low = hop(far_top, "ch", 1), hop(far_low, "ch", 1)
-    grads = project_far(ids, turned, [far_top, core_top, far_low, core_low], total, query_gate)
+    *low_grads, sums = project_far(ids, turned, [far_top, core_top, far_low, core_low], total, query_gate)
     spread = lambda blocks: [blocks[0]] + [hop(blocks[s], "ctx", s) for s in range(1, parts)]
-    low_grads, high_grads = spread(grads[:parts]), spread(grads[parts:])
+    low_grads, high = spread(low_grads), list(gate_high(ids, sums, query_gate))
+    low_spec, high[2], high[3] = lax.optimization_barrier((low_spec, high[2], high[3]))
+    high_grads = spread(high)
     low = spread(correlate(ids, low_grads, low_spec, tables))
     high = spread(correlate(ids, high_grads, high_spec, tables))
-    return tuple(finish(ids, low, high, key_proj, value_proj, 1.0 / math.sqrt(parts * length)))
+    factor = 1.0 / math.sqrt(parts * length)
+    low[2], low[3], high[1] = lax.optimization_barrier((low[2], low[3], high[1]))
+    near = finish(ids, low[:2], high[:2], (0, 1), key_proj, value_proj, factor)
+    return tuple(finish(ids, low[2:], high[2:], (2, 3), key_proj, value_proj, factor, near))
 
 
 def per_device(*arrays):

time: 75.8 us -> 71.4 us (0.942)
  waiting for transfers between devices: 23.9 us -> 17.3 us
  Pallas kernels: 18.1 us -> 19.9 us
    ppermute x21, waiting for transfers between devices: 18.7 us -> 14.8 us  [hop(): return lax.ppermute(x, axis, [(j, j ^ distance) for j in range(n)])]
    all_to_all x1, waiting for transfers between devices: 5.21 us -> 2.55 us  [exchanged_layer(): lax.all_to_all(sent, 'ctx', 0, 0, tiled=True)]
    pallas_call x1 -> x3, Pallas kernels: 2.47 us -> 4.66 us  [the longest x2 3.33 us: finish(): pl.pallas_call(functools.partial(finish_kernel, factor, distances), out_s...]
    unnamed x22 -> x26, local copies, waits for them, and re-layouts: 2.98 us -> 3.47 us
  transfers between devices with their start and end apart: 22 -> 22, of which waited for: 10 -> 10; matrix products, arithmetic and copies ran while one was open for 0% -> 0% of each run, Pallas kernels for 21% -> 26%
where the time goes in v3:
time: 71.4 us; the launch traced here: 71 us
  starting transfers between devices  29.4 us (41%)
  Pallas kernels  19.9 us (28%)
  waiting for transfers between devices  17.3 us (24%)
  local copies, waits for them, and re-layouts  3.51 us (5%)
  between operations  0.85 us (1%)
    ppermute x21, starting transfers between devices, hop(): return lax.ppermute(x, axis, [(j, j ^ distance) for j in range(n)])  24.5 us
    ppermute x21, waiting for transfers between devices, hop(): return lax.ppermute(x, axis, [(j, j ^ distance) for j in range(n)])  14.8 us
    pallas_call x2, Pallas kernels, correlate(): pl.pallas_call(correlate_kernel, out_shape=[jax.ShapeDtypeStruct((length,...  5.38 us
    all_to_all x1, starting transfers between devices, exchanged_layer(): lax.all_to_all(sent, 'ctx', 0, 0, tiled=True)  4.88 us
    unnamed x26, local copies, waits for them, and re-layouts  3.47 us
    pallas_call x2, Pallas kernels, finish(): pl.pallas_call(functools.partial(finish_kernel, factor, distances), out_s...  3.33 us
    pallas_call x1, Pallas kernels, project_near(): pl.pallas_call(project_near_kernel, in_specs=[SMEM] + [VMEM] * (1 + len(b...  3.04 us
    all_to_all x1, waiting for transfers between devices, exchanged_layer(): lax.all_to_all(sent, 'ctx', 0, 0, tiled=True)  2.55 us
  transfers between devices with their start and end apart: 22, of which 10 were waited for; matrix products, arithmetic and copies ran while one was open for 0% of the time, Pallas kernels for 26%

profile of v3, /device:TPU:0, one launch (start us, length us, event | category | flops | bytes accessed | tf_op | source)
XLA Modules:
  0.0 71.0 jit_solution(12407328054709609075)
XLA Ops:
  0.6 3.0 %collective-permute-start.1 = (bf16[512,512]{1,0:T(8,128)(2,1)}, bf16[512,512]{1,0:T(8,128)(2,1)S(1)}, u32[]{:S(2)}, u32[]{:S(2)}) collective-permute-start(bf16[512,512]{1,0:T(8,128)(2,1)} %refs_0_.1), channel_id=1, source_target_pairs={{0,2},{1,3},{2,0},{3,1},{4,6},{5,7},{6,4},{7,5},{8,10},{9,11},{10,... | collective-permute-start | bytes 1572872 | tf_op jit(solution)/shard_map/ppermute | solution.py:525
  3.6 1.5 %collective-permute-start.3 = (bf16[512,512]{1,0:T(8,128)(2,1)}, bf16[512,512]{1,0:T(8,128)(2,1)S(1)}, u32[]{:S(2)}, u32[]{:S(2)}) collective-permute-start(bf16[512,512]{1,0:T(8,128)(2,1)} %refs_0_.1), channel_id=1, source_target_pairs={{0,4},{1,5},{2,6},{3,7},{4,0},{5,1},{6,2},{7,3},{8,12},{9,13},{10,... | collective-permute-start | bytes 1572872 | tf_op jit(solution)/shard_map/ppermute | solution.py:525
  5.2 2.5 %shard_map.123 = bf16[4,512,256]{2,1,0:T(8,128)(2,1)} custom-call(bf16[512,512]{1,0:T(8,128)(2,1)} %taps_hbm.1, bf16[512,512]{1,0:T(8,128)(2,1)} %refs_4_.3, bf16[512,512]{1,0:T(8,128)(2,1)} %refs_5_.3), custom_call_target="tpu_custom_call" | custom-call | bytes 2621440 | tf_op jit(solution)/shard_map/pallas_call | solution.py:355
  7.7 4.9 %all-to-all-start = ((bf16[4,512,256]{2,1,0:T(8,128)(2,1)}), bf16[4,512,256]{2,1,0:T(8,128)(2,1)S(1)}, u32[]{:S(2)}, u32[]{:S(2)}) async-start(bf16[4,512,256]{2,1,0:T(8,128)(2,1)} %shard_map.123), calls=%async_computation | async-start | bytes 2097152 | tf_op jit(solution)/shard_map/all_to_all | solution.py:536
  12.6 3.2 %collective-permute-done.1.refs_2_ = bf16[512,512]{1,0:T(8,128)(2,1)S(1)} collective-permute-done((bf16[512,512]{1,0:T(8,128)(2,1)}, bf16[512,512]{1,0:T(8,128)(2,1)S(1)}, u32[]{:S(2)}, u32[]{:S(2)}) %collective-permute-start.1) | collective-permute-done | bytes 524320 | tf_op jit(solution)/shard_map/ppermute | solution.py:525
  15.8 1.5 %collective-permute-done.3.refs_4_ = bf16[512,512]{1,0:T(8,128)(2,1)S(1)} collective-permute-done((bf16[512,512]{1,0:T(8,128)(2,1)}, bf16[512,512]{1,0:T(8,128)(2,1)S(1)}, u32[]{:S(2)}, u32[]{:S(2)}) %collective-permute-start.3) | collective-permute-done | bytes 524320 | tf_op jit(solution)/shard_map/ppermute | solution.py:525
  18.2 1.6 %collective-permute-start.6 = (bf16[256,512]{1,0:T(8,128)(2,1)S(1)}, bf16[256,512]{1,0:T(8,128)(2,1)S(1)}, u32[]{:S(2)}, u32[]{:S(2)}) collective-permute-start(bf16[256,512]{1,0:T(8,128)(2,1)S(1)} %slice.9), channel_id=1, source_target_pairs={{0,4},{1,5},{2,6},{3,7},{4,0},{5,1},{6,2},{7,3},{8,12},{9,13},{10,... | collective-permute-start | bytes 786440 | tf_op jit(solution)/shard_map/ppermute | solution.py:525
  19.8 2.2 %copy-done.7 = bf16[512,4096]{1,0:T(8,128)(2,1)S(1)} copy-done((bf16[512,4096]{1,0:T(8,128)(2,1)S(1)}, bf16[512,4096]{1,0:T(8,128)(2,1)}, u32[]{:S(2)}) %copy-start.7) | copy-done | bytes 4194328
  22.0 3.0 %shard_map.121 = (f32[512,512]{1,0:T(8,128)S(1)}, bf16[1024,512]{1,0:T(8,128)(2,1)S(1)}) custom-call(s32[2]{0:T(128)S(1)} %pad_add_fusion.ids_ref, bf16[512,4096]{1,0:T(8,128)(2,1)S(1)} %copy-done.7, bf16[512,512]{1,0:T(8,128)(2,1)S(1)} %copy-done.8, bf16[512,512]{1,0:T(8,128)(2,1)S(1)} %collective-permute-done.refs_1_, ...), custom_call_target="tpu_custom_call" | custom-call | flops 5000000000 | tf_op jit(solution)/shard_map/pallas_call | solution.py:315
  25.1 1.1 %collective-permute-done.5.top0 = bf16[256,512]{1,0:T(8,128)(2,1)S(1)} collective-permute-done((bf16[256,512]{1,0:T(8,128)(2,1)S(1)}, bf16[256,512]{1,0:T(8,128)(2,1)S(1)}, u32[]{:S(2)}, u32[]{:S(2)}) %collective-permute-start.5) | collective-permute-done | bytes 262176 | tf_op jit(solution)/shard_map/ppermute | solution.py:525
  26.8 1.0 %collective-permute-done.7.top1 = bf16[256,512]{1,0:T(8,128)(2,1)S(1)} collective-permute-done((bf16[256,512]{1,0:T(8,128)(2,1)S(1)}, bf16[256,512]{1,0:T(8,128)(2,1)S(1)}, u32[]{:S(2)}, u32[]{:S(2)}) %collective-permute-start.7) | collective-permute-done | bytes 262176 | tf_op jit(solution)/shard_map/ppermute | solution.py:525
  28.2 2.1 %shard_map.122 = (bf16[256,128]{1,0:T(8,128)(2,1)S(1)}, bf16[256,128]{1,0:T(8,128)(2,1)}, bf16[256,128]{1,0:T(8,128)(2,1)}, bf16[256,128]{1,0:T(8,128)(2,1)}, f32[512,512]{1,0:T(8,128)S(1)}) custom-call(s32[2]{0:T(128)S(1)} %pad_add_fusion.ids_ref, bf16[1024,512]{1,0:T(8,128)(2,1)S(1)} %get-tuple-element.34.turned_ref, ...), custom_call_target="tpu_custom_call" | custom-call | flops 536870912 | tf_op jit(solution)/shard_map/pallas_call | solution.py:328
  30.4 2.7 %collective-permute-start.10 = (bf16[256,128]{1,0:T(8,128)(2,1)}, bf16[256,128]{1,0:T(8,128)(2,1)S(1)}, u32[]{:S(2)}, u32[]{:S(2)}) collective-permute-start(bf16[256,128]{1,0:T(8,128)(2,1)} %get-tuple-element.41), channel_id=1, source_target_pairs={{0,16},{8,24},{16,0},{24,8},{1,17},{9,25},{17,1},{25,9},{2,18},{10... | collective-permute-start | bytes 196616 | tf_op jit(solution)/shard_map/ppermute | solution.py:525
  33.1 1.3 %collective-permute-start.11 = (bf16[256,128]{1,0:T(8,128)(2,1)}, bf16[256,128]{1,0:T(8,128)(2,1)S(1)}, u32[]{:S(2)}, u32[]{:S(2)}) collective-permute-start(bf16[256,128]{1,0:T(8,128)(2,1)} %get-tuple-element.42), channel_id=1, source_target_pairs={{0,24},{8,16},{16,8},{24,0},{1,25},{9,17},{17,9},{25,1},{2,26},{10... | collective-permute-start | bytes 196616 | tf_op jit(solution)/shard_map/ppermute | solution.py:525
  34.7 1.3 %shard_map.125 = (bf16[256,128]{1,0:T(8,128)(2,1)S(1)}, bf16[256,128]{1,0:T(8,128)(2,1)}, bf16[256,128]{1,0:T(8,128)(2,1)S(1)}, bf16[256,128]{1,0:T(8,128)(2,1)S(1)}) custom-call(s32[2]{0:T(128)S(1)} %pad_add_fusion.ids_ref, f32[512,512]{1,0:T(8,128)S(1)} %get-tuple-element.43.sums, bf16[512,512]{1,0:T(8,128)(2,1)S(1)} %copy-done.5), custom_call_target="tpu_custom_call" | custom-call | flops 262144 | tf_op jit(solution)/shard_map/pallas_call | solution.py:342
  37.3 1.8 %collective-permute-start.14 = (bf16[256,128]{1,0:T(8,128)(2,1)}, bf16[256,128]{1,0:T(8,128)(2,1)S(1)}, u32[]{:S(2)}, u32[]{:S(2)}) collective-permute-start(bf16[256,128]{1,0:T(8,128)(2,1)} %get-tuple-element.50), channel_id=1, source_target_pairs={{0,8},{8,0},{16,24},{24,16},{1,9},{9,1},{17,25},{25,17},{2,10},{10... | collective-permute-start | bytes 196616 | tf_op jit(solution)/shard_map/ppermute | solution.py:525
  39.1 2.6 %all-to-all-done = bf16[4,512,256]{2,1,0:T(8,128)(2,1)S(1)} async-done(((bf16[4,512,256]{2,1,0:T(8,128)(2,1)}), bf16[4,512,256]{2,1,0:T(8,128)(2,1)S(1)}, u32[]{:S(2)}, u32[]{:S(2)}) %all-to-all-start) | async-done | bytes 1048608 | tf_op jit(solution)/shard_map/all_to_all | solution.py:536
  41.7 1.1 %shard_map.124.spec_ref = bf16[8,512,128]{2,1,0:T(8,128)(2,1)S(1)} custom-call(bf16[2048,256]{1,0:T(8,128)(2,1)S(1)} %bitcast.3, bf16[2,256,256]{2,1,0:T(8,128)(2,1)S(1)} %copy-done.4, bf16[7,512,256]{2,1,0:T(8,128)(2,1)S(1)} %copy-done), custom_call_target="tpu_custom_call" | custom-call | flops 536870912 | tf_op jit(solution)/shard_map/pallas_call | solution.py:369
  42.8 1.6 %collective-permute-start.16 = (bf16[256,128]{1,0:T(8,128)(2,1)S(1)}, bf16[256,128]{1,0:T(8,128)(2,1)S(1)}, u32[]{:S(2)}, u32[]{:S(2)}) collective-permute-start(bf16[256,128]{1,0:T(8,128)(2,1)S(1)} %copy-done.10), channel_id=1, source_target_pairs={{0,24},{8,16},{16,8},{24,0},{1,25},{9,17},{17,9},{25,1},{2,26},{10... | collective-permute-start | bytes 196616 | tf_op jit(solution)/shard_map/ppermute | solution.py:525
  44.5 2.7 %shard_map.126 = (bf16[512,128]{1,0:T(8,128)(2,1)S(1)}, bf16[512,128]{1,0:T(8,128)(2,1)S(1)}, bf16[512,128]{1,0:T(8,128)(2,1)S(1)}, bf16[512,128]{1,0:T(8,128)(2,1)S(1)}) custom-call(s32[2]{0:T(128)S(1)} %pad_add_fusion.ids_ref, bf16[256,128]{1,0:T(8,128)(2,1)S(1)} %get-tuple-element.39.g0, bf16[256,128]{1,0:T(8,128)(2,1)S(1)} %collective-permute-done.9.g1, ...), custom_call_target="tpu_custom_call" | custom-call | flops 1073741824 | tf_op jit(solution)/shard_map/pallas_call | solution.py:383
  47.2 2.0 %collective-permute-start.12 = (bf16[512,128]{1,0:T(8,128)(2,1)S(1)}, bf16[512,128]{1,0:T(8,128)(2,1)S(1)}, u32[]{:S(2)}, u32[]{:S(2)}) collective-permute-start(bf16[512,128]{1,0:T(8,128)(2,1)S(1)} %get-tuple-element.47), channel_id=1, source_target_pairs={{0,16},{8,24},{16,0},{24,8},{1,17},{9,25},{17,1},{25,9},{2,18},{10... | collective-permute-start | bytes 393224 | tf_op jit(solution)/shard_map/ppermute | solution.py:525
  49.2 2.3 %collective-permute-start.13 = (bf16[512,128]{1,0:T(8,128)(2,1)S(1)}, bf16[512,128]{1,0:T(8,128)(2,1)S(1)}, u32[]{:S(2)}, u32[]{:S(2)}) collective-permute-start(bf16[512,128]{1,0:T(8,128)(2,1)S(1)} %get-tuple-element.48), channel_id=1, source_target_pairs={{0,24},{8,16},{16,8},{24,0},{1,25},{9,17},{17,9},{25,1},{2,26},{10... | collective-permute-start | bytes 393224 | tf_op jit(solution)/shard_map/ppermute | solution.py:525
  51.5 1.1 %shard_map.127.spec_ref = bf16[8,512,128]{2,1,0:T(8,128)(2,1)S(1)} custom-call(bf16[2048,256]{1,0:T(8,128)(2,1)S(1)} %bitcast.4, bf16[2,256,256]{2,1,0:T(8,128)(2,1)S(1)} %copy-done.4, bf16[7,512,256]{2,1,0:T(8,128)(2,1)S(1)} %copy-done), custom_call_target="tpu_custom_call" | custom-call | flops 536870912 | tf_op jit(solution)/shard_map/pallas_call | solution.py:369
  52.6 2.7 %shard_map.128 = (bf16[512,128]{1,0:T(8,128)(2,1)S(1)}, bf16[512,128]{1,0:T(8,128)(2,1)S(1)}, bf16[512,128]{1,0:T(8,128)(2,1)S(1)}, bf16[512,128]{1,0:T(8,128)(2,1)S(1)}) custom-call(s32[2]{0:T(128)S(1)} %pad_add_fusion.ids_ref, bf16[256,128]{1,0:T(8,128)(2,1)S(1)} %get-tuple-element.49.g0, bf16[256,128]{1,0:T(8,128)(2,1)S(1)} %collective-permute-done.14.g1, ...), custom_call_target="tpu_custom_call" | custom-call | flops 1073741824 | tf_op jit(solution)/shard_map/pallas_call | solution.py:383
  55.8 1.6 %collective-permute-start.20 = (bf16[512,128]{1,0:T(8,128)(2,1)S(1)}, bf16[512,128]{1,0:T(8,128)(2,1)S(1)}, u32[]{:S(2)}, u32[]{:S(2)}) collective-permute-start(bf16[512,128]{1,0:T(8,128)(2,1)S(1)} %get-tuple-element.59), channel_id=1, source_target_pairs={{0,8},{8,0},{16,24},{24,16},{1,9},{9,1},{17,25},{25,17},{2,10},{10... | collective-permute-start | bytes 393224 | tf_op jit(solution)/shard_map/ppermute | solution.py:525
  57.4 1.1 %collective-permute-start.18 = (bf16[512,128]{1,0:T(8,128)(2,1)S(1)}, bf16[512,128]{1,0:T(8,128)(2,1)S(1)}, u32[]{:S(2)}, u32[]{:S(2)}) collective-permute-start(bf16[512,128]{1,0:T(8,128)(2,1)S(1)} %get-tuple-element.56), channel_id=1, source_target_pairs={{0,16},{8,24},{16,0},{24,8},{1,17},{9,25},{17,1},{25,9},{2,18},{10... | collective-permute-start | bytes 393224 | tf_op jit(solution)/shard_map/ppermute | solution.py:525
  58.5 1.8 %collective-permute-start.19 = (bf16[512,128]{1,0:T(8,128)(2,1)S(1)}, bf16[512,128]{1,0:T(8,128)(2,1)S(1)}, u32[]{:S(2)}, u32[]{:S(2)}) collective-permute-start(bf16[512,128]{1,0:T(8,128)(2,1)S(1)} %get-tuple-element.57), channel_id=1, source_target_pairs={{0,24},{8,16},{16,8},{24,0},{1,25},{9,17},{17,9},{25,1},{2,26},{10... | collective-permute-start | bytes 393224 | tf_op jit(solution)/shard_map/ppermute | solution.py:525
  60.2 1.5 %collective-permute-done.17.refs_3_ = bf16[512,128]{1,0:T(8,128)(2,1)S(1)} collective-permute-done((bf16[512,128]{1,0:T(8,128)(2,1)S(1)}, bf16[512,128]{1,0:T(8,128)(2,1)S(1)}, u32[]{:S(2)}, u32[]{:S(2)}) %collective-permute-start.17) | collective-permute-done | bytes 131104 | tf_op jit(solution)/shard_map/ppermute | solution.py:525
  61.7 3.8 %collective-permute-done.20.refs_1_ = bf16[512,128]{1,0:T(8,128)(2,1)S(1)} collective-permute-done((bf16[512,128]{1,0:T(8,128)(2,1)S(1)}, bf16[512,128]{1,0:T(8,128)(2,1)S(1)}, u32[]{:S(2)}, u32[]{:S(2)}) %collective-permute-start.20) | collective-permute-done | bytes 131104 | tf_op jit(solution)/shard_map/ppermute | solution.py:525
  65.5 1.7 %shard_map.129 = (bf16[512,512]{1,0:T(8,128)(2,1)}, bf16[512,512]{1,0:T(8,128)(2,1)}, f32[512,512]{1,0:T(8,128)}) custom-call(s32[2]{0:T(128)S(1)} %pad_add_fusion.ids_ref, bf16[512,128]{1,0:T(8,128)(2,1)S(1)} %get-tuple-element.58.refs_0_, bf16[512,128]{1,0:T(8,128)(2,1)S(1)} %collective-permute-done.20.refs_1_, ...), custom_call_target="tpu_custom_call" | custom-call | bytes 2097152 | tf_op jit(solution)/shard_map/pallas_call | solution.py:404
  67.2 2.1 %collective-permute-done.18.refs_2_ = bf16[512,128]{1,0:T(8,128)(2,1)S(1)} collective-permute-done((bf16[512,128]{1,0:T(8,128)(2,1)S(1)}, bf16[512,128]{1,0:T(8,128)(2,1)S(1)}, u32[]{:S(2)}, u32[]{:S(2)}) %collective-permute-start.18) | collective-permute-done | bytes 131104 | tf_op jit(solution)/shard_map/ppermute | solution.py:525
  69.3 1.7 %shard_map.130 = (bf16[512,512]{1,0:T(8,128)(2,1)}, bf16[512,512]{1,0:T(8,128)(2,1)}, f32[512,512]{1,0:T(8,128)}) custom-call(s32[2]{0:T(128)S(1)} %pad_add_fusion.ids_ref, bf16[512,128]{1,0:T(8,128)(2,1)S(1)} %collective-permute-done.12.refs_0_, ...), custom_call_target="tpu_custom_call", output_to_operand_aliasing={{0}: (7, {}), {1}: (8, {}), {2}: (9, {})} | custom-call | bytes 2097152 | tf_op jit(solution)/shard_map/pallas_call | solution.py:404
  (51 shorter events, 4.2 us)
Async XLA Ops:
  0.6 11.9 %copy-start.8 = (bf16[512,512]{1,0:T(8,128)(2,1)S(1)}, bf16[512,512]{1,0:T(8,128)(2,1)}, u32[]{:S(2)}) copy-start(bf16[512,512]{1,0:T(8,128)(2,1)} %refs_0_.1) | copy-start | bytes 1572868
  0.6 15.1 %collective-permute-start.1 = (bf16[512,512]{1,0:T(8,128)(2,1)}, bf16[512,512]{1,0:T(8,128)(2,1)S(1)}, u32[]{:S(2)}, u32[]{:S(2)}) collective-permute-start(bf16[512,512]{1,0:T(8,128)(2,1)} %refs_0_.1), channel_id=1, source_target_pairs={{0,2},{1,3},{2,0},{3,1},{4,6},{5,7},{6,4},{7,5},{8,10},{9,11},{10,... | collective-permute-start | bytes 1572872 | tf_op jit(solution)/shard_map/ppermute | solution.py:525
  3.6 13.6 %collective-permute-start.3 = (bf16[512,512]{1,0:T(8,128)(2,1)}, bf16[512,512]{1,0:T(8,128)(2,1)S(1)}, u32[]{:S(2)}, u32[]{:S(2)}) collective-permute-start(bf16[512,512]{1,0:T(8,128)(2,1)} %refs_0_.1), channel_id=1, source_target_pairs={{0,4},{1,5},{2,6},{3,7},{4,0},{5,1},{6,2},{7,3},{8,12},{9,13},{10,... | collective-permute-start | bytes 1572872 | tf_op jit(solution)/shard_map/ppermute | solution.py:525
  7.7 34.0 %all-to-all-start = ((bf16[4,512,256]{2,1,0:T(8,128)(2,1)}), bf16[4,512,256]{2,1,0:T(8,128)(2,1)S(1)}, u32[]{:S(2)}, u32[]{:S(2)}) async-start(bf16[4,512,256]{2,1,0:T(8,128)(2,1)} %shard_map.123), calls=%async_computation | async-start | bytes 2097152 | tf_op jit(solution)/shard_map/all_to_all | solution.py:536
  12.6 7.3 %collective-permute-start = (bf16[512,512]{1,0:T(8,128)(2,1)S(1)}, bf16[512,512]{1,0:T(8,128)(2,1)S(1)}, u32[]{:S(2)}, u32[]{:S(2)}) collective-permute-start(bf16[512,512]{1,0:T(8,128)(2,1)S(1)} %copy-done.8), channel_id=1, source_target_pairs={{0,1},{1,0},{2,3},{3,2},{4,5},{5,4},{6,7},{7,6},{8,9},{9,8},{10,11... | collective-permute-start | bytes 1572872 | tf_op jit(solution)/shard_map/ppermute | solution.py:525
  15.8 4.0 %collective-permute-start.2 = (bf16[512,512]{1,0:T(8,128)(2,1)S(1)}, bf16[512,512]{1,0:T(8,128)(2,1)}, u32[]{:S(2)}, u32[]{:S(2)}) collective-permute-start(bf16[512,512]{1,0:T(8,128)(2,1)S(1)} %collective-permute-done.1.refs_2_), channel_id=1, source_target_pairs={{0,1},{1,0},{2,3},{3,2},{4,5},{5,4},{6,7},{7,6},{8,9},{9,8},{10,11... | collective-permute-start | bytes 1572872 | tf_op jit(solution)/shard_map/ppermute | solution.py:525
  17.2 2.6 %collective-permute-start.4 = (bf16[512,512]{1,0:T(8,128)(2,1)S(1)}, bf16[512,512]{1,0:T(8,128)(2,1)}, u32[]{:S(2)}, u32[]{:S(2)}) collective-permute-start(bf16[512,512]{1,0:T(8,128)(2,1)S(1)} %collective-permute-done.3.refs_4_), channel_id=1, source_target_pairs={{0,1},{1,0},{2,3},{3,2},{4,5},{5,4},{6,7},{7,6},{8,9},{9,8},{10,11... | collective-permute-start | bytes 1572872 | tf_op jit(solution)/shard_map/ppermute | solution.py:525
  17.3 8.8 %collective-permute-start.5 = (bf16[256,512]{1,0:T(8,128)(2,1)S(1)}, bf16[256,512]{1,0:T(8,128)(2,1)S(1)}, u32[]{:S(2)}, u32[]{:S(2)}) collective-permute-start(bf16[256,512]{1,0:T(8,128)(2,1)S(1)} %slice.8), channel_id=1, source_target_pairs={{0,2},{1,3},{2,0},{3,1},{4,6},{5,7},{6,4},{7,5},{8,10},{9,11},{10,... | collective-permute-start | bytes 786440 | tf_op jit(solution)/shard_map/ppermute | solution.py:525
  18.2 10.0 %copy-start.5 = (bf16[512,512]{1,0:T(8,128)(2,1)S(1)}, bf16[512,512]{1,0:T(8,128)(2,1)}, u32[]{:S(2)}) copy-start(bf16[512,512]{1,0:T(8,128)(2,1)} %gate.3) | copy-start | bytes 1572868
  18.2 8.1 %collective-permute-start.6 = (bf16[256,512]{1,0:T(8,128)(2,1)S(1)}, bf16[256,512]{1,0:T(8,128)(2,1)S(1)}, u32[]{:S(2)}, u32[]{:S(2)}) collective-permute-start(bf16[256,512]{1,0:T(8,128)(2,1)S(1)} %slice.9), channel_id=1, source_target_pairs={{0,4},{1,5},{2,6},{3,7},{4,0},{5,1},{6,2},{7,3},{8,12},{9,13},{10,... | collective-permute-start | bytes 786440 | tf_op jit(solution)/shard_map/ppermute | solution.py:525
  19.8 2.2 %copy-start.7 = (bf16[512,4096]{1,0:T(8,128)(2,1)S(1)}, bf16[512,4096]{1,0:T(8,128)(2,1)}, u32[]{:S(2)}) copy-start(bf16[512,4096]{1,0:T(8,128)(2,1)} %weight_ref.1) | copy-start | bytes 12582916
  26.3 1.5 %collective-permute-start.7 = (bf16[256,512]{1,0:T(8,128)(2,1)S(1)}, bf16[256,512]{1,0:T(8,128)(2,1)S(1)}, u32[]{:S(2)}, u32[]{:S(2)}) collective-permute-start(bf16[256,512]{1,0:T(8,128)(2,1)S(1)} %collective-permute-done.5.top0), channel_id=1, source_target_pairs={{0,1},{1,0},{2,3},{3,2},{4,5},{5,4},{6,7},{7,6},{8,9},{9,8},{10,11... | collective-permute-start | bytes 786440 | tf_op jit(solution)/shard_map/ppermute | solution.py:525
  26.3 1.9 %collective-permute-start.8 = (bf16[256,512]{1,0:T(8,128)(2,1)S(1)}, bf16[256,512]{1,0:T(8,128)(2,1)S(1)}, u32[]{:S(2)}, u32[]{:S(2)}) collective-permute-start(bf16[256,512]{1,0:T(8,128)(2,1)S(1)} %collective-permute-done.6.low0), channel_id=1, source_target_pairs={{0,1},{1,0},{2,3},{3,2},{4,5},{5,4},{6,7},{7,6},{8,9},{9,8},{10,11... | collective-permute-start | bytes 786440 | tf_op jit(solution)/shard_map/ppermute | solution.py:525
  28.2 13.4 %copy-start = (bf16[7,512,256]{2,1,0:T(8,128)(2,1)S(1)}, bf16[7,512,256]{2,1,0:T(8,128)(2,1)}, u32[]{:S(2)}) copy-start(bf16[7,512,256]{2,1,0:T(8,128)(2,1)} %constant.17.clone.table_ref.f_ref) | copy-start | bytes 5505028
  28.2 13.4 %copy-start.4 = (bf16[2,256,256]{2,1,0:T(8,128)(2,1)S(1)}, bf16[2,256,256]{2,1,0:T(8,128)(2,1)}, u32[]{:S(2)}) copy-start(bf16[2,256,256]{2,1,0:T(8,128)(2,1)} %constant.16.clone.real_ref.fr_ref) | copy-start | bytes 786436
  30.4 12.4 %collective-permute-start.10 = (bf16[256,128]{1,0:T(8,128)(2,1)}, bf16[256,128]{1,0:T(8,128)(2,1)S(1)}, u32[]{:S(2)}, u32[]{:S(2)}) collective-permute-start(bf16[256,128]{1,0:T(8,128)(2,1)} %get-tuple-element.41), channel_id=1, source_target_pairs={{0,16},{8,24},{16,0},{24,8},{1,17},{9,25},{17,1},{25,9},{2,18},{10... | collective-permute-start | bytes 196616 | tf_op jit(solution)/shard_map/ppermute | solution.py:525
  33.1 11.3 %collective-permute-start.11 = (bf16[256,128]{1,0:T(8,128)(2,1)}, bf16[256,128]{1,0:T(8,128)(2,1)S(1)}, u32[]{:S(2)}, u32[]{:S(2)}) collective-permute-start(bf16[256,128]{1,0:T(8,128)(2,1)} %get-tuple-element.42), channel_id=1, source_target_pairs={{0,24},{8,16},{16,8},{24,0},{1,25},{9,17},{17,9},{25,1},{2,26},{10... | collective-permute-start | bytes 196616 | tf_op jit(solution)/shard_map/ppermute | solution.py:525
  34.5 10.0 %collective-permute-start.9 = (bf16[256,128]{1,0:T(8,128)(2,1)}, bf16[256,128]{1,0:T(8,128)(2,1)S(1)}, u32[]{:S(2)}, u32[]{:S(2)}) collective-permute-start(bf16[256,128]{1,0:T(8,128)(2,1)} %get-tuple-element.40), channel_id=1, source_target_pairs={{0,8},{8,0},{16,24},{24,16},{1,9},{9,1},{17,25},{25,17},{2,10},{10... | collective-permute-start | bytes 196616 | tf_op jit(solution)/shard_map/ppermute | solution.py:525
  37.3 15.3 %collective-permute-start.14 = (bf16[256,128]{1,0:T(8,128)(2,1)}, bf16[256,128]{1,0:T(8,128)(2,1)S(1)}, u32[]{:S(2)}, u32[]{:S(2)}) collective-permute-start(bf16[256,128]{1,0:T(8,128)(2,1)} %get-tuple-element.50), channel_id=1, source_target_pairs={{0,8},{8,0},{16,24},{24,16},{1,9},{9,1},{17,25},{25,17},{2,10},{10... | collective-permute-start | bytes 196616 | tf_op jit(solution)/shard_map/ppermute | solution.py:525
  41.6 1.2 %copy-start.10 = (bf16[256,128]{1,0:T(8,128)(2,1)S(1)}, bf16[256,128]{1,0:T(8,128)(2,1)}, u32[]{:S(2)}) copy-start(bf16[256,128]{1,0:T(8,128)(2,1)} %copy-done.9) | copy-start | bytes 196612
  41.6 2.8 %copy-start.1 = (bf16[7,512,256]{2,1,0:T(8,128)(2,1)S(1)}, bf16[7,512,256]{2,1,0:T(8,128)(2,1)}, u32[]{:S(2)}) copy-start(bf16[7,512,256]{2,1,0:T(8,128)(2,1)} %constant.19.clone.b_ref) | copy-start | bytes 5505028
  41.7 2.8 %copy-start.6 = (bf16[2,256,256]{2,1,0:T(8,128)(2,1)S(1)}, bf16[2,256,256]{2,1,0:T(8,128)(2,1)}, u32[]{:S(2)}) copy-start(bf16[2,256,256]{2,1,0:T(8,128)(2,1)} %constant.18.clone.br_ref) | copy-start | bytes 786436
  42.7 9.8 %collective-permute-start.15 = (bf16[256,128]{1,0:T(8,128)(2,1)S(1)}, bf16[256,128]{1,0:T(8,128)(2,1)S(1)}, u32[]{:S(2)}, u32[]{:S(2)}) collective-permute-start(bf16[256,128]{1,0:T(8,128)(2,1)S(1)} %copy-done.12), channel_id=1, source_target_pairs={{0,16},{8,24},{16,0},{24,8},{1,17},{9,25},{17,1},{25,9},{2,18},{10... | collective-permute-start | bytes 196616 | tf_op jit(solution)/shard_map/ppermute | solution.py:525
  42.8 9.7 %collective-permute-start.16 = (bf16[256,128]{1,0:T(8,128)(2,1)S(1)}, bf16[256,128]{1,0:T(8,128)(2,1)S(1)}, u32[]{:S(2)}, u32[]{:S(2)}) collective-permute-start(bf16[256,128]{1,0:T(8,128)(2,1)S(1)} %copy-done.10), channel_id=1, source_target_pairs={{0,24},{8,16},{16,8},{24,0},{1,25},{9,17},{17,9},{25,1},{2,26},{10... | collective-permute-start | bytes 196616 | tf_op jit(solution)/shard_map/ppermute | solution.py:525
  47.2 11.3 %collective-permute-start.12 = (bf16[512,128]{1,0:T(8,128)(2,1)S(1)}, bf16[512,128]{1,0:T(8,128)(2,1)S(1)}, u32[]{:S(2)}, u32[]{:S(2)}) collective-permute-start(bf16[512,128]{1,0:T(8,128)(2,1)S(1)} %get-tuple-element.47), channel_id=1, source_target_pairs={{0,16},{8,24},{16,0},{24,8},{1,17},{9,25},{17,1},{25,9},{2,18},{10... | collective-permute-start | bytes 393224 | tf_op jit(solution)/shard_map/ppermute | solution.py:525
  49.2 11.1 %collective-permute-start.13 = (bf16[512,128]{1,0:T(8,128)(2,1)S(1)}, bf16[512,128]{1,0:T(8,128)(2,1)S(1)}, u32[]{:S(2)}, u32[]{:S(2)}) collective-permute-start(bf16[512,128]{1,0:T(8,128)(2,1)S(1)} %get-tuple-element.48), channel_id=1, source_target_pairs={{0,24},{8,16},{16,8},{24,0},{1,25},{9,17},{17,9},{25,1},{2,26},{10... | collective-permute-start | bytes 393224 | tf_op jit(solution)/shard_map/ppermute | solution.py:525
  52.6 12.9 %copy-start.2 = (bf16[512,512]{1,0:T(8,128)(2,1)S(1)}, bf16[512,512]{1,0:T(8,128)(2,1)}, u32[]{:S(2)}) copy-start(bf16[512,512]{1,0:T(8,128)(2,1)} %refs_4_.3) | copy-start | bytes 1572868
  52.6 12.9 %copy-start.3 = (bf16[512,512]{1,0:T(8,128)(2,1)S(1)}, bf16[512,512]{1,0:T(8,128)(2,1)}, u32[]{:S(2)}) copy-start(bf16[512,512]{1,0:T(8,128)(2,1)} %refs_5_.3) | copy-start | bytes 1572868
  55.3 6.4 %collective-permute-start.17 = (bf16[512,128]{1,0:T(8,128)(2,1)S(1)}, bf16[512,128]{1,0:T(8,128)(2,1)S(1)}, u32[]{:S(2)}, u32[]{:S(2)}) collective-permute-start(bf16[512,128]{1,0:T(8,128)(2,1)S(1)} %get-tuple-element.53), channel_id=1, source_target_pairs={{0,8},{8,0},{16,24},{24,16},{1,9},{9,1},{17,25},{25,17},{2,10},{10... | collective-permute-start | bytes 393224 | tf_op jit(solution)/shard_map/ppermute | solution.py:525
  55.8 9.7 %collective-permute-start.20 = (bf16[512,128]{1,0:T(8,128)(2,1)S(1)}, bf16[512,128]{1,0:T(8,128)(2,1)S(1)}, u32[]{:S(2)}, u32[]{:S(2)}) collective-permute-start(bf16[512,128]{1,0:T(8,128)(2,1)S(1)} %get-tuple-element.59), channel_id=1, source_target_pairs={{0,8},{8,0},{16,24},{24,16},{1,9},{9,1},{17,25},{25,17},{2,10},{10... | collective-permute-start | bytes 393224 | tf_op jit(solution)/shard_map/ppermute | solution.py:525
  57.4 12.0 %collective-permute-start.18 = (bf16[512,128]{1,0:T(8,128)(2,1)S(1)}, bf16[512,128]{1,0:T(8,128)(2,1)S(1)}, u32[]{:S(2)}, u32[]{:S(2)}) collective-permute-start(bf16[512,128]{1,0:T(8,128)(2,1)S(1)} %get-tuple-element.56), channel_id=1, source_target_pairs={{0,16},{8,24},{16,0},{24,8},{1,17},{9,25},{17,1},{25,9},{2,18},{10... | collective-permute-start | bytes 393224 | tf_op jit(solution)/shard_map/ppermute | solution.py:525
  58.5 10.9 %collective-permute-start.19 = (bf16[512,128]{1,0:T(8,128)(2,1)S(1)}, bf16[512,128]{1,0:T(8,128)(2,1)S(1)}, u32[]{:S(2)}, u32[]{:S(2)}) collective-permute-start(bf16[512,128]{1,0:T(8,128)(2,1)S(1)} %get-tuple-element.57), channel_id=1, source_target_pairs={{0,24},{8,16},{16,8},{24,0},{1,25},{9,17},{17,9},{25,1},{2,26},{10... | collective-permute-start | bytes 393224 | tf_op jit(solution)/shard_map/ppermute | solution.py:525
  (3 other events, 2.3 us)

commit v4 on v3

--- a/solution.py
+++ b/solution.py
@@ -153,10 +153,12 @@
             read.wait()
         inner = key_ref[j].astype(F32) * value_ref[j].astype(F32)
         taps = taps_ref[j].astype(F32)
-        out_ref[j, :, :LANES] = join_low(taps, inner).astype(BF16)
-        out_ref[j, :, LANES:] = join_high(taps, inner).astype(BF16)
-        writes.append(pltpu.make_async_copy(out_ref.at[j], out_hbm.at[j], out_sems.at[j]))
-        writes[-1].start()
+        lanes = slice(j // 2 * LANES, (j // 2 + 1) * LANES)
+        for i, join in enumerate((join_low, join_high)):
+            owner = j % 2 * 2 + i
+            out_ref[owner, :, lanes] = join(taps, inner).astype(BF16)
+            writes.append(pltpu.make_async_copy(out_ref.at[owner, :, lanes], out_hbm.at[owner, :, lanes], out_sems.at[j, i]))
+            writes[-1].start()
     for write in writes:
         write.wait()
 
@@ -239,15 +241,18 @@
         o[...] = res_ref[pl.ds(pl.multiple_of((z ^ s) * length, length), length), :]
 
 
-def finish_kernel(factor, distances, ids_ref, *refs):
+def finish_kernel(factor, firsts, distances, ids_ref, *refs):
     n = len(distances)
-    lows, highs = refs[:n], refs[n : 2 * n]
+    parts = refs[: 2 * n]
     key_ref, value_ref = refs[2 * n : 2 * n + 2]
     gk_hbm, gv_hbm, gt_hbm, gk_ref, gv_ref, gt_ref, sems = refs[-7:]
     writes = []
     for i, distance in enumerate(distances):
-        low, high = lows[i][...].astype(F32), highs[i][...].astype(F32)
-        cols = pl.ds(pl.multiple_of((ids_ref[0] ^ distance) * LANES, LANES), LANES)
+        owner = ids_ref[0] ^ distance
+        one, other = parts[2 * i][...].astype(F32), parts[2 * i + 1][...].astype(F32)
+        even = owner % 2 == 0
+        low, high = jnp.where(even, one, other), jnp.where(even, other, one)
+        cols = pl.ds(pl.multiple_of((firsts[i] + owner // 2) * LANES, LANES), LANES)
         gt_ref[i] = join_high(low, high) * factor
         grad = join_low(low, high)
         gk_ref[i] = (value_ref[:, cols].astype(F32) * grad).astype(BF16)
@@ -281,19 +286,21 @@
         block[:half, i * depth : (i + 1) * depth] = top[...]
         block[half:, i * depth : (i + 1) * depth] = low[...]
     sums[...] = before[...] + dot(block[...], turned_ref[...])
-    gate_half(join_low, ids_ref, sums, gate, (o0, o1, o2, o3))
-
-
-def gate_half(join, ids_ref, sums, gate, outs):
+    gate_half(0, ids_ref, sums, gate, (o0, o1, o2, o3))
+
+
+def gate_half(first, ids_ref, sums, gate, outs):
     half = sums.shape[0] // 2
     for s, o in enumerate(outs):
-        cols = pl.ds(pl.multiple_of((ids_ref[0] ^ s) * LANES, LANES), LANES)
+        owner = ids_ref[0] ^ s
+        cols = pl.ds(pl.multiple_of((first + owner // 2) * LANES, LANES), LANES)
         grad = gate[:, cols].astype(F32) * sums[:, cols]
-        o[...] = join(grad[:half], grad[half:]).astype(BF16)
+        even = owner % 2 == 0
+        o[...] = jnp.where(even, join_low(grad[:half], grad[half:]), join_high(grad[:half], grad[half:])).astype(BF16)
 
 
 def gate_high_kernel(ids_ref, sums, gate, o0, o1, o2, o3):
-    gate_half(join_high, ids_ref, sums, gate, (o0, o1, o2, o3))
+    gate_half(2, ids_ref, sums, gate, (o0, o1, o2, o3))
 
 
 VMEM = pl.BlockSpec(memory_space=pltpu.VMEM)
@@ -358,7 +365,7 @@
         in_specs=[ANY] * 3,
         out_specs=ANY,
         scratch_shapes=[pltpu.VMEM((parts, length, LANES), BF16)] * 3
-        + [pltpu.VMEM(shape, BF16), pltpu.SemaphoreType.DMA((3, parts)), pltpu.SemaphoreType.DMA((parts,))],
+        + [pltpu.VMEM(shape, BF16), pltpu.SemaphoreType.DMA((3, parts)), pltpu.SemaphoreType.DMA((parts, 2))],
         compiler_params=limits(56),
         cost_estimate=cost(0, 10 * taps.size),
     )(taps, key, value)
@@ -397,12 +404,12 @@
     )(ids, *grads, spec, *tables)
 
 
-def finish(ids, lows, highs, distances, key, value, factor, before=()):
+def finish(ids, parts, firsts, distances, key, value, factor, before=()):
     length, n = key.shape[0], len(distances)
-    ins = [*lows, *highs, key, value, *before]
+    ins = [*parts, key, value, *before]
     held = lambda dtype: pltpu.VMEM((n, length, LANES), dtype)
     return pl.pallas_call(
-        functools.partial(finish_kernel, factor, distances),
+        functools.partial(finish_kernel, factor, firsts, distances),
         out_shape=[jax.ShapeDtypeStruct(key.shape, BF16), jax.ShapeDtypeStruct(key.shape, BF16), jax.ShapeDtypeStruct(key.shape, F32)],
         in_specs=[SMEM] + [VMEM] * (2 * n + 2) + [ANY] * len(before),
         out_specs=[ANY] * 3,
@@ -549,8 +556,8 @@
     high = spread(correlate(ids, high_grads, high_spec, tables))
     factor = 1.0 / math.sqrt(parts * length)
     low[2], low[3], high[1] = lax.optimization_barrier((low[2], low[3], high[1]))
-    near = finish(ids, low[:2], high[:2], (0, 1), key_proj, value_proj, factor)
-    return tuple(finish(ids, low[2:], high[2:], (2, 3), key_proj, value_proj, factor, near))
+    done = finish(ids, [*low, *high[:2]], (0, 0, 2), (0, 2, 0), key_proj, value_proj, factor)
+    return tuple(finish(ids, high[2:], (2,), (2,), key_proj, value_proj, factor, done))
 
 
 def per_device(*arrays):

time: 71.4 us -> 71.5 us (level)
    all_to_all x1, waiting for transfers between devices: 2.55 us -> 3.29 us  [exchanged_layer(): lax.all_to_all(sent, 'ctx', 0, 0, tiled=True)]
where the time goes in v4:
time: 71.5 us; the launch traced here: 71.2 us
  starting transfers between devices  28.8 us (40%)
  Pallas kernels  20.1 us (28%)
  waiting for transfers between devices  17.9 us (25%)
  local copies, waits for them, and re-layouts  3.51 us (5%)
  between operations  0.83 us (1%)
    ppermute x21, starting transfers between devices, hop(): return lax.ppermute(x, axis, [(j, j ^ distance) for j in range(n)])  23.9 us
    ppermute x21, waiting for transfers between devices, hop(): return lax.ppermute(x, axis, [(j, j ^ distance) for j in range(n)])  14.6 us
    pallas_call x2, Pallas kernels, correlate(): pl.pallas_call(correlate_kernel, out_shape=[jax.ShapeDtypeStruct((length,...  5.38 us
    all_to_all x1, starting transfers between devices, exchanged_layer(): lax.all_to_all(sent, 'ctx', 0, 0, tiled=True)  4.88 us
    unnamed x26, local copies, waits for them, and re-layouts  3.47 us
    pallas_call x2, Pallas kernels, finish(): pl.pallas_call(functools.partial(finish_kernel, factor, firsts, distances...  3.4 us
    all_to_all x1, waiting for transfers between devices, exchanged_layer(): lax.all_to_all(sent, 'ctx', 0, 0, tiled=True)  3.29 us
    pallas_call x1, Pallas kernels, project_near(): pl.pallas_call(project_near_kernel, in_specs=[SMEM] + [VMEM] * (1 + len(b...  3.04 us
  transfers between devices with their start and end apart: 22, of which 10 were waited for; matrix products, arithmetic and copies ran while one was open for 0% of the time, Pallas kernels for 26%

profile of v4, /device:TPU:0, one launch (start us, length us, event | category | flops | bytes accessed | tf_op | source)
XLA Modules:
  0.0 71.2 jit_solution(11832005900745123764)
XLA Ops:
  0.6 3.0 %collective-permute-start.1 = (bf16[512,512]{1,0:T(8,128)(2,1)}, bf16[512,512]{1,0:T(8,128)(2,1)S(1)}, u32[]{:S(2)}, u32[]{:S(2)}) collective-permute-start(bf16[512,512]{1,0:T(8,128)(2,1)} %refs_0_.1), channel_id=1, source_target_pairs={{0,2},{1,3},{2,0},{3,1},{4,6},{5,7},{6,4},{7,5},{8,10},{9,11},{10,... | collective-permute-start | bytes 1572872 | tf_op jit(solution)/shard_map/ppermute | solution.py:532
  3.6 1.5 %collective-permute-start.3 = (bf16[512,512]{1,0:T(8,128)(2,1)}, bf16[512,512]{1,0:T(8,128)(2,1)S(1)}, u32[]{:S(2)}, u32[]{:S(2)}) collective-permute-start(bf16[512,512]{1,0:T(8,128)(2,1)} %refs_0_.1), channel_id=1, source_target_pairs={{0,4},{1,5},{2,6},{3,7},{4,0},{5,1},{6,2},{7,3},{8,12},{9,13},{10,... | collective-permute-start | bytes 1572872 | tf_op jit(solution)/shard_map/ppermute | solution.py:532
  5.2 2.5 %shard_map.124 = bf16[4,512,256]{2,1,0:T(8,128)(2,1)} custom-call(bf16[512,512]{1,0:T(8,128)(2,1)} %taps_hbm.1, bf16[512,512]{1,0:T(8,128)(2,1)} %refs_2_.1, bf16[512,512]{1,0:T(8,128)(2,1)} %refs_3_.1), custom_call_target="tpu_custom_call" | custom-call | bytes 2621440 | tf_op jit(solution)/shard_map/pallas_call | solution.py:362
  7.7 4.9 %all-to-all-start = ((bf16[4,512,256]{2,1,0:T(8,128)(2,1)}), bf16[4,512,256]{2,1,0:T(8,128)(2,1)S(1)}, u32[]{:S(2)}, u32[]{:S(2)}) async-start(bf16[4,512,256]{2,1,0:T(8,128)(2,1)} %shard_map.124), calls=%async_computation | async-start | bytes 2097152 | tf_op jit(solution)/shard_map/all_to_all | solution.py:543
  12.6 3.2 %collective-permute-done.1.refs_2_ = bf16[512,512]{1,0:T(8,128)(2,1)S(1)} collective-permute-done((bf16[512,512]{1,0:T(8,128)(2,1)}, bf16[512,512]{1,0:T(8,128)(2,1)S(1)}, u32[]{:S(2)}, u32[]{:S(2)}) %collective-permute-start.1) | collective-permute-done | bytes 524320 | tf_op jit(solution)/shard_map/ppermute | solution.py:532
  15.8 1.5 %collective-permute-done.3.refs_4_ = bf16[512,512]{1,0:T(8,128)(2,1)S(1)} collective-permute-done((bf16[512,512]{1,0:T(8,128)(2,1)}, bf16[512,512]{1,0:T(8,128)(2,1)S(1)}, u32[]{:S(2)}, u32[]{:S(2)}) %collective-permute-start.3) | collective-permute-done | bytes 524320 | tf_op jit(solution)/shard_map/ppermute | solution.py:532
  17.3 0.9 %collective-permute-start.5 = (bf16[256,512]{1,0:T(8,128)(2,1)S(1)}, bf16[256,512]{1,0:T(8,128)(2,1)S(1)}, u32[]{:S(2)}, u32[]{:S(2)}) collective-permute-start(bf16[256,512]{1,0:T(8,128)(2,1)S(1)} %slice.8), channel_id=1, source_target_pairs={{0,2},{1,3},{2,0},{3,1},{4,6},{5,7},{6,4},{7,5},{8,10},{9,11},{10,... | collective-permute-start | bytes 786440 | tf_op jit(solution)/shard_map/ppermute | solution.py:532
  18.2 1.6 %collective-permute-start.6 = (bf16[256,512]{1,0:T(8,128)(2,1)S(1)}, bf16[256,512]{1,0:T(8,128)(2,1)S(1)}, u32[]{:S(2)}, u32[]{:S(2)}) collective-permute-start(bf16[256,512]{1,0:T(8,128)(2,1)S(1)} %slice.9), channel_id=1, source_target_pairs={{0,4},{1,5},{2,6},{3,7},{4,0},{5,1},{6,2},{7,3},{8,12},{9,13},{10,... | collective-permute-start | bytes 786440 | tf_op jit(solution)/shard_map/ppermute | solution.py:532
  19.8 2.2 %copy-done.7 = bf16[512,4096]{1,0:T(8,128)(2,1)S(1)} copy-done((bf16[512,4096]{1,0:T(8,128)(2,1)S(1)}, bf16[512,4096]{1,0:T(8,128)(2,1)}, u32[]{:S(2)}) %copy-start.7) | copy-done | bytes 4194328
  22.0 3.0 %shard_map.121 = (f32[512,512]{1,0:T(8,128)S(1)}, bf16[1024,512]{1,0:T(8,128)(2,1)S(1)}) custom-call(s32[2]{0:T(128)S(1)} %pad_add_fusion.ids_ref, bf16[512,4096]{1,0:T(8,128)(2,1)S(1)} %copy-done.7, bf16[512,512]{1,0:T(8,128)(2,1)S(1)} %copy-done.8, bf16[512,512]{1,0:T(8,128)(2,1)S(1)} %collective-permute-done.refs_1_, ...), custom_call_target="tpu_custom_call" | custom-call | flops 5000000000 | tf_op jit(solution)/shard_map/pallas_call | solution.py:322
  25.1 1.1 %collective-permute-done.5.top0 = bf16[256,512]{1,0:T(8,128)(2,1)S(1)} collective-permute-done((bf16[256,512]{1,0:T(8,128)(2,1)S(1)}, bf16[256,512]{1,0:T(8,128)(2,1)S(1)}, u32[]{:S(2)}, u32[]{:S(2)}) %collective-permute-start.5) | collective-permute-done | bytes 262176 | tf_op jit(solution)/shard_map/ppermute | solution.py:532
  26.8 1.0 %collective-permute-done.7.top1 = bf16[256,512]{1,0:T(8,128)(2,1)S(1)} collective-permute-done((bf16[256,512]{1,0:T(8,128)(2,1)S(1)}, bf16[256,512]{1,0:T(8,128)(2,1)S(1)}, u32[]{:S(2)}, u32[]{:S(2)}) %collective-permute-start.7) | collective-permute-done | bytes 262176 | tf_op jit(solution)/shard_map/ppermute | solution.py:532
  28.2 2.2 %shard_map.122 = (bf16[256,128]{1,0:T(8,128)(2,1)S(1)}, bf16[256,128]{1,0:T(8,128)(2,1)}, bf16[256,128]{1,0:T(8,128)(2,1)}, bf16[256,128]{1,0:T(8,128)(2,1)}, f32[512,512]{1,0:T(8,128)S(1)}) custom-call(s32[2]{0:T(128)S(1)} %pad_add_fusion.ids_ref, bf16[1024,512]{1,0:T(8,128)(2,1)S(1)} %get-tuple-element.34.turned_ref, ...), custom_call_target="tpu_custom_call" | custom-call | flops 536870912 | tf_op jit(solution)/shard_map/pallas_call | solution.py:335
  30.4 1.7 %collective-permute-start.14 = (bf16[256,128]{1,0:T(8,128)(2,1)}, bf16[256,128]{1,0:T(8,128)(2,1)S(1)}, u32[]{:S(2)}, u32[]{:S(2)}) collective-permute-start(bf16[256,128]{1,0:T(8,128)(2,1)} %get-tuple-element.49), channel_id=1, source_target_pairs={{0,8},{8,0},{16,24},{24,16},{1,9},{9,1},{17,25},{25,17},{2,10},{10... | collective-permute-start | bytes 196616 | tf_op jit(solution)/shard_map/ppermute | solution.py:532
  32.2 2.6 %collective-permute-start.15 = (bf16[256,128]{1,0:T(8,128)(2,1)}, bf16[256,128]{1,0:T(8,128)(2,1)S(1)}, u32[]{:S(2)}, u32[]{:S(2)}) collective-permute-start(bf16[256,128]{1,0:T(8,128)(2,1)} %get-tuple-element.50), channel_id=1, source_target_pairs={{0,16},{8,24},{16,0},{24,8},{1,17},{9,25},{17,1},{25,9},{2,18},{10... | collective-permute-start | bytes 196616 | tf_op jit(solution)/shard_map/ppermute | solution.py:532
  34.8 1.4 %shard_map.123 = (bf16[256,128]{1,0:T(8,128)(2,1)S(1)}, bf16[256,128]{1,0:T(8,128)(2,1)}, bf16[256,128]{1,0:T(8,128)(2,1)S(1)}, bf16[256,128]{1,0:T(8,128)(2,1)S(1)}) custom-call(s32[2]{0:T(128)S(1)} %pad_add_fusion.ids_ref, f32[512,512]{1,0:T(8,128)S(1)} %get-tuple-element.39.sums, bf16[512,512]{1,0:T(8,128)(2,1)S(1)} %copy-done.5), custom_call_target="tpu_custom_call" | custom-call | flops 262144 | tf_op jit(solution)/shard_map/pallas_call | solution.py:349
  38.3 3.3 %all-to-all-done = bf16[4,512,256]{2,1,0:T(8,128)(2,1)S(1)} async-done(((bf16[4,512,256]{2,1,0:T(8,128)(2,1)}), bf16[4,512,256]{2,1,0:T(8,128)(2,1)S(1)}, u32[]{:S(2)}, u32[]{:S(2)}) %all-to-all-start) | async-done | bytes 1048608 | tf_op jit(solution)/shard_map/all_to_all | solution.py:543
  41.7 1.1 %shard_map.125.spec_ref = bf16[8,512,128]{2,1,0:T(8,128)(2,1)S(1)} custom-call(bf16[2048,256]{1,0:T(8,128)(2,1)S(1)} %bitcast.3, bf16[2,256,256]{2,1,0:T(8,128)(2,1)S(1)} %copy-done.4, bf16[7,512,256]{2,1,0:T(8,128)(2,1)S(1)} %copy-done), custom_call_target="tpu_custom_call" | custom-call | flops 536870912 | tf_op jit(solution)/shard_map/pallas_call | solution.py:376
  43.0 1.2 %collective-permute-start.11 = (bf16[256,128]{1,0:T(8,128)(2,1)S(1)}, bf16[256,128]{1,0:T(8,128)(2,1)S(1)}, u32[]{:S(2)}, u32[]{:S(2)}) collective-permute-start(bf16[256,128]{1,0:T(8,128)(2,1)S(1)} %copy-done.10), channel_id=1, source_target_pairs={{0,24},{8,16},{16,8},{24,0},{1,25},{9,17},{17,9},{25,1},{2,26},{10... | collective-permute-start | bytes 196616 | tf_op jit(solution)/shard_map/ppermute | solution.py:532
  44.2 2.7 %shard_map.128 = (bf16[512,128]{1,0:T(8,128)(2,1)S(1)}, bf16[512,128]{1,0:T(8,128)(2,1)S(1)}, bf16[512,128]{1,0:T(8,128)(2,1)S(1)}, bf16[512,128]{1,0:T(8,128)(2,1)S(1)}) custom-call(s32[2]{0:T(128)S(1)} %pad_add_fusion.ids_ref, bf16[256,128]{1,0:T(8,128)(2,1)S(1)} %get-tuple-element.48.g0, bf16[256,128]{1,0:T(8,128)(2,1)S(1)} %collective-permute-done.14.g1, ...), custom_call_target="tpu_custom_call" | custom-call | flops 1073741824 | tf_op jit(solution)/shard_map/pallas_call | solution.py:390
  46.9 2.0 %collective-permute-start.18 = (bf16[512,128]{1,0:T(8,128)(2,1)S(1)}, bf16[512,128]{1,0:T(8,128)(2,1)S(1)}, u32[]{:S(2)}, u32[]{:S(2)}) collective-permute-start(bf16[512,128]{1,0:T(8,128)(2,1)S(1)} %get-tuple-element.55), channel_id=1, source_target_pairs={{0,16},{8,24},{16,0},{24,8},{1,17},{9,25},{17,1},{25,9},{2,18},{10... | collective-permute-start | bytes 393224 | tf_op jit(solution)/shard_map/ppermute | solution.py:532
  48.9 2.5 %collective-permute-start.19 = (bf16[512,128]{1,0:T(8,128)(2,1)S(1)}, bf16[512,128]{1,0:T(8,128)(2,1)S(1)}, u32[]{:S(2)}, u32[]{:S(2)}) collective-permute-start(bf16[512,128]{1,0:T(8,128)(2,1)S(1)} %get-tuple-element.56), channel_id=1, source_target_pairs={{0,24},{8,16},{16,8},{24,0},{1,25},{9,17},{17,9},{25,1},{2,26},{10... | collective-permute-start | bytes 393224 | tf_op jit(solution)/shard_map/ppermute | solution.py:532
  51.5 1.1 %shard_map.126.spec_ref = bf16[8,512,128]{2,1,0:T(8,128)(2,1)S(1)} custom-call(bf16[2048,256]{1,0:T(8,128)(2,1)S(1)} %bitcast.4, bf16[2,256,256]{2,1,0:T(8,128)(2,1)S(1)} %copy-done.4, bf16[7,512,256]{2,1,0:T(8,128)(2,1)S(1)} %copy-done), custom_call_target="tpu_custom_call" | custom-call | flops 536870912 | tf_op jit(solution)/shard_map/pallas_call | solution.py:376
  52.6 2.7 %shard_map.127 = (bf16[512,128]{1,0:T(8,128)(2,1)S(1)}, bf16[512,128]{1,0:T(8,128)(2,1)S(1)}, bf16[512,128]{1,0:T(8,128)(2,1)S(1)}, bf16[512,128]{1,0:T(8,128)(2,1)S(1)}) custom-call(s32[2]{0:T(128)S(1)} %pad_add_fusion.ids_ref, bf16[256,128]{1,0:T(8,128)(2,1)S(1)} %get-tuple-element.40.g0, bf16[256,128]{1,0:T(8,128)(2,1)S(1)} %collective-permute-done.9.g1, ...), custom_call_target="tpu_custom_call" | custom-call | flops 1073741824 | tf_op jit(solution)/shard_map/pallas_call | solution.py:390
  55.3 0.9 %collective-permute-start.20 = (bf16[512,128]{1,0:T(8,128)(2,1)S(1)}, bf16[512,128]{1,0:T(8,128)(2,1)S(1)}, u32[]{:S(2)}, u32[]{:S(2)}) collective-permute-start(bf16[512,128]{1,0:T(8,128)(2,1)S(1)} %get-tuple-element.57), channel_id=1, source_target_pairs={{0,8},{8,0},{16,24},{24,16},{1,9},{9,1},{17,25},{25,17},{2,10},{10... | collective-permute-start | bytes 393224 | tf_op jit(solution)/shard_map/ppermute | solution.py:532
  56.2 1.2 %collective-permute-start.17 = (bf16[512,128]{1,0:T(8,128)(2,1)S(1)}, bf16[512,128]{1,0:T(8,128)(2,1)S(1)}, u32[]{:S(2)}, u32[]{:S(2)}) collective-permute-start(bf16[512,128]{1,0:T(8,128)(2,1)S(1)} %get-tuple-element.54), channel_id=1, source_target_pairs={{0,8},{8,0},{16,24},{24,16},{1,9},{9,1},{17,25},{25,17},{2,10},{10... | collective-permute-start | bytes 393224 | tf_op jit(solution)/shard_map/ppermute | solution.py:532
  57.4 2.6 %collective-permute-start.12 = (bf16[512,128]{1,0:T(8,128)(2,1)S(1)}, bf16[512,128]{1,0:T(8,128)(2,1)S(1)}, u32[]{:S(2)}, u32[]{:S(2)}) collective-permute-start(bf16[512,128]{1,0:T(8,128)(2,1)S(1)} %get-tuple-element.46), channel_id=1, source_target_pairs={{0,16},{8,24},{16,0},{24,8},{1,17},{9,25},{17,1},{25,9},{2,18},{10... | collective-permute-start | bytes 393224 | tf_op jit(solution)/shard_map/ppermute | solution.py:532
  60.6 2.0 %collective-permute-done.20.refs_5_ = bf16[512,128]{1,0:T(8,128)(2,1)S(1)} collective-permute-done((bf16[512,128]{1,0:T(8,128)(2,1)S(1)}, bf16[512,128]{1,0:T(8,128)(2,1)S(1)}, u32[]{:S(2)}, u32[]{:S(2)}) %collective-permute-start.20) | collective-permute-done | bytes 131104 | tf_op jit(solution)/shard_map/ppermute | solution.py:532
  62.6 4.0 %collective-permute-done.17.refs_1_ = bf16[512,128]{1,0:T(8,128)(2,1)S(1)} collective-permute-done((bf16[512,128]{1,0:T(8,128)(2,1)S(1)}, bf16[512,128]{1,0:T(8,128)(2,1)S(1)}, u32[]{:S(2)}, u32[]{:S(2)}) %collective-permute-start.17) | collective-permute-done | bytes 131104 | tf_op jit(solution)/shard_map/ppermute | solution.py:532
  66.5 1.9 %shard_map.129 = (bf16[512,512]{1,0:T(8,128)(2,1)}, bf16[512,512]{1,0:T(8,128)(2,1)}, f32[512,512]{1,0:T(8,128)}) custom-call(s32[2]{0:T(128)S(1)} %pad_add_fusion.ids_ref, bf16[512,128]{1,0:T(8,128)(2,1)S(1)} %get-tuple-element.53.refs_0_, bf16[512,128]{1,0:T(8,128)(2,1)S(1)} %collective-permute-done.17.refs_1_, ...), custom_call_target="tpu_custom_call" | custom-call | bytes 3145728 | tf_op jit(solution)/shard_map/pallas_call | solution.py:411
  68.5 1.3 %collective-permute-done.12.refs_0_ = bf16[512,128]{1,0:T(8,128)(2,1)S(1)} collective-permute-done((bf16[512,128]{1,0:T(8,128)(2,1)S(1)}, bf16[512,128]{1,0:T(8,128)(2,1)S(1)}, u32[]{:S(2)}, u32[]{:S(2)}) %collective-permute-start.12) | collective-permute-done | bytes 131104 | tf_op jit(solution)/shard_map/ppermute | solution.py:532
  69.7 1.5 %shard_map.130 = (bf16[512,512]{1,0:T(8,128)(2,1)}, bf16[512,512]{1,0:T(8,128)(2,1)}, f32[512,512]{1,0:T(8,128)}) custom-call(s32[2]{0:T(128)S(1)} %pad_add_fusion.ids_ref, bf16[512,128]{1,0:T(8,128)(2,1)S(1)} %collective-permute-done.12.refs_0_, ...), custom_call_target="tpu_custom_call", output_to_operand_aliasing={{0}: (5, {}), {1}: (6, {}), {2}: (7, {})} | custom-call | bytes 1048576 | tf_op jit(solution)/shard_map/pallas_call | solution.py:411
  (51 shorter events, 4.2 us)
Async XLA Ops:
  0.6 11.9 %copy-start.8 = (bf16[512,512]{1,0:T(8,128)(2,1)S(1)}, bf16[512,512]{1,0:T(8,128)(2,1)}, u32[]{:S(2)}) copy-start(bf16[512,512]{1,0:T(8,128)(2,1)} %refs_0_.1) | copy-start | bytes 1572868
  0.6 15.1 %collective-permute-start.1 = (bf16[512,512]{1,0:T(8,128)(2,1)}, bf16[512,512]{1,0:T(8,128)(2,1)S(1)}, u32[]{:S(2)}, u32[]{:S(2)}) collective-permute-start(bf16[512,512]{1,0:T(8,128)(2,1)} %refs_0_.1), channel_id=1, source_target_pairs={{0,2},{1,3},{2,0},{3,1},{4,6},{5,7},{6,4},{7,5},{8,10},{9,11},{10,... | collective-permute-start | bytes 1572872 | tf_op jit(solution)/shard_map/ppermute | solution.py:532
  3.6 13.6 %collective-permute-start.3 = (bf16[512,512]{1,0:T(8,128)(2,1)}, bf16[512,512]{1,0:T(8,128)(2,1)S(1)}, u32[]{:S(2)}, u32[]{:S(2)}) collective-permute-start(bf16[512,512]{1,0:T(8,128)(2,1)} %refs_0_.1), channel_id=1, source_target_pairs={{0,4},{1,5},{2,6},{3,7},{4,0},{5,1},{6,2},{7,3},{8,12},{9,13},{10,... | collective-permute-start | bytes 1572872 | tf_op jit(solution)/shard_map/ppermute | solution.py:532
  7.7 34.0 %all-to-all-start = ((bf16[4,512,256]{2,1,0:T(8,128)(2,1)}), bf16[4,512,256]{2,1,0:T(8,128)(2,1)S(1)}, u32[]{:S(2)}, u32[]{:S(2)}) async-start(bf16[4,512,256]{2,1,0:T(8,128)(2,1)} %shard_map.124), calls=%async_computation | async-start | bytes 2097152 | tf_op jit(solution)/shard_map/all_to_all | solution.py:543
  12.5 7.3 %collective-permute-start = (bf16[512,512]{1,0:T(8,128)(2,1)S(1)}, bf16[512,512]{1,0:T(8,128)(2,1)S(1)}, u32[]{:S(2)}, u32[]{:S(2)}) collective-permute-start(bf16[512,512]{1,0:T(8,128)(2,1)S(1)} %copy-done.8), channel_id=1, source_target_pairs={{0,1},{1,0},{2,3},{3,2},{4,5},{5,4},{6,7},{7,6},{8,9},{9,8},{10,11... | collective-permute-start | bytes 1572872 | tf_op jit(solution)/shard_map/ppermute | solution.py:532
  15.8 4.0 %collective-permute-start.2 = (bf16[512,512]{1,0:T(8,128)(2,1)S(1)}, bf16[512,512]{1,0:T(8,128)(2,1)}, u32[]{:S(2)}, u32[]{:S(2)}) collective-permute-start(bf16[512,512]{1,0:T(8,128)(2,1)S(1)} %collective-permute-done.1.refs_2_), channel_id=1, source_target_pairs={{0,1},{1,0},{2,3},{3,2},{4,5},{5,4},{6,7},{7,6},{8,9},{9,8},{10,11... | collective-permute-start | bytes 1572872 | tf_op jit(solution)/shard_map/ppermute | solution.py:532
  17.2 2.6 %collective-permute-start.4 = (bf16[512,512]{1,0:T(8,128)(2,1)S(1)}, bf16[512,512]{1,0:T(8,128)(2,1)}, u32[]{:S(2)}, u32[]{:S(2)}) collective-permute-start(bf16[512,512]{1,0:T(8,128)(2,1)S(1)} %collective-permute-done.3.refs_4_), channel_id=1, source_target_pairs={{0,1},{1,0},{2,3},{3,2},{4,5},{5,4},{6,7},{7,6},{8,9},{9,8},{10,11... | collective-permute-start | bytes 1572872 | tf_op jit(solution)/shard_map/ppermute | solution.py:532
  17.3 8.8 %collective-permute-start.5 = (bf16[256,512]{1,0:T(8,128)(2,1)S(1)}, bf16[256,512]{1,0:T(8,128)(2,1)S(1)}, u32[]{:S(2)}, u32[]{:S(2)}) collective-permute-start(bf16[256,512]{1,0:T(8,128)(2,1)S(1)} %slice.8), channel_id=1, source_target_pairs={{0,2},{1,3},{2,0},{3,1},{4,6},{5,7},{6,4},{7,5},{8,10},{9,11},{10,... | collective-permute-start | bytes 786440 | tf_op jit(solution)/shard_map/ppermute | solution.py:532
  18.2 10.0 %copy-start.5 = (bf16[512,512]{1,0:T(8,128)(2,1)S(1)}, bf16[512,512]{1,0:T(8,128)(2,1)}, u32[]{:S(2)}) copy-start(bf16[512,512]{1,0:T(8,128)(2,1)} %gate.3) | copy-start | bytes 1572868
  18.2 8.1 %collective-permute-start.6 = (bf16[256,512]{1,0:T(8,128)(2,1)S(1)}, bf16[256,512]{1,0:T(8,128)(2,1)S(1)}, u32[]{:S(2)}, u32[]{:S(2)}) collective-permute-start(bf16[256,512]{1,0:T(8,128)(2,1)S(1)} %slice.9), channel_id=1, source_target_pairs={{0,4},{1,5},{2,6},{3,7},{4,0},{5,1},{6,2},{7,3},{8,12},{9,13},{10,... | collective-permute-start | bytes 786440 | tf_op jit(solution)/shard_map/ppermute | solution.py:532
  19.8 2.2 %copy-start.7 = (bf16[512,4096]{1,0:T(8,128)(2,1)S(1)}, bf16[512,4096]{1,0:T(8,128)(2,1)}, u32[]{:S(2)}) copy-start(bf16[512,4096]{1,0:T(8,128)(2,1)} %weight_ref.1) | copy-start | bytes 12582916
  26.3 1.5 %collective-permute-start.7 = (bf16[256,512]{1,0:T(8,128)(2,1)S(1)}, bf16[256,512]{1,0:T(8,128)(2,1)S(1)}, u32[]{:S(2)}, u32[]{:S(2)}) collective-permute-start(bf16[256,512]{1,0:T(8,128)(2,1)S(1)} %collective-permute-done.5.top0), channel_id=1, source_target_pairs={{0,1},{1,0},{2,3},{3,2},{4,5},{5,4},{6,7},{7,6},{8,9},{9,8},{10,11... | collective-permute-start | bytes 786440 | tf_op jit(solution)/shard_map/ppermute | solution.py:532
  26.3 1.9 %collective-permute-start.8 = (bf16[256,512]{1,0:T(8,128)(2,1)S(1)}, bf16[256,512]{1,0:T(8,128)(2,1)S(1)}, u32[]{:S(2)}, u32[]{:S(2)}) collective-permute-start(bf16[256,512]{1,0:T(8,128)(2,1)S(1)} %collective-permute-done.6.low0), channel_id=1, source_target_pairs={{0,1},{1,0},{2,3},{3,2},{4,5},{5,4},{6,7},{7,6},{8,9},{9,8},{10,11... | collective-permute-start | bytes 786440 | tf_op jit(solution)/shard_map/ppermute | solution.py:532
  28.2 13.4 %copy-start = (bf16[7,512,256]{2,1,0:T(8,128)(2,1)S(1)}, bf16[7,512,256]{2,1,0:T(8,128)(2,1)}, u32[]{:S(2)}) copy-start(bf16[7,512,256]{2,1,0:T(8,128)(2,1)} %constant.17.clone.table_ref.f_ref) | copy-start | bytes 5505028
  28.2 13.4 %copy-start.4 = (bf16[2,256,256]{2,1,0:T(8,128)(2,1)S(1)}, bf16[2,256,256]{2,1,0:T(8,128)(2,1)}, u32[]{:S(2)}) copy-start(bf16[2,256,256]{2,1,0:T(8,128)(2,1)} %constant.16.clone.real_ref.fr_ref) | copy-start | bytes 786436
  30.4 12.6 %collective-permute-start.14 = (bf16[256,128]{1,0:T(8,128)(2,1)}, bf16[256,128]{1,0:T(8,128)(2,1)S(1)}, u32[]{:S(2)}, u32[]{:S(2)}) collective-permute-start(bf16[256,128]{1,0:T(8,128)(2,1)} %get-tuple-element.49), channel_id=1, source_target_pairs={{0,8},{8,0},{16,24},{24,16},{1,9},{9,1},{17,25},{25,17},{2,10},{10... | collective-permute-start | bytes 196616 | tf_op jit(solution)/shard_map/ppermute | solution.py:532
  32.2 12.0 %collective-permute-start.15 = (bf16[256,128]{1,0:T(8,128)(2,1)}, bf16[256,128]{1,0:T(8,128)(2,1)S(1)}, u32[]{:S(2)}, u32[]{:S(2)}) collective-permute-start(bf16[256,128]{1,0:T(8,128)(2,1)} %get-tuple-element.50), channel_id=1, source_target_pairs={{0,16},{8,24},{16,0},{24,8},{1,17},{9,25},{17,1},{25,9},{2,18},{10... | collective-permute-start | bytes 196616 | tf_op jit(solution)/shard_map/ppermute | solution.py:532
  34.8 9.5 %collective-permute-start.16 = (bf16[256,128]{1,0:T(8,128)(2,1)}, bf16[256,128]{1,0:T(8,128)(2,1)S(1)}, u32[]{:S(2)}, u32[]{:S(2)}) collective-permute-start(bf16[256,128]{1,0:T(8,128)(2,1)} %get-tuple-element.51), channel_id=1, source_target_pairs={{0,24},{8,16},{16,8},{24,0},{1,25},{9,17},{17,9},{25,1},{2,26},{10... | collective-permute-start | bytes 196616 | tf_op jit(solution)/shard_map/ppermute | solution.py:532
  37.5 15.0 %collective-permute-start.9 = (bf16[256,128]{1,0:T(8,128)(2,1)}, bf16[256,128]{1,0:T(8,128)(2,1)S(1)}, u32[]{:S(2)}, u32[]{:S(2)}) collective-permute-start(bf16[256,128]{1,0:T(8,128)(2,1)} %get-tuple-element.41), channel_id=1, source_target_pairs={{0,8},{8,0},{16,24},{24,16},{1,9},{9,1},{17,25},{25,17},{2,10},{10... | collective-permute-start | bytes 196616 | tf_op jit(solution)/shard_map/ppermute | solution.py:532
  41.6 1.4 %copy-start.10 = (bf16[256,128]{1,0:T(8,128)(2,1)S(1)}, bf16[256,128]{1,0:T(8,128)(2,1)}, u32[]{:S(2)}) copy-start(bf16[256,128]{1,0:T(8,128)(2,1)} %copy-done.9) | copy-start | bytes 196612
  41.6 2.6 %copy-start.1 = (bf16[7,512,256]{2,1,0:T(8,128)(2,1)S(1)}, bf16[7,512,256]{2,1,0:T(8,128)(2,1)}, u32[]{:S(2)}) copy-start(bf16[7,512,256]{2,1,0:T(8,128)(2,1)} %constant.19.clone.b_ref) | copy-start | bytes 5505028
  41.6 2.6 %copy-start.6 = (bf16[2,256,256]{2,1,0:T(8,128)(2,1)S(1)}, bf16[2,256,256]{2,1,0:T(8,128)(2,1)}, u32[]{:S(2)}) copy-start(bf16[2,256,256]{2,1,0:T(8,128)(2,1)} %constant.18.clone.br_ref) | copy-start | bytes 786436
  42.7 9.8 %collective-permute-start.10 = (bf16[256,128]{1,0:T(8,128)(2,1)S(1)}, bf16[256,128]{1,0:T(8,128)(2,1)S(1)}, u32[]{:S(2)}, u32[]{:S(2)}) collective-permute-start(bf16[256,128]{1,0:T(8,128)(2,1)S(1)} %copy-done.12), channel_id=1, source_target_pairs={{0,16},{8,24},{16,0},{24,8},{1,17},{9,25},{17,1},{25,9},{2,18},{10... | collective-permute-start | bytes 196616 | tf_op jit(solution)/shard_map/ppermute | solution.py:532
  43.0 9.5 %collective-permute-start.11 = (bf16[256,128]{1,0:T(8,128)(2,1)S(1)}, bf16[256,128]{1,0:T(8,128)(2,1)S(1)}, u32[]{:S(2)}, u32[]{:S(2)}) collective-permute-start(bf16[256,128]{1,0:T(8,128)(2,1)S(1)} %copy-done.10), channel_id=1, source_target_pairs={{0,24},{8,16},{16,8},{24,0},{1,25},{9,17},{17,9},{25,1},{2,26},{10... | collective-permute-start | bytes 196616 | tf_op jit(solution)/shard_map/ppermute | solution.py:532
  46.9 13.1 %collective-permute-start.18 = (bf16[512,128]{1,0:T(8,128)(2,1)S(1)}, bf16[512,128]{1,0:T(8,128)(2,1)S(1)}, u32[]{:S(2)}, u32[]{:S(2)}) collective-permute-start(bf16[512,128]{1,0:T(8,128)(2,1)S(1)} %get-tuple-element.55), channel_id=1, source_target_pairs={{0,16},{8,24},{16,0},{24,8},{1,17},{9,25},{17,1},{25,9},{2,18},{10... | collective-permute-start | bytes 393224 | tf_op jit(solution)/shard_map/ppermute | solution.py:532
  48.9 11.6 %collective-permute-start.19 = (bf16[512,128]{1,0:T(8,128)(2,1)S(1)}, bf16[512,128]{1,0:T(8,128)(2,1)S(1)}, u32[]{:S(2)}, u32[]{:S(2)}) collective-permute-start(bf16[512,128]{1,0:T(8,128)(2,1)S(1)} %get-tuple-element.56), channel_id=1, source_target_pairs={{0,24},{8,16},{16,8},{24,0},{1,25},{9,17},{17,9},{25,1},{2,26},{10... | collective-permute-start | bytes 393224 | tf_op jit(solution)/shard_map/ppermute | solution.py:532
  52.6 14.0 %copy-start.2 = (bf16[512,512]{1,0:T(8,128)(2,1)S(1)}, bf16[512,512]{1,0:T(8,128)(2,1)}, u32[]{:S(2)}) copy-start(bf16[512,512]{1,0:T(8,128)(2,1)} %refs_2_.1) | copy-start | bytes 1572868
  52.6 14.0 %copy-start.3 = (bf16[512,512]{1,0:T(8,128)(2,1)S(1)}, bf16[512,512]{1,0:T(8,128)(2,1)}, u32[]{:S(2)}) copy-start(bf16[512,512]{1,0:T(8,128)(2,1)} %refs_3_.1) | copy-start | bytes 1572868
  55.3 7.3 %collective-permute-start.20 = (bf16[512,128]{1,0:T(8,128)(2,1)S(1)}, bf16[512,128]{1,0:T(8,128)(2,1)S(1)}, u32[]{:S(2)}, u32[]{:S(2)}) collective-permute-start(bf16[512,128]{1,0:T(8,128)(2,1)S(1)} %get-tuple-element.57), channel_id=1, source_target_pairs={{0,8},{8,0},{16,24},{24,16},{1,9},{9,1},{17,25},{25,17},{2,10},{10... | collective-permute-start | bytes 393224 | tf_op jit(solution)/shard_map/ppermute | solution.py:532
  56.2 10.4 %collective-permute-start.17 = (bf16[512,128]{1,0:T(8,128)(2,1)S(1)}, bf16[512,128]{1,0:T(8,128)(2,1)S(1)}, u32[]{:S(2)}, u32[]{:S(2)}) collective-permute-start(bf16[512,128]{1,0:T(8,128)(2,1)S(1)} %get-tuple-element.54), channel_id=1, source_target_pairs={{0,8},{8,0},{16,24},{24,16},{1,9},{9,1},{17,25},{25,17},{2,10},{10... | collective-permute-start | bytes 393224 | tf_op jit(solution)/shard_map/ppermute | solution.py:532
  57.4 12.4 %collective-permute-start.12 = (bf16[512,128]{1,0:T(8,128)(2,1)S(1)}, bf16[512,128]{1,0:T(8,128)(2,1)S(1)}, u32[]{:S(2)}, u32[]{:S(2)}) collective-permute-start(bf16[512,128]{1,0:T(8,128)(2,1)S(1)} %get-tuple-element.46), channel_id=1, source_target_pairs={{0,16},{8,24},{16,0},{24,8},{1,17},{9,25},{17,1},{25,9},{2,18},{10... | collective-permute-start | bytes 393224 | tf_op jit(solution)/shard_map/ppermute | solution.py:532
  60.0 9.7 %collective-permute-start.13 = (bf16[512,128]{1,0:T(8,128)(2,1)S(1)}, bf16[512,128]{1,0:T(8,128)(2,1)S(1)}, u32[]{:S(2)}, u32[]{:S(2)}) collective-permute-start(bf16[512,128]{1,0:T(8,128)(2,1)S(1)} %get-tuple-element.47), channel_id=1, source_target_pairs={{0,24},{8,16},{16,8},{24,0},{1,25},{9,17},{17,9},{25,1},{2,26},{10... | collective-permute-start | bytes 393224 | tf_op jit(solution)/shard_map/ppermute | solution.py:532
  (3 other events, 2.3 us)
